TPU v7x, 32 devices: a whole 2x2x4 slice. The times are simulated.
32 devices in a mesh: dp: 4 (over z), head: 2 (over x), seq: 4 (over y, core).
Axes of the slice: x: 2, y: 2, z: 4, core: 2. Of those that a mesh axis runs over, the one named last changes fastest.
Arguments:
- tokens: int32 [12288], P(('dp', 'head', 'seq')), may hold values from 0 to 8191
- segments: int32 [12288], P(('dp', 'head', 'seq')), may hold values from 0 to 24, as said below
- live_lengths: int32 [4, 25], P('dp'), may hold values from 1 to 3072, as said below
- timesteps: int32 [4, 25], P('dp'), may hold values from 0 to 1999
- table: bfloat16 [8192, 128], P('seq')
- input_weight: bfloat16 [128, 768], replicated, may hold values from -6 to 6
- time_first: bfloat16 [128, 768], replicated, may hold values from -0.5 to 0.5
- time_second: bfloat16 [768, 768], replicated, may hold values from -0.21875 to 0.21875
- first_gain: float32 [768], replicated, may hold values from 0.25 to 1.75
- first_shift: float32 [768], replicated, may hold values from -1.75 to 1.75
- query_weight: bfloat16 [768, 768], replicated, may hold values from -0.21875 to 0.21875
- key_weight: bfloat16 [768, 768], replicated, may hold values from -0.21875 to 0.21875
- value_weight: bfloat16 [768, 768], replicated, may hold values from -0.21875 to 0.21875
- output_weight: bfloat16 [768, 768], replicated, may hold values from -4 to 4
- second_gain: float32 [768], replicated, may hold values from 0.25 to 1.75
- second_shift: float32 [768], replicated, may hold values from -1.75 to 1.75
- up_weight: bfloat16 [768, 3072], replicated, may hold values from -0.21875 to 0.21875
- down_weight: bfloat16 [3072, 768], replicated, may hold values from -0.109375 to 0.109375
- upstream: bfloat16 [12288, 768], P(('dp', 'head', 'seq')), may hold values from -6 to 6
Outputs:
- activation: bfloat16 [12288, 768], P(('dp', 'head', 'seq'))
- embed_grad: float32 [12288, 128], P(('dp', 'head', 'seq'))
- table_grad: float32 [8192, 128], P('seq')
- input_grad: float32 [128, 768], P('dp')
- time_first_grad: float32 [128, 768], P('dp')
- time_second_grad: float32 [768, 768], P('dp')
- first_gain_grad: float32 [768], replicated
- first_shift_grad: float32 [768], replicated
- query_grad: float32 [768, 768], P('dp')
- key_grad: float32 [768, 768], P('dp')
- value_grad: float32 [768, 768], P('dp')
- output_grad: float32 [768, 768], P('dp')
- second_gain_grad: float32 [768], replicated
- second_shift_grad: float32 [768], replicated
- up_grad: float32 [768, 3072], P('dp')
- down_grad: float32 [3072, 768], P('dp')
Inputs may be any that keep to these rules, and one draw needn't show every extreme that they name: Within each group of 3072 tokens (one index of dp) segments start at 0 and never fall; every slot with tokens holds 64 tokens except one that holds 1536 tokens or more, up to the whole group; slots of a group may be left without tokens. `live_lengths`: the live tokens of each slot are its first ones; the rest are padding. The slot holding the long item is live in full.
All inputs are finite; a program needn't handle non-finite values.
Results may differ from a plain program's by a relative error of at most 0.019.
Values may be sent and summed in bfloat16 or wider, within the bound.
A program may use at most 192 MiB of HBM per device.

v0:
```python
import math

import jax
import jax.numpy as jnp
from jax import lax
from jax.sharding import PartitionSpec as P

HEADS = 12
HEAD_DIM = 64
VOCAB = 8192


EPSILON = 1e-05
MASKED = -1e30


def layer_norm(values, gain, shift):
    centre = values - jnp.mean(values, axis=-1, keepdims=True)
    spread = jnp.mean(centre * centre, axis=-1, keepdims=True)
    return centre * lax.rsqrt(spread + EPSILON) * gain + shift


def time_features(steps, width):
    half = width // 2
    freqs = jnp.exp(-math.log(10000.0) * jnp.arange(half, dtype=jnp.float32) / half)
    angles = steps.astype(jnp.float32)[:, None] * freqs[None, :]
    return jnp.concatenate([jnp.cos(angles), jnp.sin(angles)], axis=1)


def contract(left, right):
    return lax.dot_general(
        left, right, (((0,), (0,)), ((), ())), preferred_element_type=jnp.float32
    )


def against(left, right):
    return lax.dot_general(
        left, right, (((1,), (1,)), ((), ())), preferred_element_type=jnp.float32
    )


def contract_exact(left, right):
    return lax.dot_general(left, right, (((0,), (0,)), ((), ())), precision=lax.Precision.HIGHEST)


def key_layout(all_ids, lengths_row, head_count, seq_count, local_count):
    slot_count = lengths_row.shape[0]
    hits = all_ids[:, None] == jnp.arange(slot_count, dtype=jnp.int32)[None, :]
    counts = jnp.sum(hits.astype(jnp.int32), axis=0)
    starts = jnp.cumsum(counts) - counts
    first = jnp.sum(jnp.where(hits, starts[None, :], 0), axis=1)
    limit = jnp.sum(jnp.where(hits, lengths_row[None, :], 0), axis=1)
    live = jnp.arange(all_ids.shape[0], dtype=jnp.int32) - first < limit

    def reorder(array):
        return array.reshape(head_count, seq_count, local_count).transpose(1, 0, 2).reshape(-1)

    return (reorder(all_ids), reorder(live))


def body(
    tokens,
    segments,
    live_lengths,
    timesteps,
    table,
    input_weight,
    time_first,
    time_second,
    first_gain,
    first_shift,
    query_weight,
    key_weight,
    value_weight,
    output_weight,
    second_gain,
    second_shift,
    up_weight,
    down_weight,
    upstream,
):
    head_count = lax.axis_size("head")
    seq_count = lax.axis_size("seq")
    local_count = tokens.shape[0]
    width = query_weight.shape[0]
    shard_rows = table.shape[0]
    slot_count = live_lengths.shape[1]
    heads_here = HEADS // head_count
    scale = HEAD_DIM ** (-0.5)
    highest = lax.Precision.HIGHEST
    query_rows = head_count * local_count
    all_ids = lax.all_gather(segments, ("head", "seq"), axis=0, tiled=True)
    key_ids, key_live = key_layout(all_ids, live_lengths[0], head_count, seq_count, local_count)
    seq_index = lax.axis_index("seq")
    query_ids = lax.dynamic_slice_in_dim(key_ids, seq_index * query_rows, query_rows)
    piece = lax.all_gather(table, "seq", axis=0, tiled=True)
    count = piece.shape[0]
    inside = (tokens >= 0) & (tokens < count)
    picked = jnp.take(piece, jnp.clip(tokens, 0, count - 1), axis=0).astype(jnp.float32)
    found = jnp.where(inside[:, None], picked, 0.0)
    widened = piece.astype(jnp.float32)
    norm_sum = jnp.sum(jnp.sqrt(jnp.sum(widened * widened, axis=1)))
    found, norm_sum = (found, norm_sum)
    mean_norm = norm_sum / VOCAB
    embedded = found / mean_norm
    embed_low = embedded.astype(jnp.bfloat16)
    features = time_features(timesteps[0], time_first.shape[0])
    first_wide = time_first.astype(jnp.float32)
    second_wide = time_second.astype(jnp.float32)
    time_hidden = jnp.dot(features, first_wide, precision=highest)
    time_act = jax.nn.silu(time_hidden)
    time_out = jnp.dot(time_act, second_wide, precision=highest)
    picker = (segments[:, None] == jnp.arange(slot_count, dtype=jnp.int32)[None, :]).astype(
        jnp.float32
    )
    time_vec = jnp.dot(picker, time_out, precision=highest)
    stream = jnp.dot(embed_low, input_weight, preferred_element_type=jnp.float32) + time_vec
    normed_one = layer_norm(stream, first_gain, first_shift).astype(jnp.bfloat16)
    query = jnp.dot(normed_one, query_weight, preferred_element_type=jnp.float32).astype(
        jnp.bfloat16
    )
    keys = jnp.dot(normed_one, key_weight, preferred_element_type=jnp.float32).astype(jnp.bfloat16)
    values = jnp.dot(normed_one, value_weight, preferred_element_type=jnp.float32).astype(
        jnp.bfloat16
    )

    def to_heads(array):
        return array.reshape(local_count, head_count, width // head_count)

    query_in, key_in, value_in = (
        lax.all_to_all(to_heads(query), "head", split_axis=1, concat_axis=0, tiled=True),
        lax.all_to_all(to_heads(keys), "head", split_axis=1, concat_axis=0, tiled=True),
        lax.all_to_all(to_heads(values), "head", split_axis=1, concat_axis=0, tiled=True),
    )
    query_heads = query_in.reshape(query_rows, heads_here, HEAD_DIM)
    key_flat = key_in.reshape(query_rows, heads_here * HEAD_DIM)
    value_flat = value_in.reshape(query_rows, heads_here * HEAD_DIM)
    key_all, value_all = (
        lax.all_gather(key_flat, "seq", axis=0, tiled=True),
        lax.all_gather(value_flat, "seq", axis=0, tiled=True),
    )
    total = key_all.shape[0]
    block = math.gcd(total, 512)
    blocks = total // block
    key_blocks = key_all.reshape(blocks, block, heads_here, HEAD_DIM)
    value_blocks = value_all.reshape(blocks, block, heads_here, HEAD_DIM)
    id_blocks = key_ids.reshape(blocks, block)
    live_blocks = key_live.reshape(blocks, block)

    def scores(key_part, id_part, live_part):
        raw = (
            jnp.einsum("qhd,khd->hqk", query_heads, key_part, preferred_element_type=jnp.float32)
            * scale
        )
        allowed = (query_ids[:, None] == id_part[None, :]) & live_part[None, :]
        return jnp.where(allowed[None], raw, MASKED)

    def stats_step(carry, part):
        top, summed = carry
        current = scores(part[0], part[1], part[2])
        new_top = jnp.maximum(top, jnp.max(current, axis=-1))
        summed = summed * jnp.exp(top - new_top) + jnp.sum(
            jnp.exp(current - new_top[..., None]), axis=-1
        )
        return ((new_top, summed), None)

    stats_start = (
        jnp.full((heads_here, query_rows), MASKED, jnp.float32),
        jnp.zeros((heads_here, query_rows), jnp.float32),
    )
    (top, summed), _ = lax.scan(stats_step, stats_start, (key_blocks, id_blocks, live_blocks))
    log_total = top + jnp.log(summed)

    def value_step(gathered, part):
        key_part, value_part, id_part, live_part = part
        weights = jnp.exp(scores(key_part, id_part, live_part) - log_total[..., None]).astype(
            jnp.bfloat16
        )
        return (
            gathered
            + jnp.einsum("hqk,khd->qhd", weights, value_part, preferred_element_type=jnp.float32),
            None,
        )

    attended, _ = lax.scan(
        value_step,
        jnp.zeros((query_rows, heads_here, HEAD_DIM), jnp.float32),
        (key_blocks, value_blocks, id_blocks, live_blocks),
    )
    attended_low = attended.astype(jnp.bfloat16).reshape(query_rows, 1, heads_here * HEAD_DIM)
    mixed = lax.all_to_all(attended_low, "head", split_axis=0, concat_axis=1, tiled=True).reshape(
        local_count, width
    )
    middle = stream + jnp.dot(mixed, output_weight, preferred_element_type=jnp.float32)
    normed_two = layer_norm(middle, second_gain, second_shift).astype(jnp.bfloat16)
    hidden_pre = jnp.dot(normed_two, up_weight, preferred_element_type=jnp.float32)
    hidden = jax.nn.gelu(hidden_pre, approximate=False).astype(jnp.bfloat16)
    activation = (middle + jnp.dot(hidden, down_weight, preferred_element_type=jnp.float32)).astype(
        jnp.bfloat16
    )
    upstream_wide = upstream.astype(jnp.float32)
    down_grad = contract(hidden, upstream)
    hidden_grad = against(upstream, down_weight)
    _, gelu_back = jax.vjp(lambda inner: jax.nn.gelu(inner, approximate=False), hidden_pre)
    pre_grad = gelu_back(hidden_grad)[0].astype(jnp.bfloat16)
    up_grad = contract(normed_two, pre_grad)
    normed_two_grad = against(pre_grad, up_weight)
    _, second_back = jax.vjp(layer_norm, middle, second_gain, second_shift)
    middle_part, second_gain_grad, second_shift_grad = second_back(normed_two_grad)
    middle_grad = upstream_wide + middle_part
    middle_low = middle_grad.astype(jnp.bfloat16)
    output_grad = contract(mixed, middle_low)
    mixed_grad = against(middle_low, output_weight).astype(jnp.bfloat16)
    attended_grad = lax.all_to_all(
        mixed_grad.reshape(local_count, head_count, width // head_count),
        "head",
        split_axis=1,
        concat_axis=0,
        tiled=True,
    ).reshape(query_rows, heads_here, HEAD_DIM)
    row_dot = jnp.sum(attended_grad.astype(jnp.float32) * attended, axis=-1).T

    def back_step(query_sum, part):
        key_part, value_part, id_part, live_part = part
        probs = jnp.exp(scores(key_part, id_part, live_part) - log_total[..., None])
        probs_low = probs.astype(jnp.bfloat16)
        prob_grad = jnp.einsum(
            "qhd,khd->hqk", attended_grad, value_part, preferred_element_type=jnp.float32
        )
        score_grad = (probs * (prob_grad - row_dot[..., None])).astype(jnp.bfloat16)
        query_sum = query_sum + jnp.einsum(
            "hqk,khd->qhd", score_grad, key_part, preferred_element_type=jnp.float32
        )
        key_part_grad = jnp.einsum(
            "hqk,qhd->khd", score_grad, query_heads, preferred_element_type=jnp.float32
        )
        value_part_grad = jnp.einsum(
            "hqk,qhd->khd", probs_low, attended_grad, preferred_element_type=jnp.float32
        )
        return (query_sum, (key_part_grad, value_part_grad))

    query_sum, (key_terms, value_terms) = lax.scan(
        back_step,
        jnp.zeros((query_rows, heads_here, HEAD_DIM), jnp.float32),
        (key_blocks, value_blocks, id_blocks, live_blocks),
    )
    key_terms = key_terms.reshape(total, heads_here * HEAD_DIM) * scale
    value_terms = value_terms.reshape(total, heads_here * HEAD_DIM)
    key_sum, value_sum = (
        lax.psum_scatter(
            key_terms.astype(jnp.bfloat16), "seq", scatter_dimension=0, tiled=True
        ).astype(jnp.float32),
        lax.psum_scatter(
            value_terms.astype(jnp.bfloat16), "seq", scatter_dimension=0, tiled=True
        ).astype(jnp.float32),
    )
    query_back = (
        (query_sum * scale).astype(jnp.bfloat16).reshape(query_rows, 1, heads_here * HEAD_DIM)
    )
    key_back = key_sum.astype(jnp.bfloat16).reshape(query_rows, 1, heads_here * HEAD_DIM)
    value_back = value_sum.astype(jnp.bfloat16).reshape(query_rows, 1, heads_here * HEAD_DIM)
    query_tok, key_tok, value_tok = (
        lax.all_to_all(query_back, "head", split_axis=0, concat_axis=1, tiled=True),
        lax.all_to_all(key_back, "head", split_axis=0, concat_axis=1, tiled=True),
        lax.all_to_all(value_back, "head", split_axis=0, concat_axis=1, tiled=True),
    )
    query_tok = query_tok.reshape(local_count, width)
    key_tok = key_tok.reshape(local_count, width)
    value_tok = value_tok.reshape(local_count, width)
    query_grad = contract(normed_one, query_tok)
    key_grad = contract(normed_one, key_tok)
    value_grad = contract(normed_one, value_tok)
    normed_one_grad = (
        against(query_tok, query_weight)
        + against(key_tok, key_weight)
        + against(value_tok, value_weight)
    )
    _, first_back = jax.vjp(layer_norm, stream, first_gain, first_shift)
    stream_part, first_gain_grad, first_shift_grad = first_back(normed_one_grad)
    stream_grad = middle_grad + stream_part
    stream_low = stream_grad.astype(jnp.bfloat16)
    input_grad = contract(embed_low, stream_low)
    embed_grad = against(stream_low, input_weight)
    time_out_grad = contract_exact(picker, stream_grad)
    time_second_grad = contract_exact(time_act, time_out_grad)
    act_grad = lax.dot_general(
        time_out_grad, second_wide, (((1,), (1,)), ((), ())), precision=highest
    )
    _, silu_back = jax.vjp(jax.nn.silu, time_hidden)
    time_hidden_grad = silu_back(act_grad)[0]
    time_first_grad = contract_exact(features, time_hidden_grad)
    (
        input_part,
        first_part,
        second_part,
        query_part,
        key_part,
        value_part,
        output_part,
        up_part,
        down_part,
    ) = (
        lax.psum_scatter(
            input_grad.astype(jnp.bfloat16), "dp", scatter_dimension=0, tiled=True
        ).astype(jnp.float32),
        lax.psum_scatter(
            time_first_grad.astype(jnp.bfloat16), "dp", scatter_dimension=0, tiled=True
        ).astype(jnp.float32),
        lax.psum_scatter(
            time_second_grad.astype(jnp.bfloat16), "dp", scatter_dimension=0, tiled=True
        ).astype(jnp.float32),
        lax.psum_scatter(
            query_grad.astype(jnp.bfloat16), "dp", scatter_dimension=0, tiled=True
        ).astype(jnp.float32),
        lax.psum_scatter(
            key_grad.astype(jnp.bfloat16), "dp", scatter_dimension=0, tiled=True
        ).astype(jnp.float32),
        lax.psum_scatter(
            value_grad.astype(jnp.bfloat16), "dp", scatter_dimension=0, tiled=True
        ).astype(jnp.float32),
        lax.psum_scatter(
            output_grad.astype(jnp.bfloat16), "dp", scatter_dimension=0, tiled=True
        ).astype(jnp.float32),
        lax.psum_scatter(
            up_grad.astype(jnp.bfloat16), "dp", scatter_dimension=0, tiled=True
        ).astype(jnp.float32),
        lax.psum_scatter(
            down_grad.astype(jnp.bfloat16), "dp", scatter_dimension=0, tiled=True
        ).astype(jnp.float32),
    )
    shards = (
        lax.psum(input_part.astype(jnp.bfloat16), ("head", "seq")).astype(jnp.float32),
        lax.psum(first_part.astype(jnp.bfloat16), ("head", "seq")).astype(jnp.float32),
        lax.psum(second_part.astype(jnp.bfloat16), ("head", "seq")).astype(jnp.float32),
        lax.psum(query_part.astype(jnp.bfloat16), ("head", "seq")).astype(jnp.float32),
        lax.psum(key_part.astype(jnp.bfloat16), ("head", "seq")).astype(jnp.float32),
        lax.psum(value_part.astype(jnp.bfloat16), ("head", "seq")).astype(jnp.float32),
        lax.psum(output_part.astype(jnp.bfloat16), ("head", "seq")).astype(jnp.float32),
        lax.psum(up_part.astype(jnp.bfloat16), ("head", "seq")).astype(jnp.float32),
        lax.psum(down_part.astype(jnp.bfloat16), ("head", "seq")).astype(jnp.float32),
    )
    mean_part = -jnp.sum(embed_grad * found) / (mean_norm * mean_norm)
    scaled_grad = embed_grad / mean_norm
    full_table = jax.ops.segment_sum(scaled_grad, tokens, num_segments=VOCAB)
    small = lax.psum(
        (
            first_gain_grad,
            first_shift_grad,
            second_gain_grad,
            second_shift_grad,
            mean_part,
            full_table,
        ),
        ("dp", "head", "seq"),
    )
    table_rows = lax.dynamic_slice_in_dim(small[5], seq_index * shard_rows, shard_rows)
    table_wide = table.astype(jnp.float32)
    row_norms = jnp.sqrt(jnp.sum(table_wide * table_wide, axis=1))
    table_grad = table_rows + small[4] / VOCAB * table_wide / row_norms[:, None]
    return (
        activation,
        embed_grad,
        table_grad,
        shards[0],
        shards[1],
        shards[2],
        small[0],
        small[1],
        shards[3],
        shards[4],
        shards[5],
        shards[6],
        small[2],
        small[3],
        shards[7],
        shards[8],
    )


def solution(mesh):
    return jax.shard_map(
        body,
        mesh=mesh,
        in_specs=(
            P(("dp", "head", "seq")),
            P(("dp", "head", "seq")),
            P("dp", None),
            P("dp", None),
            P("seq", None),
            P(),
            P(),
            P(),
            P(),
            P(),
            P(),
            P(),
            P(),
            P(),
            P(),
            P(),
            P(),
            P(),
            P(("dp", "head", "seq"), None),
        ),
        out_specs=(
            P(("dp", "head", "seq"), None),
            P(("dp", "head", "seq"), None),
            P("seq", None),
            P("dp", None),
            P("dp", None),
            P("dp", None),
            P(),
            P(),
            P("dp", None),
            P("dp", None),
            P("dp", None),
            P("dp", None),
            P(),
            P(),
            P("dp", None),
            P("dp", None),
        ),
        check_vma=False,
    )
```

profile of v0, /device:TPU:0, one launch (start us, length us, event | category | flops | bytes accessed | tf_op | source)
XLA Modules:
  0.0 1131.8 jit_solution(1162741884844442980)
XLA Ops:
  13.4 21.5 %all-gather.5.cloned.1.call-done = bf16[8192,128]{1,0:T(8,128)(2,1)} async-done(((bf16[2048,128]{1,0:T(8,128)(2,1)}), bf16[8192,128]{1,0:T(8,128)(2,1)}) %all-gather.5.cloned.1.call-update) | async-done | bytes 2097168 | tf_op jit(solution)/shard_map/all_gather | solution.py:96
  45.9 12.5 %all_to_all.120 = bf16[384,2,384]{2,0,1:T(8,128)(2,1)} all-to-all(bf16[384,2,384]{2,0,1:T(8,128)(2,1)S(1)} %bitcast.284), channel_id=1, replica_groups=mesh['dp'=4,'head'=2,'seq'=4] {'head'}, dimensions={1} | all-to-all | bytes 1179648 | tf_op jit(solution)/shard_map/all_to_all | solution.py:133
  60.4 11.7 %all_to_all.121 = bf16[384,2,384]{2,0,1:T(8,128)(2,1)} all-to-all(bf16[384,2,384]{2,0,1:T(8,128)(2,1)S(1)} %bitcast.285), channel_id=1, replica_groups=mesh['dp'=4,'head'=2,'seq'=4] {'head'}, dimensions={1} | all-to-all | bytes 1179648 | tf_op jit(solution)/shard_map/all_to_all | solution.py:132
  72.1 7.7 all-gather
  87.3 9.0 all-to-all-done.2
  100.2 8.2 reshape.407
  108.4 7.1 copy.196
  115.5 8.1 reshape.408
  123.6 7.1 copy.197
  130.7 30.4 %while.39 = (s32[]{:T(128)}, f32[6,768]{1,0:T(8,128)S(1)}, f32[6,768]{1,0:T(8,128)S(1)}, s32[768]{0:T(1024)S(1)}, s32[6,512]{1,0:T(8,128)S(1)}, /*index=5*/pred[...) while((s32[]{:T(128)}, f32[6,768]{1,0:T(8,128)S(1)}, ...), condition=%wide.region_11.12_spmd.clone, body=%wide.region_8.11_spmd.clone.sunk | while | flops 319314432 | bytes 21287556 | solution.py:171
  161.2 35.5 %while.40 = (s32[]{:T(128)}, f32[768,6,64]{0,2,1:T(8,128)}, bf16[6,512,6,64]{1,3,2,0:T(8,128)(2,1)}, s32[768]{0:T(1024)S(1)}, s32[6,512]{1,0:T(8,128)S(1)}, /*in...) while((s32[]{:T(128)}, f32[768,6,64]{0,2,1:T(8,128)}, ...), condition=%wide.region_13.14_spmd.clone, body=%wide.region_12.13_spmd.clone.sunk | while | flops 614793216 | bytes 4552838 | solution.py:185
  167.1 5.6 fusion.187
  173.1 5.6 fusion.187
  179.1 5.6 fusion.187
  203.8 12.4 %all_to_all.122 = bf16[2,2,73728]{2,1,0:T(2,128)(2,1)S(1)} all-to-all(bf16[2,2,73728]{2,1,0:T(2,128)(2,1)} %reshape.416), channel_id=1, replica_groups=mesh['dp'=4,'head'=2,'seq'=4] {'head'}, dimensions={0} | all-to-all | bytes 1179648 | tf_op jit(solution)/shard_map/all_to_all | solution.py:191
  228.4 14.1 %add_convert_fusion = (bf16[384,3072]{1,0:T(8,128)(2,1)S(1)}, f32[384,3072]{1,0:T(8,128)}) fusion(f32[384,3072]{1,0:T(8,128)S(1)} %fusion.98, bf16[384,768]{1,0:T(8,128)(2,1)S(1)} %copy-done.18, bf16[3072,768]{1,0:T(8,128)(2,1)S(1)} %bitcast.304), kind=kOutput, calls=%fused_computation.68 | convolution fusion | flops 1896873984 | bytes 17104896 | tf_op jit(solution)/shard_map/dot_general | solution.py:37
  252.4 7.3 all-to-all-done.4
  265.6 94.5 %while.41 = (s32[]{:T(128)}, f32[768,6,64]{0,2,1:T(8,128)S(1)}, f32[6,512,6,64]{1,3,2,0:T(8,128)}, bf16[6,512,6,64]{1,3,2,0:T(8,128)(2,1)}, bf16[6,512,6,64]{1,3...) while((s32[]{:T(128)}, f32[768,6,64]{0,2,1:T(8,128)S(1)}, ...), condition=%wide.region_20.21_spmd.clone, body=%wide.region_19.20_spmd.clone.sunk | while | flops 1534918656 | bytes 51331824 | solution.py:242
  378.9 20.3 %reduce-scatter.14.cloned.1.call-done = bf16[768,384]{0,1:T(8,128)(2,1)} async-done(((bf16[3072,384]{0,1:T(8,128)(2,1)}), bf16[768,384]{0,1:T(8,128)(2,1)}) %reduce-scatter.14.cloned.1.call-update) | async-done | bytes 589840 | tf_op jit(solution)/shard_map/reduce_scatter | solution.py:253
  407.1 28.3 %reduce-scatter.12.cloned.1.call-done = bf16[768,384]{0,1:T(8,128)(2,1)} async-done(((bf16[3072,384]{0,1:T(8,128)(2,1)}), bf16[768,384]{0,1:T(8,128)(2,1)}) %reduce-scatter.12.cloned.1.call-update) | async-done | bytes 589840 | tf_op jit(solution)/shard_map/reduce_scatter | solution.py:250
  480.1 7.1 convolution_convert_fusion.1
  508.0 24.5 %reduce-scatter.28.cloned.1.call-done = bf16[192,768]{1,0:T(8,128)(2,1)} async-done(((bf16[768,768]{1,0:T(8,128)(2,1)}), bf16[192,768]{1,0:T(8,128)(2,1)}) %reduce-scatter.28.cloned.1.call-update) | async-done | bytes 294928 | tf_op jit(solution)/shard_map/reduce_scatter | solution.py:321
  532.5 30.2 %reduce-scatter.22.cloned.1.call-done = bf16[192,768]{1,0:T(8,128)(2,1)} async-done(((bf16[768,768]{1,0:T(8,128)(2,1)}), bf16[192,768]{1,0:T(8,128)(2,1)}) %reduce-scatter.22.cloned.1.call-update) | async-done | bytes 294928 | tf_op jit(solution)/shard_map/reduce_scatter | solution.py:312
  562.7 30.1 %reduce-scatter.26.cloned.1.call-done = bf16[192,768]{1,0:T(8,128)(2,1)} async-done(((bf16[768,768]{1,0:T(8,128)(2,1)}), bf16[192,768]{1,0:T(8,128)(2,1)}) %reduce-scatter.26.cloned.1.call-update) | async-done | bytes 294928 | tf_op jit(solution)/shard_map/reduce_scatter | solution.py:318
  592.8 30.2 %reduce-scatter.24.cloned.1.call-done = bf16[192,768]{1,0:T(8,128)(2,1)} async-done(((bf16[768,768]{1,0:T(8,128)(2,1)}), bf16[192,768]{1,0:T(8,128)(2,1)}) %reduce-scatter.24.cloned.1.call-update) | async-done | bytes 294928 | tf_op jit(solution)/shard_map/reduce_scatter | solution.py:315
  623.0 30.7 %reduce-scatter.20.cloned.1.call-done = bf16[192,768]{1,0:T(8,128)(2,1)} async-done(((bf16[768,768]{1,0:T(8,128)(2,1)}), bf16[192,768]{1,0:T(8,128)(2,1)}) %reduce-scatter.20.cloned.1.call-update) | async-done | bytes 294928 | tf_op jit(solution)/shard_map/reduce_scatter | solution.py:309
  653.7 86.3 %reduce-scatter.30.cloned.1.call-done = bf16[192,3072]{1,0:T(8,128)(2,1)} async-done(((bf16[768,3072]{1,0:T(8,128)(2,1)}), bf16[192,3072]{1,0:T(8,128)(2,1)}) %reduce-scatter.30.cloned.1.call-update) | async-done | bytes 1179664 | tf_op jit(solution)/shard_map/reduce_scatter | solution.py:324
  740.0 88.0 %reduce-scatter.32.cloned.1.call-done = bf16[768,768]{1,0:T(8,128)(2,1)} async-done(((bf16[3072,768]{1,0:T(8,128)(2,1)}), bf16[768,768]{1,0:T(8,128)(2,1)}) %reduce-scatter.32.cloned.1.call-update) | async-done | bytes 1179664 | tf_op jit(solution)/shard_map/reduce_scatter | solution.py:327
  829.7 5.9 fusion.65
  836.3 41.2 %all-reduce = (f32[]{:T(128)}, f32[768]{0:T(1024)}, f32[768]{0:T(1024)}, f32[768]{0:T(1024)}, f32[768]{0:T(1024)}) all-reduce(f32[]{:T(128)S(6)} %div.96, f32[768]{0:T(1024)S(1)} %get-tuple-element.471, f32[768]{0:T(1024)S(1)} %copy-done.56, f32[768]{0:T(1024)S(1)} %copy-done.64, ...), channel_id=1, replica_groups=mesh['dp'=4,'head'=2,'seq'=4] {'dp','head','seq'}, use_global_device_ids=true, to_apply=%region_28.29 | all-reduce | flops 3073 | bytes 24584 | tf_op jit(solution)/shard_map/psum | solution.py:345
  886.2 145.9 %all-reduce.7.cloned.1.call-done = f32[8192,128]{1,0:T(8,128)} async-done(((f32[8192,128]{1,0:T(8,128)}), f32[8192,128]{1,0:T(8,128)}) %all-reduce.7.cloned.1.call-update) | async-done | bytes 4194320 | tf_op jit(solution)/shard_map/psum | solution.py:345
  1034.6 79.9 %all-reduce.11.cloned.1.call-done = (bf16[192,768]{1,0:T(8,128)(2,1)}, bf16[192,768]{1,0:T(8,128)(2,1)}, bf16[192,768]{1,0:T(8,128)(2,1)}, bf16[192,768]{1,0:T(8...) async-done(((bf16[192,768]{1,0:T(8,128)(2,1)}, bf16[192,768]{1,0:T(8,128)(2,1)}, bf16[192,768]{1,0:T(8,128)(2,1)}, ...) | async-done | bytes 3833872 | tf_op jit(solution)/shard_map/psum | solution.py:334
  (467 shorter events, 320.0 us)
Async XLA Ops:
  7.2 37.9 %copy-start = (bf16[768,768]{1,0:T(8,128)(2,1)S(1)}, bf16[768,768]{1,0:T(8,128)(2,1)}, u32[]{:S(2)}) copy-start(bf16[768,768]{1,0:T(8,128)(2,1)} %param.37) | copy-start | bytes 3538948
  7.2 27.7 %all-gather.5.cloned.1.call-start = ((), (), s32[]{:S(2)}) async-start(), calls=%async_computation.19 | async-start | bytes 2621440 | tf_op jit(solution)/shard_map/all_gather | solution.py:96
  7.9 92.3 %all-gather.7.cloned.1.call-start = ((), (), s32[]{:S(2)}) async-start(), calls=%async_computation.20 | async-start | bytes 2949120 | tf_op jit(solution)/shard_map/all_gather | solution.py:140
  10.0 32.0 %copy-start.57 = (pred[384]{0:T(512)(128)(4,1)}, pred[384]{0:T(512)(128)(4,1)S(1)}, u32[]{:S(2)}) copy-start(pred[384]{0:T(512)(128)(4,1)S(1)} %get-tuple-element.559) | copy-start | bytes 1156
  10.0 32.0 %copy-start.59 = (pred[384]{0:T(512)(128)(4,1)}, pred[384]{0:T(512)(128)(4,1)S(1)}, u32[]{:S(2)}) copy-start(pred[384]{0:T(512)(128)(4,1)S(1)} %get-tuple-element.560) | copy-start | bytes 1156
  10.2 31.8 %copy-start.39 = (f32[25,64]{1,0:T(8,128)}, f32[25,64]{1,0:T(8,128)S(1)}, u32[]{:S(2)}) copy-start(f32[25,64]{1,0:T(8,128)S(1)} %get-tuple-element.561) | copy-start | bytes 19204
  10.2 32.4 %copy-start.34 = (bf16[128,768]{1,0:T(8,128)(2,1)S(1)}, bf16[128,768]{1,0:T(8,128)(2,1)}, u32[]{:S(2)}) copy-start(bf16[128,768]{1,0:T(8,128)(2,1)} %param.30) | copy-start | bytes 589828
  43.9 177.3 %copy-start.1 = (f32[384,768]{1,0:T(8,128)}, f32[384,768]{1,0:T(8,128)S(1)}, u32[]{:S(2)}) copy-start(f32[384,768]{1,0:T(8,128)S(1)} %get-tuple-element.564) | copy-start | bytes 3538948
  45.1 35.3 %copy-start.7 = (bf16[384,768]{1,0:T(8,128)(2,1)}, bf16[384,768]{1,0:T(8,128)(2,1)S(1)}, u32[]{:S(2)}) copy-start(bf16[384,768]{1,0:T(8,128)(2,1)S(1)} %add_convert_fusion.2) | copy-start | bytes 1769476
  58.4 57.1 %all-gather.9.cloned.1.call-start = ((), (), s32[]{:S(2)}) async-start(), calls=%async_computation.21 | async-start | bytes 2949120 | tf_op jit(solution)/shard_map/all_gather | solution.py:139
  83.3 13.1 %all-to-all-start.2 = ((bf16[384,2,384]{2,0,1:T(8,128)(2,1)}), bf16[384,2,384]{2,0,1:T(8,128)(2,1)S(1)}, u32[]{:S(2)}, u32[]{:S(2)}) async-start(bf16[384,2,384]{2,0,1:T(8,128)(2,1)} %bitcast.282), calls=%async_computation.2 | async-start | bytes 1179648 | tf_op jit(solution)/shard_map/all_to_all | solution.py:131
  248.3 11.3 %all-to-all-start.4 = ((bf16[384,2,384]{2,0,1:T(8,128)(2,1)}), bf16[384,2,384]{2,0,1:T(8,128)(2,1)S(1)}, u32[]{:S(2)}, u32[]{:S(2)}) async-start(bf16[384,2,384]{2,0,1:T(8,128)(2,1)} %bitcast.203), calls=%async_computation.4 | async-start | bytes 1179648 | tf_op jit(solution)/shard_map/all_to_all | solution.py:214
  251.8 147.4 %reduce-scatter.14.cloned.1.call-start = ((), (), s32[]{:S(2)}) async-start(), calls=%async_computation.23 | async-start | bytes 2949120 | tf_op jit(solution)/shard_map/reduce_scatter | solution.py:253
  365.7 69.7 %reduce-scatter.12.cloned.1.call-start = ((), (), s32[]{:S(2)}) async-start(), calls=%async_computation.22 | async-start | bytes 2949120 | tf_op jit(solution)/shard_map/reduce_scatter | solution.py:250
  375.4 27.2 %all-to-all-start.5 = ((bf16[2,2,73728]{2,1,0:T(2,128)(2,1)}), bf16[2,2,73728]{2,1,0:T(2,128)(2,1)S(1)}, u32[]{:S(2)}, u32[]{:S(2)}) async-start(bf16[2,2,73728]{2,1,0:T(2,128)(2,1)} %reshape.418), calls=%async_computation.5 | async-start | bytes 1179648 | tf_op jit(solution)/shard_map/all_to_all | solution.py:263
  402.6 36.2 %all-to-all-start.7 = ((bf16[2,2,73728]{2,1,0:T(2,128)(2,1)}), bf16[2,2,73728]{2,1,0:T(2,128)(2,1)S(1)}, u32[]{:S(2)}, u32[]{:S(2)}) async-start(bf16[2,2,73728]{2,1,0:T(2,128)(2,1)} %reshape.422), calls=%async_computation.9 | async-start | bytes 1179648 | tf_op jit(solution)/shard_map/all_to_all | solution.py:265
  407.1 35.3 %copy-start.13 = (bf16[384,2,1,384]{0,3,1,2:T(8,128)(2,1)}, bf16[384,2,1,384]{0,3,1,2:T(8,128)(2,1)S(1)}, u32[]{:S(2)}) copy-start(bf16[384,2,1,384]{0,3,1,2:T(8,128)(2,1)S(1)} %copy.205) | copy-start | bytes 1769476
  438.8 12.5 %all-to-all-start.6 = ((bf16[2,2,73728]{2,1,0:T(2,128)(2,1)}), bf16[2,2,73728]{2,1,0:T(2,128)(2,1)S(1)}, u32[]{:S(2)}, u32[]{:S(2)}) async-start(bf16[2,2,73728]{2,1,0:T(2,128)(2,1)} %reshape.420), calls=%async_computation.7 | async-start | bytes 1179648 | tf_op jit(solution)/shard_map/all_to_all | solution.py:264
  442.3 55.7 %reduce-scatter.18.cloned.1.call-start = ((), (), s32[]{:S(2)}) async-start(), calls=%async_computation.26 | async-start | bytes 245760 | tf_op jit(solution)/shard_map/reduce_scatter | solution.py:306
  463.6 39.1 %reduce-scatter.16.cloned.1.call-start = ((), (), s32[]{:S(2)}) async-start(), calls=%async_computation.25 | async-start | bytes 245760 | tf_op jit(solution)/shard_map/reduce_scatter | solution.py:303
  465.7 66.8 %reduce-scatter.28.cloned.1.call-start = ((), (), s32[]{:S(2)}) async-start(), calls=%async_computation.31 | async-start | bytes 1474560 | tf_op jit(solution)/shard_map/reduce_scatter | solution.py:321
  468.6 94.1 %reduce-scatter.22.cloned.1.call-start = ((), (), s32[]{:S(2)}) async-start(), calls=%async_computation.28 | async-start | bytes 1474560 | tf_op jit(solution)/shard_map/reduce_scatter | solution.py:312
  471.7 121.1 %reduce-scatter.26.cloned.1.call-start = ((), (), s32[]{:S(2)}) async-start(), calls=%async_computation.30 | async-start | bytes 1474560 | tf_op jit(solution)/shard_map/reduce_scatter | solution.py:318
  473.7 149.4 %reduce-scatter.24.cloned.1.call-start = ((), (), s32[]{:S(2)}) async-start(), calls=%async_computation.29 | async-start | bytes 1474560 | tf_op jit(solution)/shard_map/reduce_scatter | solution.py:315
  476.7 177.0 %reduce-scatter.20.cloned.1.call-start = ((), (), s32[]{:S(2)}) async-start(), calls=%async_computation.27 | async-start | bytes 1474560 | tf_op jit(solution)/shard_map/reduce_scatter | solution.py:309
  479.8 260.2 %reduce-scatter.30.cloned.1.call-start = ((), (), s32[]{:S(2)}) async-start(), calls=%async_computation.32 | async-start | bytes 5898240 | tf_op jit(solution)/shard_map/reduce_scatter | solution.py:324
  487.3 340.7 %reduce-scatter.32.cloned.1.call-start = ((), (), s32[]{:S(2)}) async-start(), calls=%async_computation.33 | async-start | bytes 5898240 | tf_op jit(solution)/shard_map/reduce_scatter | solution.py:327
  498.0 385.3 %all-reduce.9.cloned.1.call-start = ((), (), s32[]{:S(2)}) async-start(), calls=%async_computation.34 | async-start | bytes 196608 | tf_op jit(solution)/shard_map/psum | solution.py:332
  502.7 529.4 %all-reduce.7.cloned.1.call-start = ((), (), s32[]{:S(2)}) async-start(), calls=%async_computation.24 | async-start | bytes 8388608 | tf_op jit(solution)/shard_map/psum | solution.py:345
  507.9 320.1 %copy-start.15 = (bf16[2048,128]{1,0:T(8,128)(2,1)S(1)}, bf16[2048,128]{1,0:T(8,128)(2,1)}, u32[]{:S(2)}) copy-start(bf16[2048,128]{1,0:T(8,128)(2,1)} %param.29) | copy-start | bytes 1572868
  507.9 321.7 %copy-start.4 = (f32[384,768]{1,0:T(8,128)S(1)}, f32[384,768]{1,0:T(8,128)}, u32[]{:S(2)}) copy-start(f32[384,768]{1,0:T(8,128)} %copy-done.3) | copy-start | bytes 3538948
  507.9 606.6 %all-reduce.11.cloned.1.call-start = ((), (), s32[]{:S(2)}) async-start(), calls=%async_computation.35 | async-start | bytes 7667712 | tf_op jit(solution)/shard_map/psum | solution.py:334
  (76 other events, 399.7 us)
Sparse Core Ops, SparseCore 0:
  9.6 25.2 all-gather.4
  58.5 23.2 all-gather.6
  83.4 24.0 all-gather.8
  365.8 33.3 reduce-scatter.13
  402.3 33.0 reduce-scatter.11
  463.7 18.4 reduce-scatter.17
  485.1 17.5 reduce-scatter.15
  505.0 27.4 reduce-scatter.27
  534.8 27.8 reduce-scatter.21
  564.9 27.8 reduce-scatter.25
  595.1 27.8 reduce-scatter.23
  625.8 27.8 reduce-scatter.19
  656.0 83.9 reduce-scatter.29
  742.2 85.7 reduce-scatter.31
  831.0 52.2 all-reduce.8
  889.6 142.4 all-reduce.6
  1036.8 77.6 all-reduce.10
where the time goes:
time: 1140 us; the launch traced here: 1130 us
  waiting for transfers between devices  646 us (57%)
  matrix products  214 us (19%)
  blocking collectives  85.6 us (8%)
  local copies, waits for them, and re-layouts  82.1 us (7%)
  other arithmetic  65.2 us (6%)
  starting transfers between devices  19.2 us (2%)
  between operations  18.8 us (2%)
    psum x1, waiting for transfers between devices, body(): lax.psum((first_gain_grad, first_shift_grad, second_gain_grad, second_shi...  146 us
    reduce_scatter x1, waiting for transfers between devices, body(): lax.psum_scatter(down_grad.astype(jnp.bfloat16), 'dp', scatter_dimension=...  88 us
    reduce_scatter x1, waiting for transfers between devices, body(): lax.psum_scatter(up_grad.astype(jnp.bfloat16), 'dp', scatter_dimension=0,...  86.3 us
    psum x1, waiting for transfers between devices, body(): lax.psum(second_part.astype(jnp.bfloat16), ('head', 'seq'))  79.9 us
    psum x1, blocking collectives, body(): lax.psum((first_gain_grad, first_shift_grad, second_gain_grad, second_shi...  41.2 us
    unnamed x169, local copies, waits for them, and re-layouts  38.3 us
    dot_general x6, matrix products, value_step(): jnp.einsum('hqk,khd->qhd', weights, value_part, preferred_element_type=jn...  33.3 us
    reduce_scatter x1, waiting for transfers between devices, body(): lax.psum_scatter(time_second_grad.astype(jnp.bfloat16), 'dp', scatter_dim...  30.7 us
  transfers between devices with their start and end apart: 22, of which 17 were waited for; matrix products, arithmetic and copies ran while one was open for 9% of the time, Pallas kernels for 0%

commit v1 on v0

v1 whole, which is shorter than its diff:
```python
import functools
import math

import jax
import jax.numpy as jnp
from jax import lax
from jax.experimental import pallas as pl
from jax.experimental.pallas import tpu as pltpu
from jax.sharding import PartitionSpec as P

HEADS = 12
HEAD_DIM = 64
VOCAB = 8192
EPSILON = 1e-05
MASKED = -1e30
LOG2E = math.log2(math.e)
LN2 = math.log(2.0)
KEY_BLOCK = 512
SLOTS = 32
DEAD = 25
ONES = 32
VMEM_LIMIT = 60 * 2**20

F32 = jnp.float32
BF16 = jnp.bfloat16


def dot(left, right, left_dim=1, right_dim=0):
    return lax.dot_general(
        left, right, (((left_dim,), (right_dim,)), ((), ())), preferred_element_type=F32
    )


def contract_exact(left, right):
    return lax.dot_general(left, right, (((0,), (0,)), ((), ())), precision=lax.Precision.HIGHEST)


def whole(shape):
    return pl.BlockSpec(shape, lambda *_: (0,) * len(shape))


def params(**more):
    return pltpu.CompilerParams(vmem_limit_bytes=VMEM_LIMIT, **more)


def norm_parts(values):
    centre = values - jnp.mean(values, axis=-1, keepdims=True)
    spread = jnp.mean(centre * centre, axis=-1, keepdims=True)
    scale = lax.rsqrt(spread + EPSILON)
    return centre * scale, scale


def norm_back(incoming, gain, unit, scale):
    scaled = incoming * gain
    inner = scaled - jnp.mean(scaled, axis=-1, keepdims=True)
    return scale * (inner - unit * jnp.mean(scaled * unit, axis=-1, keepdims=True))


def embed_kernel(
    own,
    tokens,
    slots,
    all_slots,
    lengths,
    mean_norm,
    table,
    entry,
    gain,
    shift,
    query_weight,
    key_weight,
    value_weight,
    normed_out,
    key_out,
    value_out,
    mark_out,
    stream_out,
    query_out,
    low_out,
    picked,
    limits,
):
    step = pl.program_id(0)
    blocks = pl.num_programs(0)
    rows = picked.shape[0]
    block = lax.rem(own[0] + step, blocks)
    base = block * rows

    @pl.when(step == 0)
    def _():
        lanes = lax.broadcasted_iota(jnp.int32, (all_slots.shape[0], 128), 1)
        below = jnp.where(all_slots[...] < lanes, 1.0, 0.0)
        limits[...] = jnp.sum(below, axis=0, keepdims=True) + lengths[...]

    def pick(index, carry):
        for inner in range(8):
            row = index * 8 + inner
            picked[pl.ds(row, 1), :] = table[pl.ds(tokens[base + row], 1), :]
        return carry

    lax.fori_loop(0, rows // 8, pick, 0)
    low = (picked[...] / mean_norm[0]).astype(BF16)
    lanes = lax.broadcasted_iota(jnp.int32, (rows, 128), 1)
    slot = slots[...]
    same = jnp.where((lanes & (SLOTS - 1)) == slot, 1.0, 0.0)
    spread = jnp.where(lanes < 3 * SLOTS, same, 0.0).astype(BF16)
    stream = dot(jnp.concatenate([low, spread], axis=1), entry[...])
    unit, _ = norm_parts(stream)
    normed = (unit * gain[...] + shift[...]).astype(BF16)
    normed_out[...] = normed
    key_out[...] = dot(normed, key_weight[...]).astype(BF16)
    value_out[...] = dot(normed, value_weight[...]).astype(BF16)
    first = jnp.where(lanes < SLOTS, same, 0.0)
    limit = jnp.sum(first * limits[...], axis=1, keepdims=True)
    index = (base + lax.broadcasted_iota(jnp.int32, (rows, 1), 0)).astype(F32)
    dead = jnp.where(index < limit, 0.0, 1.0)
    marks = jnp.where(lanes == DEAD, dead, first)
    marks = jnp.where((lanes >= ONES) & (lanes < ONES + 2), 1.0, marks)
    mark_out[...] = marks.astype(BF16)

    @pl.when(step == 0)
    def _():
        stream_out[...] = stream
        low_out[...] = low
        query = dot(query_weight[...], normed, 0, 1) * (LOG2E / math.sqrt(HEAD_DIM))
        query_out[...] = query.astype(BF16)


def embed(own, tokens, slots, lengths, mean_norm, table, entry, gain, shift, wq, wk, wv, blocks):
    group = tokens.shape[0]
    rows = group // blocks
    width = wq.shape[0]
    turn = lambda step, own, tokens: (lax.rem(own[0] + step, blocks), 0)
    return pl.pallas_call(
        embed_kernel,
        grid_spec=pltpu.PrefetchScalarGridSpec(
            num_scalar_prefetch=2,
            grid=(blocks,),
            in_specs=[
                pl.BlockSpec((rows, 1), turn),
                whole((group, 1)),
                whole((1, 128)),
                pl.BlockSpec(memory_space=pltpu.SMEM),
                whole(table.shape),
                whole(entry.shape),
                whole((1, width)),
                whole((1, width)),
                whole((width, width)),
                whole((width, width)),
                whole((width, width)),
            ],
            out_specs=[
                pl.BlockSpec((rows, width), turn),
                pl.BlockSpec((rows, width), turn),
                pl.BlockSpec((rows, width), turn),
                pl.BlockSpec((rows, 128), turn),
                whole((rows, width)),
                whole((width, rows)),
                whole((rows, 128)),
            ],
            scratch_shapes=[pltpu.VMEM((rows, 128), F32), pltpu.VMEM((1, 128), F32)],
        ),
        out_shape=[
            jax.ShapeDtypeStruct((group, width), BF16),
            jax.ShapeDtypeStruct((group, width), BF16),
            jax.ShapeDtypeStruct((group, width), BF16),
            jax.ShapeDtypeStruct((group, 128), BF16),
            jax.ShapeDtypeStruct((rows, width), F32),
            jax.ShapeDtypeStruct((width, rows), BF16),
            jax.ShapeDtypeStruct((rows, 128), BF16),
        ],
        compiler_params=params(),
        name="embed",
    )(own, tokens, slots, slots, lengths, mean_norm, table, entry, gain, shift, wq, wk, wv)


def pair_columns(target, pair, rows):
    target[0:HEAD_DIM, 0:rows] = pair[0:HEAD_DIM]
    target[0:HEAD_DIM, rows : 2 * rows] = jnp.zeros((HEAD_DIM, rows), BF16)
    target[HEAD_DIM : 2 * HEAD_DIM, 0:rows] = jnp.zeros((HEAD_DIM, rows), BF16)
    target[HEAD_DIM : 2 * HEAD_DIM, rows : 2 * rows] = pair[HEAD_DIM : 2 * HEAD_DIM]


def forward_kernel(query, keys, values, marks, slots, probs_out, mixed_out, inverse_out, right, scores):
    rows = query.shape[1]
    group = keys.shape[0]
    blocks = group // KEY_BLOCK
    pair_columns(right, query, rows)
    kinds = lax.broadcasted_iota(jnp.int32, (128, rows), 0)
    away = jnp.where((kinds < DEAD) & (kinds != slots[...]), MASKED, 0.0)
    away = jnp.where(kinds == DEAD, MASKED, away).astype(BF16)
    right[128:256, 0:rows] = away
    right[128:256, rows : 2 * rows] = away

    def score(index, top):
        part = pl.ds(pl.multiple_of(index * KEY_BLOCK, KEY_BLOCK), KEY_BLOCK)
        left = jnp.concatenate([keys[part, :], marks[part, :]], axis=1)
        current = dot(left, right[...])
        scores[part, :] = current
        return jnp.maximum(top, jnp.max(current.reshape(KEY_BLOCK // 8, 8, 2 * rows), axis=0))

    top = lax.fori_loop(0, blocks, score, jnp.full((8, 2 * rows), MASKED, F32))
    top = jnp.max(top, axis=0, keepdims=True)
    ones = jnp.ones((16, KEY_BLOCK), BF16)

    def weigh(index, total):
        part = pl.ds(pl.multiple_of(index * KEY_BLOCK, KEY_BLOCK), KEY_BLOCK)
        probs = jnp.exp2(scores[part, :] - top).astype(BF16)
        probs_out[part, :] = probs
        left = jnp.concatenate([values[part, :].T, ones], axis=0)
        return total + dot(left, probs)

    total = lax.fori_loop(0, blocks, weigh, jnp.zeros((144, 2 * rows), F32))
    inverse = 1.0 / total[128:129]
    mixed_out[0:HEAD_DIM] = total[0:HEAD_DIM, 0:rows] * inverse[:, 0:rows]
    mixed_out[HEAD_DIM:128] = total[HEAD_DIM:128, rows : 2 * rows] * inverse[:, rows : 2 * rows]
    inverse_out[0, 0:1] = inverse[:, 0:rows]
    inverse_out[0, 1:2] = inverse[:, rows : 2 * rows]


def attend(query, keys, values, marks, slots):
    width, rows = query.shape
    group = keys.shape[0]
    pairs = width // 128
    column = pl.BlockSpec((group, 128), lambda pair: (0, pair))
    return pl.pallas_call(
        forward_kernel,
        grid=(pairs,),
        in_specs=[
            pl.BlockSpec((128, rows), lambda pair: (pair, 0)),
            column,
            column,
            whole((group, 128)),
            whole((1, rows)),
        ],
        out_specs=[
            pl.BlockSpec((group, 2 * rows), lambda pair: (0, pair)),
            pl.BlockSpec((128, rows), lambda pair: (pair, 0)),
            pl.BlockSpec((1, 2, rows), lambda pair: (pair, 0, 0)),
        ],
        out_shape=[
            jax.ShapeDtypeStruct((group, pairs * 2 * rows), BF16),
            jax.ShapeDtypeStruct((width, rows), F32),
            jax.ShapeDtypeStruct((pairs, 2, rows), F32),
        ],
        scratch_shapes=[pltpu.VMEM((256, 2 * rows), BF16), pltpu.VMEM((group, 2 * rows), F32)],
        compiler_params=params(),
        name="attend",
    )(query, keys, values, marks, slots)


def feed_kernel(
    mixed_wide,
    inverse,
    stream,
    upstream,
    gain,
    shift,
    output_hbm,
    up_hbm,
    down_hbm,
    activation_out,
    middle_grad_out,
    norm_out,
    mixed_grad_out,
    row_out,
    output_grad_hbm,
    up_grad_hbm,
    down_grad_hbm,
    output_weight,
    up_weight,
    down_weight,
    output_grad,
    up_grad,
    down_grad,
    loads,
    stores,
):
    rows, width = stream.shape
    hidden_width = up_weight.shape[1]
    chunk = 512
    chunks = hidden_width // chunk
    load_output = pltpu.make_async_copy(output_hbm, output_weight, loads.at[0])
    load_up = pltpu.make_async_copy(up_hbm, up_weight, loads.at[1])
    load_down = pltpu.make_async_copy(down_hbm, down_weight, loads.at[2])
    load_output.start()
    load_up.start()
    load_down.start()
    mixed = mixed_wide[...].astype(BF16)
    load_output.wait()
    middle = stream[...] + dot(mixed, output_weight[...], 0, 0)
    unit, scale = norm_parts(middle)
    normed = (unit * gain[...] + shift[...]).astype(BF16)
    normed_t = normed.T
    load_up.wait()
    load_down.wait()
    incoming = upstream[...]
    activation = middle
    normed_grad = jnp.zeros((rows, width), F32)
    for index in range(chunks):
        part = slice(index * chunk, (index + 1) * chunk)
        pre = dot(normed, up_weight[:, part])
        cdf = 0.5 * (1.0 + lax.erf(pre * math.sqrt(0.5)))
        slope = cdf + pre * jnp.exp(-0.5 * pre * pre) * (1.0 / math.sqrt(2.0 * math.pi))
        hidden = (pre * cdf).astype(BF16)
        back = dot(incoming, down_weight[part, :], 1, 1)
        pre_grad = (back * slope).astype(BF16)
        activation = activation + dot(hidden, down_weight[part, :])
        down_grad[part, :] = dot(hidden, incoming, 0, 0).astype(BF16)
        up_grad[:, part] = dot(normed_t, pre_grad).astype(BF16)
        normed_grad = normed_grad + dot(pre_grad, up_weight[:, part], 1, 1)
    store_up = pltpu.make_async_copy(up_grad, up_grad_hbm, stores.at[1])
    store_down = pltpu.make_async_copy(down_grad, down_grad_hbm, stores.at[2])
    store_up.start()
    store_down.start()
    activation_out[...] = activation.astype(BF16)
    norm_out[0:1] = jnp.sum(normed_grad * unit, axis=0, keepdims=True)
    norm_out[1:2] = jnp.sum(normed_grad, axis=0, keepdims=True)
    middle_grad = incoming.astype(F32) + norm_back(normed_grad, gain[...], unit, scale)
    middle_grad_out[...] = middle_grad
    middle_low = middle_grad.astype(BF16)
    output_grad[...] = dot(mixed, middle_low).astype(BF16)
    store_output = pltpu.make_async_copy(output_grad, output_grad_hbm, stores.at[0])
    store_output.start()
    mixed_grad = dot(output_weight[...], middle_low, 1, 1).astype(BF16).astype(F32)
    for head in range(HEADS):
        part = slice(head * HEAD_DIM, (head + 1) * HEAD_DIM)
        factor = inverse[head : head + 1]
        mixed_grad_out[part, :] = (mixed_grad[part] * factor).astype(BF16)
        row_out[head : head + 1] = factor * jnp.sum(
            mixed_grad[part] * mixed_wide[part, :], axis=0, keepdims=True
        )
    store_up.wait()
    store_down.wait()
    store_output.wait()


def feed(mixed, inverse, stream, upstream, gain, shift, output_weight, up_weight, down_weight):
    rows, width = stream.shape
    hidden_width = up_weight.shape[1]
    vmem = pl.BlockSpec(memory_space=pltpu.VMEM)
    hbm = pl.BlockSpec(memory_space=pltpu.HBM)
    return pl.pallas_call(
        feed_kernel,
        in_specs=[vmem] * 6 + [hbm] * 3,
        out_specs=[vmem] * 5 + [hbm] * 3,
        out_shape=[
            jax.ShapeDtypeStruct((rows, width), BF16),
            jax.ShapeDtypeStruct((rows, width), F32),
            jax.ShapeDtypeStruct((2, width), F32),
            jax.ShapeDtypeStruct((width, rows), BF16),
            jax.ShapeDtypeStruct((HEADS, rows), F32),
            jax.ShapeDtypeStruct((width, width), BF16),
            jax.ShapeDtypeStruct((width, hidden_width), BF16),
            jax.ShapeDtypeStruct((hidden_width, width), BF16),
        ],
        scratch_shapes=[
            pltpu.VMEM((width, width), BF16),
            pltpu.VMEM((width, hidden_width), BF16),
            pltpu.VMEM((hidden_width, width), BF16),
            pltpu.VMEM((width, width), BF16),
            pltpu.VMEM((width, hidden_width), BF16),
            pltpu.VMEM((hidden_width, width), BF16),
            pltpu.SemaphoreType.DMA((3,)),
            pltpu.SemaphoreType.DMA((3,)),
        ],
        compiler_params=params(),
        name="feed",
    )(mixed, inverse, stream, upstream, gain, shift, output_weight, up_weight, down_weight)


def back_kernel(query, keys, values, marks, probs, mixed_grad, row_sums, query_out, key_out, value_out, left, right):
    rows = query.shape[1]
    group = keys.shape[0]
    blocks = group // KEY_BLOCK
    pair_columns(left, query, rows)
    pair_columns(right, mixed_grad, rows)
    kinds = lax.broadcasted_iota(jnp.int32, (128, rows), 0)
    for half in range(2):
        total = -row_sums[0, half : half + 1]
        high = total.astype(BF16)
        rest = (total - high.astype(F32)).astype(BF16)
        shape = (128, rows)
        fill = jnp.where(kinds == ONES, jnp.broadcast_to(high.astype(F32), shape), 0.0)
        fill = jnp.where(kinds == ONES + 1, jnp.broadcast_to(rest.astype(F32), shape), fill)
        right[128:256, half * rows : (half + 1) * rows] = fill.astype(BF16)

    def step(index, total):
        part = pl.ds(pl.multiple_of(index * KEY_BLOCK, KEY_BLOCK), KEY_BLOCK)
        weights = probs[part, :]
        inner = dot(jnp.concatenate([values[part, :], marks[part, :]], axis=1), right[...])
        score_grad = (weights.astype(F32) * inner).astype(BF16)
        key_out[part, :] = (dot(score_grad, left[...], 1, 1) * LN2).astype(BF16)
        value_out[part, :] = dot(weights, right[0:128, :], 1, 1).astype(BF16)
        return total + dot(keys[part, :].T, score_grad)

    total = lax.fori_loop(0, blocks, step, jnp.zeros((128, 2 * rows), F32))
    scale = HEAD_DIM**-0.5
    query_out[0:HEAD_DIM] = (total[0:HEAD_DIM, 0:rows] * scale).astype(BF16)
    query_out[HEAD_DIM:128] = (total[HEAD_DIM:128, rows : 2 * rows] * scale).astype(BF16)


def attend_back(query, keys, values, marks, probs, mixed_grad, row_sums):
    width, rows = query.shape
    group = keys.shape[0]
    pairs = width // 128
    column = pl.BlockSpec((group, 128), lambda pair: (0, pair))
    row = pl.BlockSpec((128, rows), lambda pair: (pair, 0))
    return pl.pallas_call(
        back_kernel,
        grid=(pairs,),
        in_specs=[
            row,
            column,
            column,
            whole((group, 128)),
            pl.BlockSpec((group, 2 * rows), lambda pair: (0, pair)),
            row,
            pl.BlockSpec((1, 2, rows), lambda pair: (pair, 0, 0)),
        ],
        out_specs=[row, column, column],
        out_shape=[
            jax.ShapeDtypeStruct((width, rows), BF16),
            jax.ShapeDtypeStruct((group, width), BF16),
            jax.ShapeDtypeStruct((group, width), BF16),
        ],
        scratch_shapes=[pltpu.VMEM((128, 2 * rows), BF16), pltpu.VMEM((256, 2 * rows), BF16)],
        compiler_params=params(),
        name="attend_back",
    )(query, keys, values, marks, probs, mixed_grad, row_sums)


def time_features(steps, width):
    half = width // 2
    freqs = jnp.exp(-math.log(10000.0) * jnp.arange(half, dtype=F32) / half)
    angles = steps.astype(F32)[:, None] * freqs[None, :]
    return jnp.concatenate([jnp.cos(angles), jnp.sin(angles)], axis=1)


def split_three(values):
    high = values.astype(BF16)
    rest = values - high.astype(F32)
    middle = rest.astype(BF16)
    return high, middle, (rest - middle.astype(F32)).astype(BF16)


def body(
    tokens,
    segments,
    live_lengths,
    timesteps,
    table,
    input_weight,
    time_first,
    time_second,
    first_gain,
    first_shift,
    query_weight,
    key_weight,
    value_weight,
    output_weight,
    second_gain,
    second_shift,
    up_weight,
    down_weight,
    upstream,
):
    head_count = lax.axis_size("head")
    seq_count = lax.axis_size("seq")
    blocks = head_count * seq_count
    rows = tokens.shape[0]
    width = query_weight.shape[0]
    shard_rows = table.shape[0]
    slot_count = live_lengths.shape[1]
    highest = lax.Precision.HIGHEST
    seq_index = lax.axis_index("seq")
    own = lax.axis_index("head") * seq_count + seq_index

    all_tokens, all_slots = (
        lax.all_gather(tokens, ("head", "seq"), axis=0, tiled=True),
        lax.all_gather(segments, ("head", "seq"), axis=0, tiled=True),
    )
    full_table = lax.all_gather(table, "seq", axis=0, tiled=True).astype(F32)
    mean_norm = jnp.sum(jnp.sqrt(jnp.sum(full_table * full_table, axis=1))) / VOCAB
    features = time_features(timesteps[0], time_first.shape[0])
    second_wide = time_second.astype(F32)
    time_hidden = jnp.dot(features, time_first.astype(F32), precision=highest)
    time_act = jax.nn.silu(time_hidden)
    time_out = jnp.dot(time_act, second_wide, precision=highest)
    time_rows = jnp.pad(time_out, ((0, SLOTS - slot_count), (0, 0)))
    entry = jnp.concatenate(
        [input_weight, *split_three(time_rows), jnp.zeros((SLOTS, width), BF16)], axis=0
    )
    lengths = jnp.pad(live_lengths.astype(F32), ((0, 0), (0, 128 - slot_count)))
    normed, keys, values, marks, stream, query, embed_low = embed(
        own[None],
        all_tokens,
        all_slots[:, None],
        lengths,
        mean_norm[None],
        full_table,
        entry,
        first_gain[None],
        first_shift[None],
        query_weight,
        key_weight,
        value_weight,
        blocks,
    )
    probs, mixed, inverse = attend(query, keys, values, marks, segments[None])
    activation, middle_grad, second_norm, mixed_grad, row_sums, output_grad, up_grad, down_grad = feed(
        mixed,
        inverse.reshape(HEADS, rows),
        stream,
        upstream,
        second_gain[None],
        second_shift[None],
        output_weight,
        up_weight,
        down_weight,
    )
    query_back, key_back, value_back = attend_back(
        query, keys, values, marks, probs, mixed_grad, row_sums.reshape(HEADS // 2, 2, rows)
    )
    own_normed = lax.dynamic_slice_in_dim(normed, own * rows, rows)
    query_grad = dot(own_normed, query_back, 0, 1)
    key_grad = dot(normed, key_back, 0, 0)
    value_grad = dot(normed, value_back, 0, 0)
    partial = dot(key_back, key_weight, 1, 1) + dot(value_back, value_weight, 1, 1)
    normed_grad = lax.psum_scatter(
        partial.astype(BF16), ("head", "seq"), scatter_dimension=0, tiled=True
    ).astype(F32) + dot(query_back, query_weight, 0, 1)

    def one_norm(values, gain, shift):
        unit, _ = norm_parts(values)
        return unit * gain + shift

    _, first_back = jax.vjp(one_norm, stream, first_gain, first_shift)
    stream_part, first_gain_grad, first_shift_grad = first_back(normed_grad)
    stream_grad = middle_grad + stream_part
    stream_low = stream_grad.astype(BF16)
    input_grad = dot(embed_low, stream_low, 0, 0)
    embed_grad = dot(stream_low, input_weight, 1, 1)
    picker = (segments[:, None] == jnp.arange(slot_count, dtype=jnp.int32)[None, :]).astype(F32)
    time_out_grad = contract_exact(picker, stream_grad)
    time_second_grad = contract_exact(time_act, time_out_grad)
    act_grad = lax.dot_general(
        time_out_grad, second_wide, (((1,), (1,)), ((), ())), precision=highest
    )
    _, silu_back = jax.vjp(jax.nn.silu, time_hidden)
    time_hidden_grad = silu_back(act_grad)[0]
    time_first_grad = contract_exact(features, time_hidden_grad)

    def reduce(value):
        part = lax.psum_scatter(value.astype(BF16), "dp", scatter_dimension=0, tiled=True)
        return lax.psum(part, ("head", "seq")).astype(F32)

    shards = [
        reduce(value)
        for value in (
            input_grad,
            time_first_grad,
            time_second_grad,
            query_grad,
            key_grad,
            value_grad,
            output_grad,
            up_grad,
            down_grad,
        )
    ]
    found = jnp.take(full_table, tokens, axis=0)
    mean_part = -jnp.sum(embed_grad * found) / (mean_norm * mean_norm)
    scaled_grad = embed_grad / mean_norm
    table_sum = jax.ops.segment_sum(scaled_grad, tokens, num_segments=VOCAB)
    small = lax.psum(
        (first_gain_grad, first_shift_grad, second_norm[0], second_norm[1], mean_part, table_sum),
        ("dp", "head", "seq"),
    )
    table_rows = lax.dynamic_slice_in_dim(small[5], seq_index * shard_rows, shard_rows)
    table_wide = table.astype(F32)
    row_norms = jnp.sqrt(jnp.sum(table_wide * table_wide, axis=1))
    table_grad = table_rows + small[4] / VOCAB * table_wide / row_norms[:, None]
    return (
        activation,
        embed_grad,
        table_grad,
        shards[0],
        shards[1],
        shards[2],
        small[0],
        small[1],
        shards[3],
        shards[4],
        shards[5],
        shards[6],
        small[2],
        small[3],
        shards[7],
        shards[8],
    )


def solution(mesh):
    tokens = P(("dp", "head", "seq"))
    wide = P(("dp", "head", "seq"), None)
    group = P("dp", None)
    return jax.shard_map(
        body,
        mesh=mesh,
        in_specs=(tokens, tokens, group, group, P("seq", None)) + (P(),) * 13 + (wide,),
        out_specs=(wide, wide, P("seq", None), group, group, group, P(), P())
        + (group,) * 4
        + (P(), P(), group, group),
        check_vma=False,
    )
```

time: 1140 us -> 923 us (0.81)
  matrix products: 214 us -> 43.8 us
  Pallas kernels: 0 us -> 123 us
  local copies, waits for them, and re-layouts: 82.1 us -> 23.6 us
  other arithmetic: 65.2 us -> 30.2 us
  waiting for transfers between devices: 646 us -> 618 us
  blocking collectives: 85.6 us -> 59.4 us
  starting transfers between devices: 19.2 us -> 1.14 us
    dot_general x65 -> x9, matrix products: 206 us -> 37.2 us  [the longest x8 36.9 us: dot(): lax.dot_general(left, right, (((left_dim,), (right_dim,)), ((), ())), pre...]
    pallas_call x0 -> x4, Pallas kernels: none -> 123 us  [the longest x1 38.7 us: attend_back(): pl.pallas_call(back_kernel, grid=(pairs,), in_specs=[row, column, column,...]
    all_to_all x3 -> x0, blocking collectives: 36.6 us -> none  [the longest x1 12.5 us: body(): lax.all_to_all(to_heads(values), 'head', split_axis=1, concat_axis=0, til...]
    unnamed x169 -> x76, local copies, waits for them, and re-layouts: 38.3 us -> 8.42 us
    all_gather x3 -> x1, waiting for transfers between devices: 21.5 us -> 0.01 us  [body(): full_table = lax.all_gather(table, 'seq', axis=0, tiled=True).astype(F32)]
    reshape x11 -> x2, local copies, waits for them, and re-layouts: 23 us -> 2.7 us  [the longest x1 1.36 us: body(): row_sums.reshape(HEADS // 2, 2, rows)]
    all_to_all x5 -> x0, waiting for transfers between devices: 19.4 us -> none  [the longest x1 9.02 us: body(): lax.all_to_all(to_heads(query), 'head', split_axis=1, concat_axis=0, tile...]
    all_to_all x5 -> x0, starting transfers between devices: 17.7 us -> none  [the longest x1 3.67 us: body(): lax.all_to_all(to_heads(query), 'head', split_axis=1, concat_axis=0, tile...]
  transfers between devices with their start and end apart: 22 -> 14, of which waited for: 17 -> 12; matrix products, arithmetic and copies ran while one was open for 9% -> 6% of each run, Pallas kernels for 0% -> 0%
where the time goes in v1:
time: 923 us; the launch traced here: 917 us
  waiting for transfers between devices  618 us (67%)
  Pallas kernels  123 us (13%)
  blocking collectives  59.4 us (6%)
  matrix products  43.8 us (5%)
  other arithmetic  30.2 us (3%)
  local copies, waits for them, and re-layouts  23.6 us (3%)
  between operations  17.6 us (2%)
    reduce_scatter x9, waiting for transfers between devices, reduce(): lax.psum_scatter(value.astype(BF16), 'dp', scatter_dimension=0, tiled=True)  331 us
    psum x1, waiting for transfers between devices, body(): lax.psum((first_gain_grad, first_shift_grad, second_norm[0], second_norm[...  145 us
    psum x2, waiting for transfers between devices, reduce(): return lax.psum(part, ('head', 'seq')).astype(F32)  89.7 us
    reduce_scatter x1, waiting for transfers between devices, body(): lax.psum_scatter(partial.astype(BF16), ('head', 'seq'), scatter_dimension...  49.7 us
    psum x1, blocking collectives, body(): lax.psum((first_gain_grad, first_shift_grad, second_norm[0], second_norm[...  39.4 us
    pallas_call x1, Pallas kernels, attend_back(): pl.pallas_call(back_kernel, grid=(pairs,), in_specs=[row, column, column,...  38.7 us
    dot_general x8, matrix products, dot(): lax.dot_general(left, right, (((left_dim,), (right_dim,)), ((), ())), pre...  36.9 us
    pallas_call x1, Pallas kernels, attend(): pl.pallas_call(forward_kernel, grid=(pairs,), in_specs=[pl.BlockSpec((128...  34.2 us
  transfers between devices with their start and end apart: 14, of which 12 were waited for; matrix products, arithmetic and copies ran while one was open for 6% of the time, Pallas kernels for 0%

profile of v1, /device:TPU:0, one launch (start us, length us, event | category | flops | bytes accessed | tf_op | source)
XLA Modules:
  0.0 917.0 jit_solution(14711847010993581542)
XLA Ops:
  16.4 10.3 %all-gather.1 = s32[8,1,384]{2,1,0:T(1,128)S(1)} all-gather(s32[1,1,384]{2,1,0:T(1,128)S(1)} %reshape.111), channel_id=1, replica_groups=mesh['dp'=4,'head'=2,'seq'=4] {'head','seq'}, dimensions={0}, use_global_device_ids=true | all-gather | bytes 13824 | tf_op jit(solution)/shard_map/all_gather | solution.py:481
  28.9 9.7 %all-gather = s32[8,1,384]{2,1,0:T(1,128)} all-gather(s32[1,1,384]{2,1,0:T(1,128)S(1)} %reshape.109), channel_id=1, replica_groups=mesh['dp'=4,'head'=2,'seq'=4] {'head','seq'}, dimensions={0}, use_global_device_ids=true | all-gather | bytes 13824 | tf_op jit(solution)/shard_map/all_gather | solution.py:480
  43.5 2.9 multiply_reduce_fusion
  47.6 2.4 convert_element_type.96.table
  49.9 26.3 %embed.1 = (bf16[3072,768]{1,0:T(8,128)(2,1)}, bf16[3072,768]{1,0:T(8,128)(2,1)}, bf16[3072,768]{1,0:T(8,128)(2,1)}, bf16[3072,128]{1,0:T(8,128)(2,1)}, f32[384,...) custom-call(s32[1]{0:T(128)} %bitcast.own, s32[3072]{0:T(1024)} %bitcast.25, ...), custom_call_target="tpu_custom_call" | custom-call | tf_op jit(solution)/shard_map/embed/pallas_call | solution.py:134
  76.3 34.2 %attend.1 = (bf16[3072,4608]{1,0:T(8,128)(2,1)}, f32[768,384]{1,0:T(8,128)}, f32[6,2,384]{2,1,0:T(2,128)}) custom-call(bf16[768,384]{1,0:T(8,128)(2,1)} %get-tuple-element.37.query, bf16[3072,768]{1,0:T(8,128)(2,1)} %get-tuple-element.38.keys, bf16[3072,768]{1,0:T(8,128)(2,1)} %get-tuple-element.39.values, bf16[3072,128]{1,0:T(8,128)(2,1)} %get-tuple-element.40.marks, ...), custom_call_target="tpu_custom_call" | custom-call | tf_op jit(solution)/shard_map/attend/pallas_call | solution.py:226
  111.8 24.0 %feed.1 = (bf16[384,768]{1,0:T(8,128)(2,1)}, f32[384,768]{1,0:T(8,128)}, f32[2,768]{1,0:T(2,128)}, bf16[768,384]{1,0:T(8,128)(2,1)}, f32[12,384]{1,0:T(8,128)}, ...) custom-call(f32[768,384]{1,0:T(8,128)} %get-tuple-element.41.mixed_wide, ...), custom_call_target="tpu_custom_call" | custom-call | tf_op jit(solution)/shard_map/feed/pallas_call | solution.py:343
  137.2 38.7 %attend_back.1 = (bf16[768,384]{1,0:T(8,128)(2,1)}, bf16[3072,768]{1,0:T(8,128)(2,1)}, bf16[3072,768]{1,0:T(8,128)(2,1)}) custom-call(bf16[768,384]{1,0:T(8,128)(2,1)} %get-tuple-element.37.query, bf16[3072,768]{1,0:T(8,128)(2,1)} %get-tuple-element.38.keys, bf16[3072,768]{1,0:T(8,128)(2,1)} %get-tuple-element.39.values, ...), custom_call_target="tpu_custom_call" | custom-call | tf_op jit(solution)/shard_map/attend_back/pallas_call | solution.py:409
  175.9 6.0 fusion.36
  181.9 5.7 add_convert_fusion
  192.3 49.7 %reduce-scatter.11.cloned.1.call-done = bf16[384,768]{1,0:T(8,128)(2,1)} async-done(((bf16[3072,768]{1,0:T(8,128)(2,1)}), bf16[384,768]{1,0:T(8,128)(2,1)}) %reduce-scatter.11.cloned.1.call-update) | async-done | bytes 589840 | tf_op jit(solution)/shard_map/reduce_scatter | solution.py:530
  242.1 3.0 multiply_reduce_fusion.1
  252.1 2.9 convolution_convert_fusion.2
  255.5 8.7 convolution_convert_fusion
  264.2 8.7 convolution_convert_fusion.1
  274.3 3.1 convolution_convert_fusion.3
  277.6 3.3 gather_fusion
  280.9 7.8 reduce-scatter.15.cloned.1.call-done
  289.7 4.0 scatter_custom_fusion
  294.0 24.4 %reduce-scatter.25.cloned.1.call-done = bf16[192,768]{1,0:T(8,128)(2,1)} async-done(((bf16[768,768]{1,0:T(8,128)(2,1)}), bf16[192,768]{1,0:T(8,128)(2,1)}) %reduce-scatter.25.cloned.1.call-update) | async-done | bytes 294928 | tf_op jit(solution)/shard_map/reduce_scatter | solution.py:555
  318.4 30.8 %reduce-scatter.19.cloned.1.call-done = bf16[192,768]{1,0:T(8,128)(2,1)} async-done(((bf16[768,768]{1,0:T(8,128)(2,1)}), bf16[192,768]{1,0:T(8,128)(2,1)}) %reduce-scatter.19.cloned.1.call-update) | async-done | bytes 294928 | tf_op jit(solution)/shard_map/reduce_scatter | solution.py:555
  349.2 30.3 %reduce-scatter.23.cloned.1.call-done = bf16[192,768]{1,0:T(8,128)(2,1)} async-done(((bf16[768,768]{1,0:T(8,128)(2,1)}), bf16[192,768]{1,0:T(8,128)(2,1)}) %reduce-scatter.23.cloned.1.call-update) | async-done | bytes 294928 | tf_op jit(solution)/shard_map/reduce_scatter | solution.py:555
  379.5 30.3 %reduce-scatter.21.cloned.1.call-done = bf16[192,768]{1,0:T(8,128)(2,1)} async-done(((bf16[768,768]{1,0:T(8,128)(2,1)}), bf16[192,768]{1,0:T(8,128)(2,1)}) %reduce-scatter.21.cloned.1.call-update) | async-done | bytes 294928 | tf_op jit(solution)/shard_map/reduce_scatter | solution.py:555
  409.9 86.4 %reduce-scatter.27.cloned.1.call-done = bf16[192,3072]{1,0:T(8,128)(2,1)} async-done(((bf16[768,3072]{1,0:T(8,128)(2,1)}), bf16[192,3072]{1,0:T(8,128)(2,1)}) %reduce-scatter.27.cloned.1.call-update) | async-done | bytes 1179664 | tf_op jit(solution)/shard_map/reduce_scatter | solution.py:555
  496.3 88.1 %reduce-scatter.29.cloned.1.call-done = bf16[768,768]{1,0:T(8,128)(2,1)} async-done(((bf16[3072,768]{1,0:T(8,128)(2,1)}), bf16[768,768]{1,0:T(8,128)(2,1)}) %reduce-scatter.29.cloned.1.call-update) | async-done | bytes 1179664 | tf_op jit(solution)/shard_map/reduce_scatter | solution.py:555
  584.3 32.7 %reduce-scatter.17.cloned.1.call-done = bf16[192,768]{1,0:T(8,128)(2,1)} async-done(((bf16[768,768]{1,0:T(8,128)(2,1)}), bf16[192,768]{1,0:T(8,128)(2,1)}) %reduce-scatter.17.cloned.1.call-update) | async-done | bytes 294928 | tf_op jit(solution)/shard_map/reduce_scatter | solution.py:555
  620.4 39.4 %all-reduce.2 = (f32[]{:T(128)}, f32[768]{0:T(1024)}, f32[768]{0:T(1024)}, f32[768]{0:T(1024)}, f32[768]{0:T(1024)}) all-reduce(f32[]{:T(128)S(6)} %div.64, f32[768]{0:T(1024)S(1)} %copy-done.32, f32[768]{0:T(1024)S(1)} %copy-done.33, f32[768]{0:T(1024)S(1)} %get-tuple-element.62, ...), channel_id=1, replica_groups=mesh['dp'=4,'head'=2,'seq'=4] {'dp','head','seq'}, use_global_device_ids=true, to_apply=%region_10.11 | all-reduce | flops 3073 | bytes 24584 | tf_op jit(solution)/shard_map/psum | solution.py:576
  660.4 10.4 %all-reduce.11.cloned.1.call-done = (bf16[32,768]{1,0:T(8,128)(2,1)}, bf16[32,768]{1,0:T(8,128)(2,1)}) async-done(((bf16[32,768]{1,0:T(8,128)(2,1)}, bf16[32,768]{1,0:T(8,128)(2,1)}), (bf16[32,768]{1,0:T(8,128)(2,1)}, bf16[32,768]{1,0:T(8,128)(2,1)})) %all-reduce.11.cloned.1.call-update) | async-done | bytes 98320 | tf_op jit(solution)/shard_map/psum | solution.py:556
  673.8 145.1 %all-reduce.9.cloned.1.call-done = f32[8192,128]{1,0:T(8,128)} async-done(((f32[8192,128]{1,0:T(8,128)}), f32[8192,128]{1,0:T(8,128)}) %all-reduce.9.cloned.1.call-update) | async-done | bytes 4194320 | tf_op jit(solution)/shard_map/psum | solution.py:576
  818.9 2.5 fusion.3
  821.4 79.3 %all-reduce.13.cloned.1.call-done = (bf16[192,768]{1,0:T(8,128)(2,1)}, bf16[192,768]{1,0:T(8,128)(2,1)}, bf16[192,768]{1,0:T(8,128)(2,1)}, bf16[192,768]{1,0:T(8...) async-done(((bf16[192,768]{1,0:T(8,128)(2,1)}, bf16[192,768]{1,0:T(8,128)(2,1)}, bf16[192,768]{1,0:T(8,128)(2,1)}, ...) | async-done | bytes 3833872 | tf_op jit(solution)/shard_map/psum | solution.py:556
  900.7 1.9 convert_element_type.113
  (152 shorter events, 46.3 us)
Async XLA Ops:
  7.2 33.1 %copy-start = (bf16[768,768]{1,0:T(8,128)(2,1)S(1)}, bf16[768,768]{1,0:T(8,128)(2,1)}, u32[]{:S(2)}) copy-start(bf16[768,768]{1,0:T(8,128)(2,1)} %param.26) | copy-start | bytes 3538948
  7.2 31.4 %copy-start.13 = (bf16[128,768]{1,0:T(8,128)(2,1)S(1)}, bf16[128,768]{1,0:T(8,128)(2,1)}, u32[]{:S(2)}) copy-start(bf16[128,768]{1,0:T(8,128)(2,1)} %param.24) | copy-start | bytes 589828
  7.2 32.1 %copy-start.35 = (s32[1,25]{1,0:T(1,128)S(1)}, s32[1,25]{1,0:T(1,128)}, u32[]{:S(2)}) copy-start(s32[1,25]{1,0:T(1,128)} %param.22) | copy-start | bytes 304
  7.2 36.3 %all-gather.4.cloned.1.call-start = ((), (), s32[]{:S(2)}) async-start(), calls=%async_computation.10 | async-start | bytes 2621440 | tf_op jit(solution)/shard_map/all_gather | solution.py:483
  8.0 32.1 %copy-start.19 = (bf16[128,768]{1,0:T(8,128)(2,1)S(1)}, bf16[128,768]{1,0:T(8,128)(2,1)}, u32[]{:S(2)}) copy-start(bf16[128,768]{1,0:T(8,128)(2,1)} %param.25) | copy-start | bytes 589828
  8.0 234.1 %reduce-scatter.11.cloned.1.call-start = ((), (), s32[]{:S(2)}) async-start(), calls=%async_computation.11 | async-start | bytes 5308416 | tf_op jit(solution)/shard_map/reduce_scatter | solution.py:530
  43.5 4.1 copy-start.2
  137.2 38.7 %copy-start.4 = (bf16[768,768]{1,0:T(8,128)(2,1)S(1)}, bf16[768,768]{1,0:T(8,128)(2,1)}, u32[]{:S(2)}) copy-start(bf16[768,768]{1,0:T(8,128)(2,1)} %key_weight.1) | copy-start | bytes 3538948
  175.9 6.0 copy-start.5
  175.9 6.0 copy-start.34
  187.7 54.4 %copy-start.6 = (bf16[768,768]{1,0:T(8,128)(2,1)S(1)}, bf16[768,768]{1,0:T(8,128)(2,1)}, u32[]{:S(2)}) copy-start(bf16[768,768]{1,0:T(8,128)(2,1)} %query_weight.1) | copy-start | bytes 3538948
  187.7 93.2 %reduce-scatter.13.cloned.1.call-start = ((), (), s32[]{:S(2)}) async-start(), calls=%async_computation.13 | async-start | bytes 245760 | tf_op jit(solution)/shard_map/reduce_scatter | solution.py:555
  242.1 3.0 copy-start.30
  248.9 39.8 %reduce-scatter.15.cloned.1.call-start = ((), (), s32[]{:S(2)}) async-start(), calls=%async_computation.14 | async-start | bytes 245760 | tf_op jit(solution)/shard_map/reduce_scatter | solution.py:555
  251.4 67.0 %reduce-scatter.25.cloned.1.call-start = ((), (), s32[]{:S(2)}) async-start(), calls=%async_computation.19 | async-start | bytes 1474560 | tf_op jit(solution)/shard_map/reduce_scatter | solution.py:555
  252.0 97.2 %reduce-scatter.19.cloned.1.call-start = ((), (), s32[]{:S(2)}) async-start(), calls=%async_computation.16 | async-start | bytes 1474560 | tf_op jit(solution)/shard_map/reduce_scatter | solution.py:555
  255.0 124.5 %reduce-scatter.23.cloned.1.call-start = ((), (), s32[]{:S(2)}) async-start(), calls=%async_computation.18 | async-start | bytes 1474560 | tf_op jit(solution)/shard_map/reduce_scatter | solution.py:555
  264.2 145.7 %reduce-scatter.21.cloned.1.call-start = ((), (), s32[]{:S(2)}) async-start(), calls=%async_computation.17 | async-start | bytes 1474560 | tf_op jit(solution)/shard_map/reduce_scatter | solution.py:555
  273.0 223.3 %reduce-scatter.27.cloned.1.call-start = ((), (), s32[]{:S(2)}) async-start(), calls=%async_computation.20 | async-start | bytes 5898240 | tf_op jit(solution)/shard_map/reduce_scatter | solution.py:555
  273.7 310.6 %reduce-scatter.29.cloned.1.call-start = ((), (), s32[]{:S(2)}) async-start(), calls=%async_computation.21 | async-start | bytes 5898240 | tf_op jit(solution)/shard_map/reduce_scatter | solution.py:555
  274.3 3.2 copy-start.28
  274.3 342.8 %reduce-scatter.17.cloned.1.call-start = ((), (), s32[]{:S(2)}) async-start(), calls=%async_computation.15 | async-start | bytes 1474560 | tf_op jit(solution)/shard_map/reduce_scatter | solution.py:555
  277.5 11.3 %copy-start.14 = (bf16[128,768]{1,0:T(8,128)(2,1)S(1)}, bf16[128,768]{1,0:T(8,128)(2,1)}, u32[]{:S(2)}) copy-start(bf16[128,768]{1,0:T(8,128)(2,1)} %param.24) | copy-start | bytes 589828
  277.5 393.4 %all-reduce.11.cloned.1.call-start = ((), (), s32[]{:S(2)}) async-start(), calls=%async_computation.22 | async-start | bytes 196608 | tf_op jit(solution)/shard_map/psum | solution.py:556
  288.7 530.2 %all-reduce.9.cloned.1.call-start = ((), (), s32[]{:S(2)}) async-start(), calls=%async_computation.12 | async-start | bytes 8388608 | tf_op jit(solution)/shard_map/psum | solution.py:576
  289.7 4.0 copy-start.12
  293.8 607.0 %all-reduce.13.cloned.1.call-start = ((), (), s32[]{:S(2)}) async-start(), calls=%async_computation.23 | async-start | bytes 7667712 | tf_op jit(solution)/shard_map/psum | solution.py:556
  617.1 3.3 copy-start.32
  617.1 3.3 copy-start.33
  900.7 3.7 copy-start.18
  900.7 4.6 copy-start.17
  902.6 3.6 copy-start.16
  (18 other events, 31.6 us)
Sparse Core Ops, SparseCore 0:
  9.6 25.3 all-gather.3
  187.8 54.1 reduce-scatter.10
  249.0 19.3 reduce-scatter.12
  271.1 17.5 reduce-scatter.14
  291.0 27.4 reduce-scatter.24
  321.3 27.8 reduce-scatter.18
  351.6 27.8 reduce-scatter.22
  382.0 27.8 reduce-scatter.20
  412.3 83.9 reduce-scatter.26
  498.5 85.7 reduce-scatter.28
  587.4 29.6 reduce-scatter.16
  620.4 50.4 all-reduce.10
  676.4 142.4 all-reduce.8
  823.0 77.6 all-reduce.12

commit v2 on v1

--- a/solution.py
+++ b/solution.py
@@ -20,6 +20,9 @@
 DEAD = 25
 ONES = 32
 VMEM_LIMIT = 60 * 2**20
+PIECE = 96
+UNIT = (2, 2, 2, 4, PIECE, 768)
+MESH = pl.DeviceIdType.MESH
 
 F32 = jnp.float32
 BF16 = jnp.bfloat16
@@ -56,14 +59,133 @@
     return scale * (inner - unit * jnp.mean(scaled * unit, axis=-1, keepdims=True))
 
 
+def place():
+    seq = lax.axis_index("seq")
+    return lax.axis_index("dp"), lax.axis_index("head"), lax.div(seq, 2), lax.rem(seq, 2)
+
+
+def device(z, x, y, c):
+    return (z, x, y * 2 + c)
+
+
+def neighbours():
+    z, x, y, c = place()
+    planes = lax.axis_size("dp")
+    near = [device(z, x, y, 1 - c), device(z, 1 - x, y, c), device(z, x, 1 - y, c)]
+    return near, [device(lax.rem(z + step, planes), x, y, c) for step in range(1, planes)]
+
+
+def greet(devices):
+    barrier = pltpu.get_barrier_semaphore()
+    for other in devices:
+        pl.semaphore_signal(barrier, inc=1, device_id=other, device_id_type=MESH)
+    pl.semaphore_wait(barrier, len(devices))
+
+
+def send(source, target, sems, slot, other):
+    return pltpu.make_async_remote_copy(
+        src_ref=source,
+        dst_ref=target,
+        send_sem=sems[0].at[slot],
+        recv_sem=sems[1].at[slot],
+        device_id=other,
+        device_id_type=MESH,
+    )
+
+
+def gather_kernel(table, notes, full, notes_all, steps_all, mean_out, sums, local, *sems):
+    z, x, y, c = place()
+    seq = y * 2 + c
+    own = x * 4 + seq
+    near, planes = neighbours()
+    others = []
+    for flip in range(1, 8):
+        xx, yy, cc = flip // 4, (flip // 2) % 2, flip % 2
+        others.append(device(z, x + xx - 2 * xx * x, y + yy - 2 * yy * y, c + cc - 2 * cc * c))
+    greet(others + planes)
+    keep = pltpu.make_async_copy(table, full.at[seq], local.at[0])
+    keep.start()
+    tables = [
+        send(table, full.at[seq], sems, 0, near[2]),
+        send(table, full.at[seq], sems, 1, near[0]),
+    ]
+    for copy in tables:
+        copy.start()
+    notes_all[own] = notes[...]
+    steps_all[z] = notes[...]
+    copies = [
+        send(notes, notes_all.at[own], sems, 3 + index, other) for index, other in enumerate(others)
+    ]
+    copies += [
+        send(notes, steps_all.at[z], sems, 13 + index, other) for index, other in enumerate(planes)
+    ]
+    for copy in copies:
+        copy.start()
+    wide = table[...].astype(F32)
+    norms = jnp.sqrt(jnp.sum(wide * wide, axis=1, keepdims=True))
+    total = jnp.sum(norms, axis=0, keepdims=True)
+    sums[seq] = jnp.broadcast_to(total, (8, 128))
+    partials = [
+        send(sums.at[seq], sums.at[seq], sems, 10 + index, other)
+        for index, other in enumerate((near[0], near[2], device(z, x, 1 - y, 1 - c)))
+    ]
+    for copy in partials:
+        copy.start()
+    tables[0].wait_recv()
+    away = (1 - y) * 2 + c
+    forward = send(full.at[away], full.at[away], sems, 2, near[0])
+    forward.start()
+    keep.wait()
+    for copy in copies + partials:
+        copy.wait()
+    mean_out[...] = jnp.sum(sums[...], axis=0) * (1.0 / VOCAB)
+    tables[1].wait_recv()
+    forward.wait()
+    for copy in tables:
+        copy.wait_send()
+
+
+def gather(table, notes):
+    rows, width = table.shape
+    planes = lax.axis_size("dp")
+    vmem = pl.BlockSpec(memory_space=pltpu.VMEM)
+    hbm = pl.BlockSpec(memory_space=pltpu.HBM)
+    slots = 13 + planes - 1
+    return pl.pallas_call(
+        gather_kernel,
+        in_specs=[vmem, vmem],
+        out_specs=[hbm, vmem, vmem, vmem],
+        out_shape=[
+            jax.ShapeDtypeStruct((4, rows, width), BF16),
+            jax.ShapeDtypeStruct((8, 8, 128), jnp.int32),
+            jax.ShapeDtypeStruct((planes, 8, 128), jnp.int32),
+            jax.ShapeDtypeStruct((8, 128), F32),
+        ],
+        scratch_shapes=[
+            pltpu.VMEM((4, 8, 128), F32),
+            pltpu.SemaphoreType.DMA((1,)),
+            pltpu.SemaphoreType.DMA((slots,)),
+            pltpu.SemaphoreType.DMA((slots,)),
+        ],
+        compiler_params=params(collective_id=0, has_side_effects=True),
+        name="gather",
+    )(table, notes)
+
+
+def column_of(row):
+    size = row.shape[1]
+    shape = (size, size)
+    same = lax.broadcasted_iota(jnp.int32, shape, 0) == lax.broadcasted_iota(jnp.int32, shape, 1)
+    return jnp.sum(jnp.where(same, jnp.broadcast_to(row, shape), 0.0), axis=1, keepdims=True)
+
+
 def embed_kernel(
     own,
     tokens,
-    slots,
-    all_slots,
+    notes,
     lengths,
     mean_norm,
-    table,
+    table_low,
     entry,
     gain,
     shift,
@@ -77,37 +199,53 @@
     stream_out,
     query_out,
     low_out,
+    found_out,
     picked,
     limits,
+    table,
 ):
     step = pl.program_id(0)
     blocks = pl.num_programs(0)
     rows = picked.shape[0]
+    width = stream_out.shape[1]
     block = lax.rem(own[0] + step, blocks)
     base = block * rows
 
     @pl.when(step == 0)
     def _():
-        lanes = lax.broadcasted_iota(jnp.int32, (all_slots.shape[0], 128), 1)
-        below = jnp.where(all_slots[...] < lanes, 1.0, 0.0)
-        limits[...] = jnp.sum(below, axis=0, keepdims=True) + lengths[...]
-
-    def pick(index, carry):
-        for inner in range(8):
-            row = index * 8 + inner
-            picked[pl.ds(row, 1), :] = table[pl.ds(tokens[base + row], 1), :]
-        return carry
-
-    lax.fori_loop(0, rows // 8, pick, 0)
-    low = (picked[...] / mean_norm[0]).astype(BF16)
+        kinds = lax.broadcasted_iota(jnp.int32, (128, 128), 0)
+        below = jnp.zeros((128, 128), F32)
+        for part in range(blocks if isinstance(blocks, int) else 8):
+            for line in range(3, 6):
+                below = below + jnp.where(notes[part, line : line + 1, :] < kinds, 1.0, 0.0)
+        starts = jnp.sum(below, axis=1, keepdims=True)
+        shape = (128, 128)
+        same = lax.broadcasted_iota(jnp.int32, shape, 0) == lax.broadcasted_iota(jnp.int32, shape, 1)
+        starts = jnp.sum(jnp.where(same, jnp.broadcast_to(starts, shape), 0.0), axis=0, keepdims=True)
+        limits[...] = starts + lengths[...]
+        for part in range(4):
+            table[part * 2048 : (part + 1) * 2048, :] = table_low[part].astype(F32)
+
+    for line in range(3):
+
+        def pick(index, carry):
+            for inner in range(8):
+                row = index * 8 + inner
+                picked[pl.ds(line * 128 + row, 1), :] = table[pl.ds(tokens[block, line, row], 1), :]
+            return carry
+
+        lax.fori_loop(0, 16, pick, 0)
+    low = (picked[...] / mean_norm[0:1]).astype(BF16)
     lanes = lax.broadcasted_iota(jnp.int32, (rows, 128), 1)
-    slot = slots[...]
-    same = jnp.where((lanes & (SLOTS - 1)) == slot, 1.0, 0.0)
+    slot = jnp.concatenate(
+        [column_of(notes[block, line : line + 1, :].astype(F32)) for line in range(3, 6)], axis=0
+    )
+    same = jnp.where((lanes & (SLOTS - 1)).astype(F32) == slot, 1.0, 0.0)
     spread = jnp.where(lanes < 3 * SLOTS, same, 0.0).astype(BF16)
     stream = dot(jnp.concatenate([low, spread], axis=1), entry[...])
     unit, _ = norm_parts(stream)
-    normed = (unit * gain[...] + shift[...]).astype(BF16)
-    normed_out[...] = normed
+    normed = (unit * gain[...].reshape(1, width) + shift[...].reshape(1, width)).astype(BF16)
+    normed_out[...] = normed.T
     key_out[...] = dot(normed, key_weight[...]).astype(BF16)
     value_out[...] = dot(normed, value_weight[...]).astype(BF16)
     first = jnp.where(lanes < SLOTS, same, 0.0)
@@ -122,56 +260,62 @@
     def _():
         stream_out[...] = stream
         low_out[...] = low
+        found_out[...] = picked[...].astype(BF16)
         query = dot(query_weight[...], normed, 0, 1) * (LOG2E / math.sqrt(HEAD_DIM))
         query_out[...] = query.astype(BF16)
 
 
-def embed(own, tokens, slots, lengths, mean_norm, table, entry, gain, shift, wq, wk, wv, blocks):
-    group = tokens.shape[0]
-    rows = group // blocks
+def embed(own, notes, lengths, mean_norm, table, entry, gain, shift, wq, wk, wv, rows, blocks):
+    group = rows * blocks
     width = wq.shape[0]
-    turn = lambda step, own, tokens: (lax.rem(own[0] + step, blocks), 0)
+    turn = lambda step, own: (lax.rem(own[0] + step, blocks), 0)
     return pl.pallas_call(
         embed_kernel,
         grid_spec=pltpu.PrefetchScalarGridSpec(
-            num_scalar_prefetch=2,
+            num_scalar_prefetch=1,
             grid=(blocks,),
             in_specs=[
-                pl.BlockSpec((rows, 1), turn),
-                whole((group, 1)),
+                pl.BlockSpec(memory_space=pltpu.SMEM),
+                whole(notes.shape),
                 whole((1, 128)),
-                pl.BlockSpec(memory_space=pltpu.SMEM),
+                whole((8, 128)),
                 whole(table.shape),
                 whole(entry.shape),
-                whole((1, width)),
-                whole((1, width)),
+                whole((width,)),
+                whole((width,)),
                 whole((width, width)),
                 whole((width, width)),
                 whole((width, width)),
             ],
             out_specs=[
-                pl.BlockSpec((rows, width), turn),
+                pl.BlockSpec((width, rows), lambda *args: turn(*args)[::-1]),
                 pl.BlockSpec((rows, width), turn),
                 pl.BlockSpec((rows, width), turn),
                 pl.BlockSpec((rows, 128), turn),
                 whole((rows, width)),
                 whole((width, rows)),
                 whole((rows, 128)),
+                whole((rows, 128)),
             ],
-            scratch_shapes=[pltpu.VMEM((rows, 128), F32), pltpu.VMEM((1, 128), F32)],
+            scratch_shapes=[
+                pltpu.VMEM((rows, 128), F32),
+                pltpu.VMEM((1, 128), F32),
+                pltpu.VMEM((VOCAB, 128), F32),
+            ],
         ),
         out_shape=[
-            jax.ShapeDtypeStruct((group, width), BF16),
+            jax.ShapeDtypeStruct((width, group), BF16),
             jax.ShapeDtypeStruct((group, width), BF16),
             jax.ShapeDtypeStruct((group, width), BF16),
             jax.ShapeDtypeStruct((group, 128), BF16),
             jax.ShapeDtypeStruct((rows, width), F32),
             jax.ShapeDtypeStruct((width, rows), BF16),
             jax.ShapeDtypeStruct((rows, 128), BF16),
+            jax.ShapeDtypeStruct((rows, 128), BF16),
         ],
         compiler_params=params(),
         name="embed",
-    )(own, tokens, slots, slots, lengths, mean_norm, table, entry, gain, shift, wq, wk, wv)
+    )(own, notes, notes, lengths, mean_norm, table, entry, gain, shift, wq, wk, wv)
 
 
 def pair_columns(target, pair, rows):
@@ -278,7 +422,7 @@
 ):
     rows, width = stream.shape
     hidden_width = up_weight.shape[1]
-    chunk = 512
+    chunk = width
     chunks = hidden_width // chunk
     load_output = pltpu.make_async_copy(output_hbm, output_weight, loads.at[0])
     load_up = pltpu.make_async_copy(up_hbm, up_weight, loads.at[1])
@@ -290,7 +434,8 @@
     load_output.wait()
     middle = stream[...] + dot(mixed, output_weight[...], 0, 0)
     unit, scale = norm_parts(middle)
-    normed = (unit * gain[...] + shift[...]).astype(BF16)
+    wide_gain = gain[...].reshape(1, width)
+    normed = (unit * wide_gain + shift[...].reshape(1, width)).astype(BF16)
     normed_t = normed.T
     load_up.wait()
     load_down.wait()
@@ -306,8 +451,12 @@
         back = dot(incoming, down_weight[part, :], 1, 1)
         pre_grad = (back * slope).astype(BF16)
         activation = activation + dot(hidden, down_weight[part, :])
-        down_grad[part, :] = dot(hidden, incoming, 0, 0).astype(BF16)
-        up_grad[:, part] = dot(normed_t, pre_grad).astype(BF16)
+        down_grad[:, :, :, index] = (
+            dot(hidden, incoming, 0, 0).astype(BF16).reshape(2, 2, 2, PIECE, width)
+        )
+        up_part = dot(normed_t, pre_grad).astype(BF16).reshape(4, 2, PIECE, width)
+        for half in range(2):
+            up_grad[index // 2, index % 2, half] = up_part[:, half]
         normed_grad = normed_grad + dot(pre_grad, up_weight[:, part], 1, 1)
     store_up = pltpu.make_async_copy(up_grad, up_grad_hbm, stores.at[1])
     store_down = pltpu.make_async_copy(down_grad, down_grad_hbm, stores.at[2])
@@ -316,10 +465,12 @@
     activation_out[...] = activation.astype(BF16)
     norm_out[0:1] = jnp.sum(normed_grad * unit, axis=0, keepdims=True)
     norm_out[1:2] = jnp.sum(normed_grad, axis=0, keepdims=True)
-    middle_grad = incoming.astype(F32) + norm_back(normed_grad, gain[...], unit, scale)
+    middle_grad = incoming.astype(F32) + norm_back(normed_grad, wide_gain, unit, scale)
     middle_grad_out[...] = middle_grad
     middle_low = middle_grad.astype(BF16)
-    output_grad[...] = dot(mixed, middle_low).astype(BF16)
+    output_part = dot(mixed, middle_low).astype(BF16).reshape(4, 2, PIECE, width)
+    for half in range(2):
+        output_grad[half] = output_part[:, half]
     store_output = pltpu.make_async_copy(output_grad, output_grad_hbm, stores.at[0])
     store_output.start()
     mixed_grad = dot(output_weight[...], middle_low, 1, 1).astype(BF16).astype(F32)
@@ -350,17 +501,17 @@
             jax.ShapeDtypeStruct((2, width), F32),
             jax.ShapeDtypeStruct((width, rows), BF16),
             jax.ShapeDtypeStruct((HEADS, rows), F32),
-            jax.ShapeDtypeStruct((width, width), BF16),
-            jax.ShapeDtypeStruct((width, hidden_width), BF16),
-            jax.ShapeDtypeStruct((hidden_width, width), BF16),
+            jax.ShapeDtypeStruct((2, 4, PIECE, width), BF16),
+            jax.ShapeDtypeStruct(UNIT, BF16),
+            jax.ShapeDtypeStruct(UNIT, BF16),
         ],
         scratch_shapes=[
             pltpu.VMEM((width, width), BF16),
             pltpu.VMEM((width, hidden_width), BF16),
             pltpu.VMEM((hidden_width, width), BF16),
-            pltpu.VMEM((width, width), BF16),
-            pltpu.VMEM((width, hidden_width), BF16),
-            pltpu.VMEM((hidden_width, width), BF16),
+            pltpu.VMEM((2, 4, PIECE, width), BF16),
+            pltpu.VMEM(UNIT, BF16),
+            pltpu.VMEM(UNIT, BF16),
             pltpu.SemaphoreType.DMA((3,)),
             pltpu.SemaphoreType.DMA((3,)),
         ],
@@ -369,65 +520,802 @@
     )(mixed, inverse, stream, upstream, gain, shift, output_weight, up_weight, down_weight)
 
 
-def back_kernel(query, keys, values, marks, probs, mixed_grad, row_sums, query_out, key_out, value_out, left, right):
-    rows = query.shape[1]
+def add_into(target, other, lead):
+    for index in lead:
+        total = target[index].astype(F32) + other[index].astype(F32)
+        target[index] = total.astype(BF16)
+
+
+class Plane:
+    def __init__(self, unit, buffers, loaded, sems):
+        self.unit, self.sems = unit, sems
+        self.local, self.one, self.two_a, self.two_b, self.three = buffers
+        self.z, self.x, self.y, self.c = place()
+        (self.core, self.across, self.along), _ = neighbours()
+        self.half = self.three.shape[-1] // 2
+        self.load = pltpu.make_async_copy(unit.at[self.c], self.local, loaded)
+
+    def copy(self, slot):
+        x, y, half = self.x, self.y, self.half
+        left, right = pl.ds(0, half), pl.ds(half, half)
+        if slot == 0:
+            return send(self.unit.at[1 - self.c], self.one, self.sems, 0, self.core)
+        if slot == 1:
+            return send(self.one.at[:, 1 - x, :, :, left], self.two_a, self.sems, 1, self.across)
+        if slot == 2:
+            return send(self.one.at[1 - y, :, :, :, right], self.two_b, self.sems, 2, self.along)
+        if slot == 3:
+            return send(
+                self.two_a.at[1 - y], self.three.at[:, :, left], self.sems, 3, self.along
+            )
+        return send(self.two_b.at[1 - x], self.three.at[:, :, right], self.sems, 4, self.across)
+
+    def start(self, *slots):
+        for slot in slots:
+            self.copy(slot).start()
+
+    def begin(self):
+        self.load.start()
+        self.start(0)
+
+    def add_one(self):
+        self.load.wait()
+        self.copy(0).wait_recv()
+        add_into(self.one, self.local, [(y, x, z) for y in range(2) for x in range(2) for z in range(4)])
+
+    def add_two(self):
+        x, y, half = self.x, self.y, self.half
+        self.copy(1).wait_recv()
+        self.copy(2).wait_recv()
+        for index in range(2):
+            for z in range(4):
+                total = self.two_a[index, z].astype(F32)
+                total = total + self.one[index, x, z, :, 0:half].astype(F32)
+                self.two_a[index, z] = total.astype(BF16)
+                total = self.two_b[index, z].astype(F32)
+                total = total + self.one[y, index, z, :, half : 2 * half].astype(F32)
+                self.two_b[index, z] = total.astype(BF16)
+
+    def add_three(self):
+        x, y, half = self.x, self.y, self.half
+        self.copy(3).wait_recv()
+        self.copy(4).wait_recv()
+        for z in range(4):
+            total = self.three[z, :, 0:half].astype(F32) + self.two_a[y, z].astype(F32)
+            self.three[z, :, 0:half] = total.astype(BF16)
+            total = self.three[z, :, half : 2 * half].astype(F32) + self.two_b[x, z].astype(F32)
+            self.three[z, :, half : 2 * half] = total.astype(BF16)
+
+    def finish(self):
+        for slot in range(5):
+            self.copy(slot).wait_send()
+
+
+def plane_buffers():
+    _, _, _, zs, piece, width = UNIT
+    return [
+        pltpu.VMEM((2, 2, zs, piece, width), BF16),
+        pltpu.VMEM((2, 2, zs, piece, width), BF16),
+        pltpu.VMEM((2, zs, piece, width // 2), BF16),
+        pltpu.VMEM((2, zs, piece, width // 2), BF16),
+        pltpu.VMEM((zs, piece, width), BF16),
+        pltpu.SemaphoreType.DMA,
+        pltpu.SemaphoreType.DMA((5,)),
+        pltpu.SemaphoreType.DMA((5,)),
+    ]
+
+
+def make_plane(unit, scratch):
+    return Plane(unit, scratch[:5], scratch[5], scratch[6:8])
+
+
+def back_kernel(
+    linked,
+    query,
+    keys,
+    values,
+    marks,
+    probs,
+    mixed_grad,
+    row_sums,
+    normed_hbm,
+    query_hbm,
+    key_hbm,
+    value_hbm,
+    output_hbm,
+    down_unit,
+    up_unit,
+    normed_unit,
+    heads_unit,
+    down_out,
+    up_out,
+    left,
+    right,
+    query_back,
+    key_back,
+    value_back,
+    normed,
+    query_weight,
+    key_weight,
+    value_weight,
+    grads,
+    staged,
+    loads,
+    stores,
+    *scratch,
+):
+    pair = pl.program_id(0)
+    pairs = pl.num_programs(0) - 1
+    width, rows = query_back.shape
     group = keys.shape[0]
     blocks = group // KEY_BLOCK
-    pair_columns(left, query, rows)
-    pair_columns(right, mixed_grad, rows)
-    kinds = lax.broadcasted_iota(jnp.int32, (128, rows), 0)
-    for half in range(2):
-        total = -row_sums[0, half : half + 1]
-        high = total.astype(BF16)
-        rest = (total - high.astype(F32)).astype(BF16)
+    owners = group // rows
+    down = make_plane(down_unit, scratch[:8]) if linked else None
+    up = make_plane(up_unit, scratch[8:16]) if linked else None
+    sources = [normed_hbm, query_hbm, key_hbm, value_hbm]
+    targets = [normed, query_weight, key_weight, value_weight]
+    copies = [
+        pltpu.make_async_copy(source, target, loads.at[index])
+        for index, (source, target) in enumerate(zip(sources, targets))
+    ]
+    output_copy = pltpu.make_async_copy(output_hbm, heads_unit.at[0, 0], loads.at[4])
+
+    @pl.when(pair == 0)
+    def _():
+        for copy in copies:
+            copy.start()
+        output_copy.start()
+        if linked:
+            greet(neighbours()[0])
+            down.begin()
+            up.begin()
+
+    def hook(spot):
+        if not linked:
+            return
+
+        def at(when, action):
+            if when % blocks == spot:
+                pl.when(pair == when // blocks)(action)
+
+        def down_one():
+            down.add_one()
+            down.start(1, 2)
+
+        def up_one():
+            up.add_one()
+            up.start(1, 2)
+
+        def down_two():
+            down.add_two()
+            down.start(3, 4)
+
+        def up_two():
+            up.add_two()
+            up.start(3, 4)
+
+        def down_three():
+            down.add_three()
+            pltpu.make_async_copy(down.three, down_out, stores.at[11]).start()
+
+        at(5, down_one)
+        at(16, up_one)
+        at(19, down_two)
+        at(29, down_three)
+        at(35, up_two)
+
+    @pl.when(pair < pairs)
+    def _():
+        pair_columns(left, query, rows)
+        pair_columns(right, mixed_grad, rows)
+        kinds = lax.broadcasted_iota(jnp.int32, (128, rows), 0)
         shape = (128, rows)
-        fill = jnp.where(kinds == ONES, jnp.broadcast_to(high.astype(F32), shape), 0.0)
-        fill = jnp.where(kinds == ONES + 1, jnp.broadcast_to(rest.astype(F32), shape), fill)
-        right[128:256, half * rows : (half + 1) * rows] = fill.astype(BF16)
-
-    def step(index, total):
-        part = pl.ds(pl.multiple_of(index * KEY_BLOCK, KEY_BLOCK), KEY_BLOCK)
-        weights = probs[part, :]
-        inner = dot(jnp.concatenate([values[part, :], marks[part, :]], axis=1), right[...])
-        score_grad = (weights.astype(F32) * inner).astype(BF16)
-        key_out[part, :] = (dot(score_grad, left[...], 1, 1) * LN2).astype(BF16)
-        value_out[part, :] = dot(weights, right[0:128, :], 1, 1).astype(BF16)
-        return total + dot(keys[part, :].T, score_grad)
-
-    total = lax.fori_loop(0, blocks, step, jnp.zeros((128, 2 * rows), F32))
-    scale = HEAD_DIM**-0.5
-    query_out[0:HEAD_DIM] = (total[0:HEAD_DIM, 0:rows] * scale).astype(BF16)
-    query_out[HEAD_DIM:128] = (total[HEAD_DIM:128, rows : 2 * rows] * scale).astype(BF16)
-
-
-def attend_back(query, keys, values, marks, probs, mixed_grad, row_sums):
+        for half in range(2):
+            total = -row_sums[0, half : half + 1]
+            high = total.astype(BF16).astype(F32)
+            fill = jnp.where(kinds == ONES, jnp.broadcast_to(high, shape), 0.0)
+            fill = jnp.where(kinds == ONES + 1, jnp.broadcast_to(total - high, shape), fill)
+            right[128:256, half * rows : (half + 1) * rows] = fill.astype(BF16)
+
+        column = pl.ds(pl.multiple_of(pair * 128, 128), 128)
+        total = jnp.zeros((128, 2 * rows), F32)
+        for index in range(blocks):
+            part = slice(index * KEY_BLOCK, (index + 1) * KEY_BLOCK)
+            weights = probs[part, :]
+            inner = dot(jnp.concatenate([values[part, :], marks[part, :]], axis=1), right[...])
+            score_grad = (weights.astype(F32) * inner).astype(BF16)
+            key_back[part, column] = (dot(score_grad, left[...], 1, 1) * LN2).astype(BF16)
+            value_back[part, column] = dot(weights, right[0:128, :], 1, 1).astype(BF16)
+            total = total + dot(keys[part, :].T, score_grad)
+            hook(index)
+        scale = HEAD_DIM**-0.5
+        base = pl.multiple_of(pair * 128, 128)
+        query_back[pl.ds(base, HEAD_DIM), :] = (total[0:HEAD_DIM, 0:rows] * scale).astype(BF16)
+        base = pl.multiple_of(pair * 128 + HEAD_DIM, HEAD_DIM)
+        query_back[pl.ds(base, HEAD_DIM), :] = (total[HEAD_DIM:128, rows : 2 * rows] * scale).astype(BF16)
+
+    @pl.when(pair == pairs)
+    def _():
+        for copy in copies:
+            copy.wait()
+        output_copy.wait()
+        own = lax.axis_index("head") * lax.axis_size("seq") + lax.axis_index("seq")
+        mine = pl.ds(pl.multiple_of(own * rows, 128), rows)
+        heads_stores = []
+
+        def keep(kind, value):
+            grads[kind - 1] = value.astype(BF16).reshape(4, 2, PIECE, width)
+
+        keep(1, dot(normed[:, mine], query_back[...], 1, 1))
+        keep(2, dot(normed[...], key_back[...]))
+        keep(3, dot(normed[...], value_back[...]))
+        for kind in (1, 2, 3):
+            for half in range(2):
+                copy = pltpu.make_async_copy(
+                    grads.at[kind - 1, :, half],
+                    heads_unit.at[kind // 2, kind % 2, half],
+                    stores.at[(kind - 1) * 2 + half],
+                )
+                copy.start()
+                heads_stores.append(copy)
+
+        def owner_store(owner):
+            x, y, c = lax.div(owner, 4), lax.rem(lax.div(owner, 2), 2), lax.rem(owner, 2)
+            slot = lax.rem(owner, 2)
+            return pltpu.make_async_copy(staged.at[slot], normed_unit.at[c, y, x], stores.at[6 + slot])
+
+        def owner_step(owner, carry):
+            part = pl.ds(pl.multiple_of(owner * rows, 128), rows)
+            total = dot(key_back[part, :], key_weight[...], 1, 1)
+            total = total + dot(value_back[part, :], value_weight[...], 1, 1)
+
+            @pl.when(owner >= 2)
+            def _():
+                owner_store(owner - 2).wait()
+
+            staged[lax.rem(owner, 2)] = total.astype(BF16).reshape(4, PIECE, width)
+
+            @pl.when(owner == own)
+            def _():
+                extra = dot(query_back[...], query_weight[...], 0, 1)
+                staged[lax.rem(owner, 2)] = (total + extra).astype(BF16).reshape(4, PIECE, width)
+
+            owner_store(owner).start()
+            return carry
+
+        lax.fori_loop(0, owners, owner_step, 0)
+        for owner in (owners - 2, owners - 1):
+            owner_store(owner).wait()
+        for copy in heads_stores:
+            copy.wait()
+        if linked:
+            up.add_three()
+            store = pltpu.make_async_copy(up.three, up_out, stores.at[10])
+            store.start()
+            store.wait()
+            pltpu.make_async_copy(down.three, down_out, stores.at[11]).wait()
+            down.finish()
+            up.finish()
+
+
+def attend_back(
+    linked, query, keys, values, marks, probs, mixed_grad, row_sums, normed, wq, wk, wv, output_part, down_unit, up_unit
+):
     width, rows = query.shape
     group = keys.shape[0]
     pairs = width // 128
-    column = pl.BlockSpec((group, 128), lambda pair: (0, pair))
-    row = pl.BlockSpec((128, rows), lambda pair: (pair, 0))
+    held = lambda pair: jnp.minimum(pair, pairs - 1)
+    column = pl.BlockSpec((group, 128), lambda pair: (0, held(pair)))
+    row = pl.BlockSpec((128, rows), lambda pair: (held(pair), 0))
+    hbm = pl.BlockSpec(memory_space=pltpu.HBM)
+    third = jax.ShapeDtypeStruct(UNIT[3:], BF16)
+    more = dict(collective_id=1, has_side_effects=True) if linked else {}
     return pl.pallas_call(
-        back_kernel,
-        grid=(pairs,),
+        functools.partial(back_kernel, linked),
+        grid=(pairs + 1,),
         in_specs=[
             row,
             column,
             column,
-            whole((group, 128)),
-            pl.BlockSpec((group, 2 * rows), lambda pair: (0, pair)),
+            pl.BlockSpec((group, 128), lambda pair: (0, 0), pipeline_mode=pl.Buffered(1)),
+            pl.BlockSpec((group, 2 * rows), lambda pair: (0, held(pair))),
             row,
-            pl.BlockSpec((1, 2, rows), lambda pair: (pair, 0, 0)),
+            pl.BlockSpec((1, 2, rows), lambda pair: (held(pair), 0, 0)),
+        ]
+        + [hbm] * 7,
+        out_specs=[hbm] * 4,
+        out_shape=[
+            jax.ShapeDtypeStruct(UNIT, BF16),
+            jax.ShapeDtypeStruct(UNIT, BF16),
+            third,
+            third,
         ],
-        out_specs=[row, column, column],
+        scratch_shapes=[
+            pltpu.VMEM((128, 2 * rows), BF16),
+            pltpu.VMEM((256, 2 * rows), BF16),
+            pltpu.VMEM((width, rows), BF16),
+            pltpu.VMEM((group, width), BF16),
+            pltpu.VMEM((group, width), BF16),
+            pltpu.VMEM((width, group), BF16),
+            pltpu.VMEM((width, width), BF16),
+            pltpu.VMEM((width, width), BF16),
+            pltpu.VMEM((width, width), BF16),
+            pltpu.VMEM((3, 4, 2, PIECE, width), BF16),
+            pltpu.VMEM((2, 4, PIECE, width), BF16),
+            pltpu.SemaphoreType.DMA((5,)),
+            pltpu.SemaphoreType.DMA((12,)),
+        ]
+        + (plane_buffers() * 2 if linked else []),
+        compiler_params=params(**more),
+        name="attend_back",
+    )(query, keys, values, marks, probs, mixed_grad, row_sums, normed, wq, wk, wv, output_part, down_unit, up_unit)
+
+
+class Line:
+    def __init__(self, three, four, out, sems):
+        self.three, self.four, self.out, self.sems = three, four, out, sems
+        self.z, self.x, self.y, self.c = place()
+        (self.core, self.across, self.along), self.planes = neighbours()
+        self.half = three.shape[-1] // 2
+
+    def copy(self, slot):
+        x, y, c = self.x, self.y, self.c
+        left, right = pl.ds(0, self.half), pl.ds(self.half, self.half)
+        if slot < 3:
+            target = lax.rem(self.z + slot + 1, 4)
+            return send(self.three.at[target], self.four.at[slot], self.sems, slot, self.planes[slot])
+        mine = self.out.at[c, y, x]
+        if slot == 3:
+            return send(mine, mine, self.sems, 3, self.across)
+        if slot == 4:
+            return send(mine, mine, self.sems, 4, self.along)
+        if slot == 5:
+            other = self.out.at[c, y, 1 - x, :, left]
+            return send(other, other, self.sems, 5, self.along)
+        if slot == 6:
+            other = self.out.at[c, 1 - y, x, :, right]
+            return send(other, other, self.sems, 6, self.across)
+        return send(self.out.at[c], self.out.at[c], self.sems, 7, self.core)
+
+    def begin(self):
+        for slot in range(3):
+            self.copy(slot).start()
+
+    def add(self):
+        total = self.three[self.z].astype(F32)
+        for slot in range(3):
+            self.copy(slot).wait_recv()
+            total = total + self.four[slot].astype(F32)
+        self.out[self.c, self.y, self.x] = total.astype(BF16)
+        self.copy(3).start()
+        self.copy(4).start()
+
+    def forward(self):
+        self.copy(3).wait_recv()
+        self.copy(4).wait_recv()
+        self.copy(5).start()
+        self.copy(6).start()
+
+    def share(self):
+        self.copy(5).wait_recv()
+        self.copy(6).wait_recv()
+        self.copy(7).start()
+
+    def finish(self):
+        self.copy(7).wait_recv()
+        for slot in range(8):
+            self.copy(slot).wait_send()
+
+
+class Rows:
+    def __init__(self, given, part, landed, out, sems):
+        self.given, self.part, self.landed, self.out, self.sems = given, part, landed, out, sems
+        self.z, self.x, self.y, self.c = place()
+        (self.core, self.across, self.along), self.planes = neighbours()
+
+    def index(self, x, y, c):
+        return x * 4 + y * 2 + c
+
+    def copy(self, slot):
+        x, y, c = self.x, self.y, self.c
+        size = self.given.shape[1] // 2
+        mine = self.given.at[self.index(x, y, c)]
+        if slot < 3:
+            return send(mine, mine, self.sems, slot, (self.core, self.across, self.along)[slot])
+        if slot == 3:
+            other = self.given.at[self.index(1 - x, y, c), pl.ds(0, size)]
+            return send(other, other, self.sems, 3, self.along)
+        if slot == 4:
+            other = self.given.at[self.index(x, 1 - y, c), pl.ds(size, size)]
+            return send(other, other, self.sems, 4, self.across)
+        if slot < 8:
+            flip_x, flip_y = ((1, 0), (0, 1), (1, 1))[slot - 5]
+            other = self.given.at[
+                self.index(x + flip_x - 2 * flip_x * x, y + flip_y - 2 * flip_y * y, c)
+            ]
+            return send(other, other, self.sems, slot, self.core)
+        if slot < 11:
+            step = slot - 8
+            target = lax.rem(self.z + step + 1, 4)
+            return send(
+                self.part.at[target], self.landed.at[step], self.sems, slot, self.planes[step]
+            )
+        if slot < 14:
+            mine = self.out.at[x, self.z]
+            return send(mine, mine, self.sems, slot, self.planes[slot - 11])
+        return send(self.out.at[x], self.out.at[x], self.sems, 14, self.across)
+
+    def start(self, *slots):
+        for slot in slots:
+            self.copy(slot).start()
+
+    def landed_all(self, *slots):
+        for slot in slots:
+            self.copy(slot).wait_recv()
+
+    def finish(self):
+        for slot in range(15):
+            self.copy(slot).wait_send()
+
+
+class Small:
+    def __init__(self, rows, entry, half_rows, half_entry, landings, out, entry_out, sems):
+        self.rows, self.entry, self.half_rows, self.half_entry = rows, entry, half_rows, half_entry
+        self.landings, self.out, self.entry_out, self.sems = landings, out, entry_out, sems
+        self.z, self.x, self.y, self.c = place()
+        (self.core, self.across, self.along), self.planes = neighbours()
+        half = rows.shape[-1] // 2
+        self.mine = pl.ds(pl.multiple_of(self.c * half, 128), half)
+        self.away = pl.ds(pl.multiple_of((1 - self.c) * half, 128), half)
+
+    def copy(self, slot):
+        rows_land, entry_land, last = self.landings
+        stage, kind = slot // 2, slot % 2
+        if stage == 0:
+            source = (self.rows.at[:, self.away], self.entry.at[:, :, self.away])[kind]
+        else:
+            source = (self.half_rows, self.half_entry)[kind]
+        if stage < 3:
+            target = (rows_land, entry_land)[kind].at[stage]
+            return send(source, target, self.sems, slot, (self.core, self.across, self.along)[stage])
+        if stage < 6:
+            step = stage - 3
+            if kind == 0:
+                target = self.out.at[self.z, :, self.mine]
+            else:
+                source = self.half_entry.at[lax.rem(self.z + step + 1, 4)]
+                target = last.at[step]
+            return send(source, target, self.sems, slot, self.planes[step])
+        part = (self.out.at[:, :, self.mine], self.entry_out.at[:, self.mine])[kind]
+        return send(part, part, self.sems, slot, self.core)
+
+    def start(self, stage):
+        self.copy(2 * stage).start()
+        self.copy(2 * stage + 1).start()
+
+    def landed(self, stage):
+        self.copy(2 * stage).wait_recv()
+        self.copy(2 * stage + 1).wait_recv()
+
+    def add(self, stage):
+        rows_land, entry_land, _ = self.landings
+        self.landed(stage)
+        if stage == 0:
+            self.half_rows[...] = self.rows[:, self.mine] + rows_land[0]
+            total = self.entry[:, :, self.mine].astype(F32) + entry_land[0].astype(F32)
+        else:
+            self.half_rows[...] = self.half_rows[...] + rows_land[stage]
+            total = self.half_entry[...].astype(F32) + entry_land[stage].astype(F32)
+        self.half_entry[...] = total.astype(BF16)
+
+    def sent(self, stage):
+        self.copy(2 * stage).wait_send()
+        self.copy(2 * stage + 1).wait_send()
+
+    def collect(self):
+        last = self.landings[2]
+        self.out[self.z, :, self.mine] = self.half_rows[...]
+        total = self.half_entry[self.z].astype(F32)
+        for step in range(3):
+            self.landed(3 + step)
+            total = total + last[step].astype(F32)
+        self.entry_out[:, self.mine] = total.astype(BF16)
+        self.start(6)
+
+
+def late_kernel(
+    slots,
+    tokens,
+    stream,
+    middle_grad,
+    gain,
+    embed_low,
+    found,
+    input_weight,
+    second_norm,
+    mean_norm,
+    down_three,
+    up_three,
+    normed_unit,
+    heads_unit,
+    embed_grad_out,
+    table_out,
+    small_out,
+    entry_out,
+    down_out,
+    up_out,
+    heads_out,
+    given,
+    part,
+    part_landed,
+    rows_own,
+    entry_own,
+    half_rows,
+    half_entry,
+    rows_land,
+    entry_land,
+    entry_last,
+    down_four,
+    up_four,
+    heads_four,
+    *scratch,
+):
+    z, x, y, c = place()
+    own = x * 4 + y * 2 + c
+    width = stream.shape[1]
+    rows = stream.shape[0]
+    near, planes = neighbours()
+    normed_plane = make_plane(normed_unit, scratch[0:8])
+    heads_plane = make_plane(heads_unit, scratch[8:16])
+    sems = scratch[16:]
+    down = Line(down_three, down_four, down_out, sems[0:2])
+    up = Line(up_three, up_four, up_out, sems[2:4])
+    heads = Line(heads_plane.three, heads_four, heads_out, sems[4:6])
+    table = Rows(given, part, part_landed, table_out, sems[6:8])
+    small = Small(
+        rows_own,
+        entry_own,
+        half_rows,
+        half_entry,
+        (rows_land, entry_land, entry_last),
+        small_out,
+        entry_out,
+        sems[8:10],
+    )
+    greet(near + planes)
+    normed_plane.begin()
+    heads_plane.begin()
+    down.begin()
+    up.begin()
+    normed_plane.add_one()
+    normed_plane.start(1, 2)
+    heads_plane.add_one()
+    unit, scale = norm_parts(stream[...])
+    normed_plane.add_two()
+    normed_plane.start(3, 4)
+    normed_plane.add_three()
+    heads_plane.start(1, 2)
+
+    incoming = normed_plane.three[...].reshape(rows, width).astype(F32)
+    stream_grad = middle_grad[...] + norm_back(incoming, gain[...].reshape(1, width), unit, scale)
+    stream_low = stream_grad.astype(BF16)
+    embed_grad = dot(stream_low, input_weight[...], 1, 1)
+    given[own] = embed_grad.astype(BF16)
+    table.start(0, 1, 2)
+    embed_grad_out[...] = embed_grad
+    entry_own[...] = dot(embed_low[...], stream_low, 0, 0).astype(BF16).reshape(4, 32, width)
+    kinds = lax.broadcasted_iota(jnp.int32, (SLOTS, rows), 0)
+    picker = jnp.where(kinds == slots[...], 1.0, 0.0).astype(BF16)
+    rest = (stream_grad - stream_low.astype(F32)).astype(BF16)
+    rows_own[0:SLOTS] = dot(picker, stream_low) + dot(picker, rest)
+    rows_own[SLOTS : SLOTS + 1] = jnp.sum(incoming * unit, axis=0, keepdims=True)
+    rows_own[SLOTS + 1 : SLOTS + 2] = jnp.sum(incoming, axis=0, keepdims=True)
+    rows_own[SLOTS + 2 : SLOTS + 4] = second_norm[...]
+    inner = jnp.sum(embed_grad * found[...].astype(F32), axis=0, keepdims=True)
+    inner = jnp.sum(inner, axis=1, keepdims=True)
+    rows_own[SLOTS + 4 : SLOTS + 5] = jnp.broadcast_to(inner, (1, width))
+    rows_own[SLOTS + 5 : SLOTS + 8] = jnp.zeros((3, width), F32)
+    small.start(0)
+    down.add()
+    up.add()
+    table.landed_all(0, 1, 2)
+    table.start(3, 4)
+    small.add(0)
+    small.start(1)
+    table.landed_all(3, 4)
+    table.start(5, 6, 7)
+    down.forward()
+    up.forward()
+    small.sent(1)
+    small.add(1)
+    small.start(2)
+    table.landed_all(5, 6, 7)
+    seq = y * 2 + c
+    all_given = given[...].reshape(8 * rows, 128)
+    size = part.shape[1]
+    for quarter in range(4):
+        base = seq * (8 * size) + x * (4 * size) + quarter * size
+        ids = lax.broadcasted_iota(jnp.int32, (size, rows), 0) + base
+        hits = jnp.concatenate(
+            [jnp.where(ids == tokens[owner], 1.0, 0.0).astype(BF16) for owner in range(8)], axis=1
+        )
+        part[quarter] = dot(hits, all_given).astype(BF16)
+    table.start(8, 9, 10)
+    small.sent(2)
+    small.add(2)
+    for stage in (3, 4, 5):
+        small.start(stage)
+    heads_plane.add_two()
+    heads_plane.start(3, 4)
+    down.share()
+    up.share()
+    total = part[z].astype(F32)
+    for slot in (8, 9, 10):
+        table.landed_all(slot)
+        total = total + part_landed[slot - 8].astype(F32)
+    table_out[x, z] = total.astype(BF16)
+    table.start(11, 12, 13)
+    small.collect()
+    heads_plane.add_three()
+    heads.begin()
+    table.landed_all(11, 12, 13)
+    table.start(14)
+    heads.add()
+    heads.forward()
+    heads.share()
+    table.landed_all(14)
+    small.landed(6)
+    small.sent(0)
+    for stage in (3, 4, 5, 6):
+        small.sent(stage)
+    table.finish()
+    normed_plane.finish()
+    heads_plane.finish()
+    down.finish()
+    up.finish()
+    heads.finish()
+
+
+def late(slots, tokens, stream, middle_grad, gain, embed_low, found, input_weight, second_norm, mean_norm, down_three, up_three, normed_unit, heads_unit):
+    rows, width = stream.shape
+    quarter = VOCAB // 4 // 8
+    vmem = pl.BlockSpec(memory_space=pltpu.VMEM)
+    hbm = pl.BlockSpec(memory_space=pltpu.HBM)
+    done = jax.ShapeDtypeStruct((2, 2, 2, PIECE, width), BF16)
+    pair = lambda count: [pltpu.SemaphoreType.DMA((count,)), pltpu.SemaphoreType.DMA((count,))]
+    return pl.pallas_call(
+        late_kernel,
+        in_specs=[vmem] * 12 + [hbm] * 2,
+        out_specs=[vmem] * 7,
         out_shape=[
-            jax.ShapeDtypeStruct((width, rows), BF16),
-            jax.ShapeDtypeStruct((group, width), BF16),
-            jax.ShapeDtypeStruct((group, width), BF16),
+            jax.ShapeDtypeStruct((rows, 128), F32),
+            jax.ShapeDtypeStruct((2, 4, quarter, 128), BF16),
+            jax.ShapeDtypeStruct((4, 40, width), F32),
+            jax.ShapeDtypeStruct((32, width), BF16),
+            done,
+            done,
+            done,
         ],
-        scratch_shapes=[pltpu.VMEM((128, 2 * rows), BF16), pltpu.VMEM((256, 2 * rows), BF16)],
+        scratch_shapes=[
+            pltpu.VMEM((8, rows, 128), BF16),
+            pltpu.VMEM((4, quarter, 128), BF16),
+            pltpu.VMEM((3, quarter, 128), BF16),
+            pltpu.VMEM((40, width), F32),
+            pltpu.VMEM((4, 32, width), BF16),
+            pltpu.VMEM((40, width // 2), F32),
+            pltpu.VMEM((4, 32, width // 2), BF16),
+            pltpu.VMEM((3, 40, width // 2), F32),
+            pltpu.VMEM((3, 4, 32, width // 2), BF16),
+            pltpu.VMEM((3, 32, width // 2), BF16),
+            pltpu.VMEM((3, PIECE, width), BF16),
+            pltpu.VMEM((3, PIECE, width), BF16),
+            pltpu.VMEM((3, PIECE, width), BF16),
+        ]
+        + plane_buffers() * 2
+        + pair(8) * 3
+        + pair(15)
+        + pair(14),
+        compiler_params=params(collective_id=2, has_side_effects=True),
+        name="late",
+    )(slots, tokens, stream, middle_grad, gain, embed_low, found, input_weight, second_norm, mean_norm, down_three, up_three, normed_unit, heads_unit)
+
+
+def finish_kernel(
+    embed_grad,
+    table_sum,
+    small,
+    entry,
+    down,
+    up,
+    heads,
+    table,
+    mean_norm,
+    hidden,
+    acts,
+    features,
+    second_weight,
+    embed_out,
+    table_out,
+    entry_out,
+    first_out,
+    second_out,
+    gain_one,
+    shift_one,
+    query_out,
+    key_out,
+    value_out,
+    output_out,
+    gain_two,
+    shift_two,
+    up_out,
+    down_out,
+):
+    width = second_weight.shape[0]
+    embed_out[...] = embed_grad[...]
+    entry_out[...] = entry[...].astype(F32)
+    for piece in range(8):
+        c, y, x = piece // 4, (piece // 2) % 2, piece % 2
+        down_out[piece * PIECE : (piece + 1) * PIECE, :] = down[c, y, x].astype(F32)
+        quarter = piece // 2
+        up_out[x * PIECE : (x + 1) * PIECE, quarter * width : (quarter + 1) * width] = up[c, y, x].astype(F32)
+        target = (output_out, query_out, key_out, value_out)[quarter]
+        target[x * PIECE : (x + 1) * PIECE, :] = heads[c, y, x].astype(F32)
+    totals = small[0, SLOTS : SLOTS + 8]
+    for plane in range(1, small.shape[0]):
+        totals = totals + small[plane, SLOTS : SLOTS + 8]
+    gain_one[...] = totals[0:1].reshape(width)
+    shift_one[...] = totals[1:2].reshape(width)
+    gain_two[...] = totals[2:3].reshape(width)
+    shift_two[...] = totals[3:4].reshape(width)
+    mean = mean_norm[0:1]
+    inverse = 1.0 / mean
+    mean_grad = -totals[4:5, 0:128] * inverse * inverse * (1.0 / VOCAB)
+    wide = table[...].astype(F32)
+    norms = jnp.sqrt(jnp.sum(wide * wide, axis=1, keepdims=True))
+    sums = table_sum[...].reshape(table.shape).astype(F32)
+    table_out[...] = sums * inverse + mean_grad * (wide / norms)
+    tog = jnp.concatenate([small[plane, 0:SLOTS] for plane in range(small.shape[0])], axis=0)
+    second_out[...] = lax.dot_general(
+        acts[...], tog, (((0,), (0,)), ((), ())), precision=lax.Precision.HIGHEST, preferred_element_type=F32
+    )
+    high = tog.astype(BF16)
+    rest = (tog - high.astype(F32)).astype(BF16)
+    act_grad = dot(high, second_weight[...], 1, 1) + dot(rest, second_weight[...], 1, 1)
+    value = hidden[...]
+    gate = 1.0 / (1.0 + jnp.exp(-value))
+    hidden_grad = act_grad * (gate * (1.0 + value * (1.0 - gate)))
+    first_out[...] = lax.dot_general(
+        features[...], hidden_grad, (((0,), (0,)), ((), ())), precision=lax.Precision.HIGHEST, preferred_element_type=F32
+    )
+
+
+def finish(embed_grad, table_sum, small, entry, down, up, heads, table, mean_norm, hidden, acts, features, second_weight):
+    rows = embed_grad.shape[0]
+    width = second_weight.shape[0]
+    wide = lambda *shape: jax.ShapeDtypeStruct(shape, F32)
+    shard = width // 4
+    return pl.pallas_call(
+        finish_kernel,
+        out_shape=[
+            wide(rows, 128),
+            wide(*table.shape),
+            wide(32, width),
+            wide(features.shape[1], width),
+            wide(acts.shape[1], width),
+            wide(width),
+            wide(width),
+            wide(shard, width),
+            wide(shard, width),
+            wide(shard, width),
+            wide(shard, width),
+            wide(width),
+            wide(width),
+            wide(shard, 4 * width),
+            wide(width, width),
+        ],
         compiler_params=params(),
-        name="attend_back",
-    )(query, keys, values, marks, probs, mixed_grad, row_sums)
+        name="finish",
+    )(embed_grad, table_sum, small, entry, down, up, heads, table, mean_norm, hidden, acts, features, second_weight)
 
 
 def time_features(steps, width):
@@ -465,71 +1353,133 @@
     down_weight,
     upstream,
 ):
-    head_count = lax.axis_size("head")
-    seq_count = lax.axis_size("seq")
-    blocks = head_count * seq_count
+    blocks = lax.axis_size("head") * lax.axis_size("seq")
+    planes = lax.axis_size("dp")
     rows = tokens.shape[0]
     width = query_weight.shape[0]
     shard_rows = table.shape[0]
     slot_count = live_lengths.shape[1]
     highest = lax.Precision.HIGHEST
+    plane = lax.axis_index("dp")
     seq_index = lax.axis_index("seq")
-    own = lax.axis_index("head") * seq_count + seq_index
-
-    all_tokens, all_slots = (
-        lax.all_gather(tokens, ("head", "seq"), axis=0, tiled=True),
-        lax.all_gather(segments, ("head", "seq"), axis=0, tiled=True),
+    own = lax.axis_index("head") * lax.axis_size("seq") + seq_index
+    linked = planes == 4
+
+    notes = jnp.concatenate(
+        [
+            tokens.reshape(3, 128),
+            segments.reshape(3, 128),
+            jnp.pad(timesteps, ((0, 1), (0, 128 - slot_count))),
+        ],
+        axis=0,
     )
-    full_table = lax.all_gather(table, "seq", axis=0, tiled=True).astype(F32)
-    mean_norm = jnp.sum(jnp.sqrt(jnp.sum(full_table * full_table, axis=1))) / VOCAB
-    features = time_features(timesteps[0], time_first.shape[0])
+    full_table, notes_all, steps_all, mean_norm = gather(table, notes)
+    steps = jnp.where(jnp.arange(SLOTS)[None, :] < slot_count, steps_all[:, 6, :SLOTS], 0).reshape(-1)
+    present = jnp.tile(jnp.arange(SLOTS) < slot_count, planes)
+    features = jnp.where(present[:, None], time_features(steps, time_first.shape[0]), 0.0)
     second_wide = time_second.astype(F32)
     time_hidden = jnp.dot(features, time_first.astype(F32), precision=highest)
     time_act = jax.nn.silu(time_hidden)
-    time_out = jnp.dot(time_act, second_wide, precision=highest)
-    time_rows = jnp.pad(time_out, ((0, SLOTS - slot_count), (0, 0)))
+    time_rows = jnp.dot(
+        lax.dynamic_slice_in_dim(time_act, plane * SLOTS, SLOTS), second_wide, precision=highest
+    )
     entry = jnp.concatenate(
         [input_weight, *split_three(time_rows), jnp.zeros((SLOTS, width), BF16)], axis=0
     )
     lengths = jnp.pad(live_lengths.astype(F32), ((0, 0), (0, 128 - slot_count)))
-    normed, keys, values, marks, stream, query, embed_low = embed(
+    normed, keys, values, marks, stream, query, embed_low, found = embed(
         own[None],
-        all_tokens,
-        all_slots[:, None],
+        notes_all,
         lengths,
-        mean_norm[None],
+        mean_norm,
         full_table,
         entry,
-        first_gain[None],
-        first_shift[None],
+        first_gain,
+        first_shift,
         query_weight,
         key_weight,
         value_weight,
+        rows,
         blocks,
     )
     probs, mixed, inverse = attend(query, keys, values, marks, segments[None])
-    activation, middle_grad, second_norm, mixed_grad, row_sums, output_grad, up_grad, down_grad = feed(
+    activation, middle_grad, second_norm, mixed_grad, row_sums, output_part, up_unit, down_unit = feed(
         mixed,
         inverse.reshape(HEADS, rows),
         stream,
         upstream,
-        second_gain[None],
-        second_shift[None],
+        second_gain,
+        second_shift,
         output_weight,
         up_weight,
         down_weight,
     )
-    query_back, key_back, value_back = attend_back(
-        query, keys, values, marks, probs, mixed_grad, row_sums.reshape(HEADS // 2, 2, rows)
+    normed_unit, heads_unit, down_three, up_three = attend_back(
+        linked,
+        query,
+        keys,
+        values,
+        marks,
+        probs,
+        mixed_grad,
+        row_sums.reshape(HEADS // 2, 2, rows),
+        normed,
+        query_weight,
+        key_weight,
+        value_weight,
+        output_part,
+        down_unit,
+        up_unit,
     )
-    own_normed = lax.dynamic_slice_in_dim(normed, own * rows, rows)
-    query_grad = dot(own_normed, query_back, 0, 1)
-    key_grad = dot(normed, key_back, 0, 0)
-    value_grad = dot(normed, value_back, 0, 0)
-    partial = dot(key_back, key_weight, 1, 1) + dot(value_back, value_weight, 1, 1)
+    if linked:
+        shard = width // planes
+        embed_grad, table_sum, small, entry_sum, down_sum, up_sum, heads_sum = late(
+            segments[None],
+            notes_all[:, 0:3].reshape(8, 1, rows),
+            stream,
+            middle_grad,
+            first_gain,
+            embed_low,
+            found,
+            input_weight,
+            second_norm,
+            mean_norm,
+            down_three,
+            up_three,
+            normed_unit,
+            heads_unit,
+        )
+        outs = finish(
+            embed_grad,
+            table_sum,
+            small,
+            entry_sum,
+            down_sum,
+            up_sum,
+            heads_sum,
+            table,
+            mean_norm,
+            time_hidden,
+            lax.dynamic_slice_in_dim(time_act, plane * shard, shard, axis=1),
+            lax.dynamic_slice_in_dim(features, plane * 32, 32, axis=1),
+            time_second,
+        )
+        return (activation, *outs)
+
+    heads_all = heads_unit.reshape(4, 2, 4, PIECE, width).transpose(0, 2, 1, 3, 4)
+    output_grad, query_grad, key_grad, value_grad = heads_all.reshape(4, width, width)
+    down_grad = down_unit.transpose(3, 0, 1, 2, 4, 5).reshape(-1, width)
+    up_grad = up_unit.transpose(3, 2, 4, 0, 1, 5).reshape(width, -1)
     normed_grad = lax.psum_scatter(
-        partial.astype(BF16), ("head", "seq"), scatter_dimension=0, tiled=True
-    ).astype(F32) + dot(query_back, query_weight, 0, 1)
+        normed_unit.transpose(2, 1, 0, 3, 4, 5).reshape(-1, width),
+        ("head", "seq"),
+        scatter_dimension=0,
+        tiled=True,
+    ).astype(F32)
+    mean_norm = mean_norm[0, 0]
+    features = lax.dynamic_slice_in_dim(features, plane * SLOTS, slot_count)
+    time_hidden = lax.dynamic_slice_in_dim(time_hidden, plane * SLOTS, slot_count)
+    time_act = lax.dynamic_slice_in_dim(time_act, plane * SLOTS, slot_count)
 
     def one_norm(values, gain, shift):
         unit, _ = norm_parts(values)
@@ -569,8 +1519,7 @@
             down_grad,
         )
     ]
-    found = jnp.take(full_table, tokens, axis=0)
-    mean_part = -jnp.sum(embed_grad * found) / (mean_norm * mean_norm)
+    mean_part = -jnp.sum(embed_grad * found.astype(F32)) / (mean_norm * mean_norm)
     scaled_grad = embed_grad / mean_norm
     table_sum = jax.ops.segment_sum(scaled_grad, tokens, num_segments=VOCAB)
     small = lax.psum(

time: 923 us -> 315 us (0.34)
  waiting for transfers between devices: 618 us -> 0 us
  Pallas kernels: 123 us -> 294 us
  blocking collectives: 59.4 us -> 0 us
  matrix products: 43.8 us -> 1.78 us
  other arithmetic: 30.2 us -> 2.46 us
  between operations: 17.6 us -> 1.24 us
  local copies, waits for them, and re-layouts: 23.6 us -> 10 us
    reduce_scatter x10 -> x0, waiting for transfers between devices: 381 us -> none  [the longest x9 331 us: reduce(): lax.psum_scatter(value.astype(BF16), 'dp', scatter_dimension=0, tiled=True)]
    psum x3 -> x0, waiting for transfers between devices: 235 us -> none  [the longest x1 145 us: body(): lax.psum((first_gain_grad, first_shift_grad, second_norm[0], second_norm[...]
    pallas_call x1 -> x4, Pallas kernels: 38.7 us -> 207 us  [the longest x1 105 us: late(): pl.pallas_call(late_kernel, in_specs=[vmem] * 12 + [hbm] * 2, out_specs=[...]
    dot_general x13 -> x1, matrix products: 43.6 us -> 0.67 us  [body(): jnp.dot(lax.dynamic_slice_in_dim(time_act, plane * SLOTS, SLOTS), second_...]
    psum x1 -> x0, blocking collectives: 39.4 us -> none  [body(): lax.psum((first_gain_grad, first_shift_grad, second_norm[0], second_norm[...]
    all_gather x2 -> x0, blocking collectives: 20 us -> none  [the longest x1 10.3 us: body(): lax.all_gather(segments, ('head', 'seq'), axis=0, tiled=True)]
    convert_element_type x10 -> x0, other arithmetic: 14.8 us -> none  [the longest x9 12.4 us: reduce(): return lax.psum(part, ('head', 'seq')).astype(F32)]
  transfers between devices with their start and end apart: 14 -> 0, of which waited for: 12 -> 0; matrix products, arithmetic and copies ran while one was open for 6% -> 0% of each run, Pallas kernels for 0% -> 0%
where the time goes in v2:
time: 315 us; the launch traced here: 310 us
  Pallas kernels  294 us (93%)
  local copies, waits for them, and re-layouts  10 us (3%)
    pallas_call x1, Pallas kernels, late(): pl.pallas_call(late_kernel, in_specs=[vmem] * 12 + [hbm] * 2, out_specs=[...  105 us
    pallas_call x1, Pallas kernels, attend_back(): pl.pallas_call(functools.partial(back_kernel, linked), grid=(pairs + 1,),...  71 us
    pallas_call x1, Pallas kernels, attend(): pl.pallas_call(forward_kernel, grid=(pairs,), in_specs=[pl.BlockSpec((128...  34.2 us
    pallas_call x1, Pallas kernels, embed(): pl.pallas_call(embed_kernel, grid_spec=pltpu.PrefetchScalarGridSpec(num_s...  29.7 us
    pallas_call x1, Pallas kernels, feed(): pl.pallas_call(feed_kernel, in_specs=[vmem] * 6 + [hbm] * 3, out_specs=[v...  23.6 us
    pallas_call x1, Pallas kernels, gather(): pl.pallas_call(gather_kernel, in_specs=[vmem, vmem], out_specs=[hbm, vmem...  22.5 us
    pallas_call x1, Pallas kernels, finish(): pl.pallas_call(finish_kernel, out_shape=[wide(rows, 128), wide(*table.sha...  8.48 us

profile of v2, /device:TPU:0, one launch (start us, length us, event | category | flops | bytes accessed | tf_op | source)
XLA Modules:
  0.0 309.9 jit_solution(3569650493199320305)
XLA Ops:
  0.6 0.0 copy-start
  0.7 0.7 convert_element_type.29
  1.4 0.5 pad.9.lengths
  1.9 0.1 broadcast_in_dim.40
  2.0 1.3 broadcast_in_dim.45.slots
  3.3 1.3 pad_add_fusion.notes
  4.6 0.9 constant_dynamic-update-slice_fusion
  5.5 22.5 %gather.1 = (bf16[4,2048,128]{2,1,0:T(8,128)(2,1)}, s32[8,8,128]{2,1,0:T(8,128)}, s32[4,8,128]{2,1,0:T(8,128)}, f32[8,128]{1,0:T(8,128)}) custom-call(bf16[2048,128]{1,0:T(8,128)(2,1)} %table.3, s32[8,128]{1,0:T(8,128)} %pad_add_fusion.notes), custom_call_target="tpu_custom_call" | custom-call | tf_op jit(solution)/shard_map/gather/pallas_call | solution.py:154
  28.0 0.0 copy-start.2
  28.1 0.8 slice_reduce_fusion
  28.9 0.1 squeeze.3
  29.0 0.8 slice.7
  29.7 0.6 reshape.77.tokens
  30.4 0.3 multiply_cosine_fusion
  30.7 0.1 maximum_select_fusion
  30.8 0.7 constant_dynamic-slice_fusion.features
  31.5 0.0 copy-done
  31.5 1.1 divide_multiply_fusion
  32.6 0.0 copy-done.2
  32.6 0.7 convert_dynamic-update-slice_fusion
  33.3 0.7 constant_dynamic-slice_fusion.1.acts
  34.1 0.0 copy-start.3
  34.1 0.7 copy-done.3
  34.8 29.7 %embed.1 = (bf16[768,3072]{1,0:T(8,128)(2,1)}, bf16[3072,768]{1,0:T(8,128)(2,1)}, bf16[3072,768]{1,0:T(8,128)(2,1)}, bf16[3072,128]{1,0:T(8,128)(2,1)}, f32[384,...) custom-call(s32[1]{0:T(128)} %bitcast.own, ...), custom_call_target="tpu_custom_call" | custom-call | tf_op jit(solution)/shard_map/embed/pallas_call | solution.py:272
  64.5 34.2 %attend.1 = (bf16[3072,4608]{1,0:T(8,128)(2,1)}, f32[768,384]{1,0:T(8,128)}, f32[6,2,384]{2,1,0:T(2,128)}) custom-call(bf16[768,384]{1,0:T(8,128)(2,1)} %get-tuple-element.69.query, bf16[3072,768]{1,0:T(8,128)(2,1)} %get-tuple-element.70.keys, bf16[3072,768]{1,0:T(8,128)(2,1)} %get-tuple-element.71.values, bf16[3072,128]{1,0:T(8,128)(2,1)} %get-tuple-element.72.marks, ...), custom_call_target="tpu_custom_call" | custom-call | tf_op jit(solution)/shard_map/attend/pallas_call | solution.py:370
  98.8 1.3 reshape.74.inverse
  100.1 23.6 %feed.1 = (bf16[384,768]{1,0:T(8,128)(2,1)}, f32[384,768]{1,0:T(8,128)}, f32[2,768]{1,0:T(2,128)}, bf16[768,384]{1,0:T(8,128)(2,1)}, f32[12,384]{1,0:T(8,128)}, ...) custom-call(f32[768,384]{1,0:T(8,128)} %get-tuple-element.73.mixed_w, ...), custom_call_target="tpu_custom_call" | custom-call | tf_op jit(solution)/shard_map/feed/pallas_call | solution.py:494
  123.7 1.4 reshape.76.row_sums
  125.1 71.0 %attend_back.1 = (bf16[2,2,2,4,96,768]{5,4,3,2,1,0:T(8,128)(2,1)}, bf16[2,2,2,4,96,768]{5,4,3,2,1,0:T(8,128)(2,1)}, bf16[4,96,768]{2,1,0:T(8,128)(2,1)}, bf16[4,96,768]{2,1,0:T(8,128)(2,1)}) custom-call(bf16[768,384]{1,0:T(8,128)(2,1)} %get-tuple-element.69.query, bf16[3072,768]{1,0:T(8,128)(2,1)} %get-tuple-element.70.keys, ...), custom_call_target="tpu_custom_call" | custom-call | tf_op jit(solution)/shard_map/attend_back/pallas_call | solution.py:813
  196.1 104.8 %late.1 = (f32[384,128]{1,0:T(8,128)}, bf16[2,4,256,128]{3,2,1,0:T(8,128)(2,1)}, f32[4,40,768]{2,1,0:T(8,128)}, bf16[32,768]{1,0:T(8,128)(2,1)}, bf16[2,2,2,96,7...) custom-call(s32[1,384]{1,0:T(1,128)} %broadcast_in_dim.45.slots, ...), custom_call_target="tpu_custom_call" | custom-call | tf_op jit(solution)/shard_map/late/pallas_call | solution.py:1186
  300.9 0.0 copy-start.1
  301.0 8.5 %finish.1 = (f32[384,128]{1,0:T(8,128)}, f32[2048,128]{1,0:T(8,128)}, f32[32,768]{1,0:T(8,128)}, f32[32,768]{1,0:T(8,128)}, f32[192,768]{1,0:T(8,128)}, /*index=...) custom-call(f32[384,128]{1,0:T(8,128)} %get-tuple-element.92.embed_g, ...), custom_call_target="tpu_custom_call" | custom-call | tf_op jit(solution)/shard_map/finish/pallas_call | solution.py:1297
  (8 shorter events, 0.1 us)
Async XLA Ops:
  0.6 30.9 %copy-start = (bf16[128,768]{1,0:T(8,128)(2,1)S(1)}, bf16[128,768]{1,0:T(8,128)(2,1)}, u32[]{:S(2)}) copy-start(bf16[128,768]{1,0:T(8,128)(2,1)} %param.25) | copy-start | bytes 589828
  28.0 4.6 %copy-start.2 = (bf16[768,768]{1,0:T(8,128)(2,1)S(1)}, bf16[768,768]{1,0:T(8,128)(2,1)}, u32[]{:S(2)}) copy-start(bf16[768,768]{1,0:T(8,128)(2,1)} %second_weight.1) | copy-start | bytes 3538948
  34.1 0.7 copy-start.3
  300.9 8.5 %copy-start.1 = (bf16[128,768]{1,0:T(8,128)(2,1)S(1)}, bf16[128,768]{1,0:T(8,128)(2,1)}, u32[]{:S(2)}) copy-start(bf16[128,768]{1,0:T(8,128)(2,1)} %param.25) | copy-start | bytes 589828

commit v3 on v2

v3 whole, which is shorter than its diff:
```python
import functools
import math

import jax
import jax.numpy as jnp
from jax import lax
from jax.experimental import pallas as pl
from jax.experimental.pallas import tpu as pltpu
from jax.sharding import PartitionSpec as P

HEADS = 12
HEAD_DIM = 64
VOCAB = 8192
EPSILON = 1e-05
MASKED = -1e30
LOG2E = math.log2(math.e)
LN2 = math.log(2.0)
KEY_BLOCK = 512
SLOTS = 32
DEAD = 25
ONES = 32
VMEM_LIMIT = 60 * 2**20
SAFE = 60.0
PIECE = 96
UNIT = (2, 2, 2, 4, PIECE, 768)
MESH = pl.DeviceIdType.MESH

(
    GREET,
    D_LOCAL,
    U_LOCAL,
    X_LOCAL,
    LOAD,
    LOADED,
    GRAD_Q,
    GRAD_K,
    GRAD_V,
    NORM,
    NORM_REST,
    D_CORE,
    D_ONE,
    D_LEFT,
    D_RIGHT,
    D_THREE,
    U_CORE,
    U_ONE,
    U_LEFT,
    U_RIGHT,
    U_THREE,
    X_CORE,
    X_ONE,
    X_LEFT,
    X_RIGHT,
    X_THREE,
    H_CORE,
    H_ONE,
    H_LEFT,
    H_RIGHT,
    H_THREE,
    D_SEND,
    D_SUM,
    D_PASS_X,
    D_PASS_Y,
    D_SHARE,
    D_END,
    U_SEND,
    U_SUM,
    U_PASS_X,
    U_PASS_Y,
    U_SHARE,
    U_END,
    H_SEND,
    H_SUM,
    H_PASS_X,
    H_PASS_Y,
    H_SHARE,
    H_END,
    T_FIRST,
    T_PASS_X,
    T_PASS_Y,
    T_CORE,
    T_ROWS,
    T_SUM,
    T_PASS,
    T_END,
    S_FIRST,
    S_CORE,
    S_X,
    S_Y,
    S_COLLECT,
    S_END,
) = range(0, 252, 4)

BACK_ORDER = (
    (
        GREET, D_CORE, D_CORE + 3, D_CORE + 2, D_CORE + 1,
    ),
    (
        D_LOCAL, D_ONE + 2, U_CORE, U_CORE + 3, U_CORE + 2, U_CORE + 1, D_ONE + 1, D_ONE + 3,
    ),
    (
        U_LOCAL, D_LEFT + 2, D_RIGHT + 2, D_RIGHT + 1, D_LEFT + 1, D_ONE,
    ),
    (
        D_THREE + 1, D_SEND + 1, U_ONE + 1, D_LEFT + 3, D_RIGHT + 3, U_ONE, D_THREE + 2, D_SEND + 2,
    ),
    (
        D_LEFT, D_RIGHT, U_ONE + 3, D_THREE + 3, D_SEND + 3, U_ONE + 2,
    ),
    (
        D_THREE, D_SUM, U_LEFT + 1, U_LEFT, U_RIGHT + 1, U_RIGHT,
    ),
    (
        D_PASS_X, D_PASS_Y, U_RIGHT + 2, U_RIGHT + 3, U_THREE + 1, U_LEFT + 2, U_LEFT + 3,
    ),
    (
        U_THREE, D_SHARE,
    ),
    (
        U_THREE + 2, U_THREE + 3, D_END,
    ),
)
LATE_ORDER = (
    GREET, X_CORE + 3, X_CORE + 1, X_LOCAL, LOAD, U_SEND + 1, U_SEND + 2, U_SEND + 3, X_CORE + 2, X_ONE + 3,
    X_CORE, X_ONE + 2, X_ONE + 1, X_ONE, LOADED, GRAD_Q, GRAD_V, X_RIGHT + 2, X_LEFT + 3, X_LEFT + 2,
    X_RIGHT + 3, GRAD_K, H_CORE + 3, X_RIGHT + 1, X_LEFT + 1, X_LEFT, X_RIGHT, H_CORE + 1, X_THREE + 2,
    H_CORE + 2, X_THREE + 3, H_CORE, H_ONE + 3, X_THREE + 1, H_ONE + 2, X_THREE, NORM, H_LEFT + 3,
    H_RIGHT + 3, T_FIRST, NORM_REST, H_THREE + 3, H_SEND + 3, H_RIGHT + 2, H_LEFT + 2, S_FIRST, T_PASS_X, T_PASS_Y,
    H_ONE + 1, U_SUM, H_THREE + 2, H_SEND + 2, T_CORE, T_ROWS, H_RIGHT + 1, H_LEFT + 1, T_ROWS + 1, H_ONE,
    U_PASS_X, T_ROWS + 2, S_CORE, H_THREE + 1, H_SEND + 1, T_ROWS + 3, H_RIGHT, U_PASS_Y, H_LEFT, T_SUM,
    S_X, H_THREE, H_SUM, U_SHARE, S_Y, H_PASS_Y, T_PASS, H_PASS_X, H_SHARE, S_COLLECT, H_END,
    U_END, S_END, T_END,
)

F32 = jnp.float32
BF16 = jnp.bfloat16


def dot(left, right, left_dim=1, right_dim=0):
    return lax.dot_general(
        left, right, (((left_dim,), (right_dim,)), ((), ())), preferred_element_type=F32
    )


def contract_exact(left, right):
    return lax.dot_general(left, right, (((0,), (0,)), ((), ())), precision=lax.Precision.HIGHEST)


def whole(shape):
    return pl.BlockSpec(shape, lambda *_: (0,) * len(shape))


def params(**more):
    return pltpu.CompilerParams(vmem_limit_bytes=VMEM_LIMIT, **more)


def norm_parts(values):
    centre = values - jnp.mean(values, axis=-1, keepdims=True)
    spread = jnp.mean(centre * centre, axis=-1, keepdims=True)
    scale = lax.rsqrt(spread + EPSILON)
    return centre * scale, scale


def norm_back(incoming, gain, unit, scale):
    scaled = incoming * gain
    inner = scaled - jnp.mean(scaled, axis=-1, keepdims=True)
    return scale * (inner - unit * jnp.mean(scaled * unit, axis=-1, keepdims=True))


def place():
    seq = lax.axis_index("seq")
    return lax.axis_index("dp"), lax.axis_index("head"), lax.div(seq, 2), lax.rem(seq, 2)


def device(z, x, y, c):
    return (z, x, y * 2 + c)


def neighbours():
    z, x, y, c = place()
    planes = lax.axis_size("dp")
    near = [device(z, x, y, 1 - c), device(z, 1 - x, y, c), device(z, x, 1 - y, c)]
    return near, [device(lax.rem(z + step, planes), x, y, c) for step in range(1, planes)]


def greet(devices):
    barrier = pltpu.get_barrier_semaphore()
    for other in devices:
        pl.semaphore_signal(barrier, inc=1, device_id=other, device_id_type=MESH)
    pl.semaphore_wait(barrier, len(devices))


def send(source, target, sems, slot, other):
    return pltpu.make_async_remote_copy(
        src_ref=source,
        dst_ref=target,
        send_sem=sems[0].at[slot],
        recv_sem=sems[1].at[slot],
        device_id=other,
        device_id_type=MESH,
    )


def column_of(row):
    size = row.shape[1]
    shape = (size, size)
    same = lax.broadcasted_iota(jnp.int32, shape, 0) == lax.broadcasted_iota(jnp.int32, shape, 1)
    return jnp.sum(jnp.where(same, jnp.broadcast_to(row, shape), 0.0), axis=1, keepdims=True)


def split_three(values):
    high = values.astype(BF16)
    rest = values - high.astype(F32)
    middle = rest.astype(BF16)
    return high, middle, (rest - middle.astype(F32)).astype(BF16)


def dot_three(left, right):
    return sum(dot(part, right) for part in split_three(left))


def gather_kernel(
    table,
    tokens,
    segments,
    timesteps,
    lengths,
    input_weight,
    first_weight,
    second_weight,
    full,
    notes_all,
    mean_out,
    entry_out,
    hidden_out,
    acts_out,
    features_out,
    steps_all,
    acts,
    sums,
    local,
    *sems,
):
    z, x, y, c = place()
    seq = y * 2 + c
    own = x * 4 + seq
    near, planes = neighbours()
    others = []
    for flip in range(1, 8):
        xx, yy, cc = flip // 4, (flip // 2) % 2, flip % 2
        others.append(device(z, x + xx - 2 * xx * x, y + yy - 2 * yy * y, c + cc - 2 * cc * c))
    slot_count = timesteps.shape[1]
    notes_all[own, 0:3] = tokens[...]
    notes_all[own, 3:6] = segments[...]
    notes_all[own, 6:8] = jnp.zeros((2, 128), jnp.int32)
    notes_all[own, 6:7, 0:slot_count] = timesteps[...]
    notes_all[own, 7:8, 0:slot_count] = lengths[...]
    notes = notes_all.at[own]
    greet(others + planes)
    keep = pltpu.make_async_copy(table, full.at[seq], local.at[0])
    keep.start()
    tables = [
        send(table, full.at[seq], sems, 0, near[2]),
        send(table, full.at[seq], sems, 1, near[0]),
    ]
    for copy in tables:
        copy.start()
    copies = [send(notes, notes, sems, 3 + index, other) for index, other in enumerate(others)]
    steps = [
        send(notes, steps_all.at[z], sems, 13 + index, other) for index, other in enumerate(planes)
    ]
    for copy in copies + steps:
        copy.start()
    wide = table[...].astype(F32)
    norms = jnp.sqrt(jnp.sum(wide * wide, axis=1, keepdims=True))
    total = jnp.sum(norms, axis=0, keepdims=True)
    sums[seq] = jnp.broadcast_to(total, (8, 128))
    partials = [
        send(sums.at[seq], sums.at[seq], sems, 10 + index, other)
        for index, other in enumerate((near[0], near[2], device(z, x, 1 - y, 1 - c)))
    ]
    for copy in partials:
        copy.start()
    for copy in steps:
        copy.wait()
    steps_all[z] = notes_all[own]

    count = steps_all.shape[0]
    half = features_out.shape[0] // 2
    lanes = lax.broadcasted_iota(jnp.int32, (SLOTS, 2 * half), 1)
    slots = lax.broadcasted_iota(jnp.int32, (SLOTS, 2 * half), 0)
    freqs = jnp.exp((-math.log(10000.0)) * jnp.where(lanes < half, lanes, lanes - half).astype(F32) / half)
    parts = []
    for plane in range(count):
        angles = column_of(steps_all[plane, 6:7].astype(F32))[0:SLOTS] * freqs
        waves = jnp.where(lanes < half, jnp.cos(angles), jnp.sin(angles))
        parts.append(jnp.where(slots < slot_count, waves, 0.0))
    features = jnp.concatenate(parts, axis=0)
    features_out[...] = features.T
    hidden = dot_three(features, first_weight[...])
    hidden_out[...] = hidden
    act = hidden / (1.0 + jnp.exp(-hidden))
    acts[...] = act
    acts_out[...] = act.T
    time_rows = dot_three(acts[pl.ds(pl.multiple_of(z * SLOTS, SLOTS), SLOTS), :], second_weight[...])
    entry_out[0:128] = input_weight[...]
    for index, part in enumerate(split_three(time_rows)):
        entry_out[128 + index * SLOTS : 128 + (index + 1) * SLOTS] = part
    entry_out[128 + 3 * SLOTS : 256] = jnp.zeros((128 - 3 * SLOTS, entry_out.shape[1]), BF16)

    for copy in copies + partials:
        copy.wait()
    mean_out[...] = jnp.sum(sums[...], axis=0) * (1.0 / VOCAB)
    tables[0].wait_recv()
    away = (1 - y) * 2 + c
    forward = send(full.at[away], full.at[away], sems, 2, near[0])
    forward.start()
    keep.wait()
    tables[1].wait_recv()
    forward.wait()
    for copy in tables:
        copy.wait_send()


def gather(table, tokens, segments, timesteps, lengths, input_weight, first_weight, second_weight):
    rows, _ = table.shape
    width = input_weight.shape[1]
    planes = lax.axis_size("dp")
    vmem = pl.BlockSpec(memory_space=pltpu.VMEM)
    hbm = pl.BlockSpec(memory_space=pltpu.HBM)
    slots = 13 + planes - 1
    return pl.pallas_call(
        gather_kernel,
        in_specs=[vmem] * 8,
        out_specs=[hbm] + [vmem] * 6,
        out_shape=[
            jax.ShapeDtypeStruct((4, rows, 128), BF16),
            jax.ShapeDtypeStruct((8, 8, 128), jnp.int32),
            jax.ShapeDtypeStruct((8, 128), F32),
            jax.ShapeDtypeStruct((256, width), BF16),
            jax.ShapeDtypeStruct((planes * SLOTS, width), F32),
            jax.ShapeDtypeStruct((width, planes * SLOTS), F32),
            jax.ShapeDtypeStruct((first_weight.shape[0], planes * SLOTS), F32),
        ],
        scratch_shapes=[
            pltpu.VMEM((planes, 8, 128), jnp.int32),
            pltpu.VMEM((planes * SLOTS, width), F32),
            pltpu.VMEM((4, 8, 128), F32),
            pltpu.SemaphoreType.DMA((1,)),
            pltpu.SemaphoreType.DMA((slots,)),
            pltpu.SemaphoreType.DMA((slots,)),
        ],
        compiler_params=params(collective_id=0, has_side_effects=True),
        name="gather",
    )(table, tokens, segments, timesteps, lengths, input_weight, first_weight, second_weight)


def embed_kernel(
    own,
    tokens,
    notes,
    mean_norm,
    table_low,
    entry,
    gain,
    shift,
    query_weight,
    key_weight,
    value_weight,
    normed_out,
    key_out,
    value_out,
    mark_out,
    stream_out,
    query_out,
    low_out,
    found_out,
    picked,
    limits,
    table,
):
    step = pl.program_id(0)
    blocks = pl.num_programs(0)
    rows = picked.shape[1]
    width = stream_out.shape[1]
    block = lax.rem(own[0] + step, blocks)
    base = block * rows

    @pl.when(step == 0)
    def _():
        kinds = lax.broadcasted_iota(jnp.int32, (128, 128), 0)
        below = jnp.zeros((128, 128), F32)
        for part in range(blocks if isinstance(blocks, int) else 8):
            for line in range(3, 6):
                below = below + jnp.where(notes[part, line : line + 1, :] < kinds, 1.0, 0.0)
        starts = jnp.sum(below, axis=1, keepdims=True)
        shape = (128, 128)
        same = lax.broadcasted_iota(jnp.int32, shape, 0) == lax.broadcasted_iota(jnp.int32, shape, 1)
        starts = jnp.sum(jnp.where(same, jnp.broadcast_to(starts, shape), 0.0), axis=0, keepdims=True)
        limits[...] = starts + notes[own[0], 7:8, :].astype(F32)
        for part in range(4):
            table[part * 2048 : (part + 1) * 2048, :] = table_low[part].astype(F32)

    def pick(slot, source, row):
        line, lane = row // 128, row % 128
        picked[slot, pl.ds(row, 1), :] = table[pl.ds(tokens[source, line, lane], 1), :]

    @pl.when(step == 0)
    def _():
        def pick_some(index, carry):
            for inner in range(32):
                pick(0, block, index * 32 + inner)
            return carry

        lax.fori_loop(0, rows // 32, pick_some, 0)

    found = picked[lax.rem(step, 2)]
    low = (found / mean_norm[0:1]).astype(BF16)
    following = lax.rem(block + 1, blocks)
    for row in range(rows):
        pick(lax.rem(step + 1, 2), following, row)
    lanes = lax.broadcasted_iota(jnp.int32, (rows, 128), 1)
    slot = jnp.concatenate(
        [column_of(notes[block, line : line + 1, :].astype(F32)) for line in range(3, 6)], axis=0
    )
    same = jnp.where((lanes & (SLOTS - 1)).astype(F32) == slot, 1.0, 0.0)
    spread = jnp.where(lanes < 3 * SLOTS, same, 0.0).astype(BF16)
    stream = dot(jnp.concatenate([low, spread], axis=1), entry[...])
    unit, _ = norm_parts(stream)
    normed = (unit * gain[...].reshape(1, width) + shift[...].reshape(1, width)).astype(BF16)
    normed_out[...] = normed.T
    for weight, target in ((key_weight, key_out), (value_weight, value_out)):
        result = dot(normed, weight[...]).astype(BF16)
        for pair in range(width // 128):
            target[pair] = result[:, pair * 128 : (pair + 1) * 128]
    first = jnp.where(lanes < SLOTS, same, 0.0)
    limit = jnp.sum(first * limits[...], axis=1, keepdims=True)
    index = (base + lax.broadcasted_iota(jnp.int32, (rows, 1), 0)).astype(F32)
    dead = jnp.where(index < limit, 0.0, 1.0)
    marks = jnp.where(lanes == DEAD, dead, first)
    marks = jnp.where((lanes >= ONES) & (lanes < ONES + 2), 1.0, marks)
    mark_out[...] = marks.astype(BF16)

    @pl.when(step == 0)
    def _():
        stream_out[...] = stream
        low_out[...] = low
        found_out[...] = found.astype(BF16)
        query = dot(query_weight[...], normed, 0, 1) * (LOG2E / math.sqrt(HEAD_DIM))
        query_out[...] = query.astype(BF16)


def embed(own, notes, mean_norm, table, entry, gain, shift, wq, wk, wv, rows, blocks):
    group = rows * blocks
    width = wq.shape[0]
    turn = lambda step, own: (lax.rem(own[0] + step, blocks), 0)
    return pl.pallas_call(
        embed_kernel,
        grid_spec=pltpu.PrefetchScalarGridSpec(
            num_scalar_prefetch=1,
            grid=(blocks,),
            in_specs=[
                pl.BlockSpec(memory_space=pltpu.SMEM),
                whole(notes.shape),
                whole((8, 128)),
                whole(table.shape),
                whole(entry.shape),
                whole((width,)),
                whole((width,)),
                whole((width, width)),
                whole((width, width)),
                whole((width, width)),
            ],
            out_specs=[
                pl.BlockSpec((width, rows), lambda *args: turn(*args)[::-1]),
                pl.BlockSpec((width // 128, rows, 128), lambda *args: (0, *turn(*args))),
                pl.BlockSpec((width // 128, rows, 128), lambda *args: (0, *turn(*args))),
                pl.BlockSpec((rows, 128), turn),
                whole((rows, width)),
                whole((width, rows)),
                whole((rows, 128)),
                whole((rows, 128)),
            ],
            scratch_shapes=[
                pltpu.VMEM((2, rows, 128), F32),
                pltpu.VMEM((1, 128), F32),
                pltpu.VMEM((VOCAB, 128), F32),
            ],
        ),
        out_shape=[
            jax.ShapeDtypeStruct((width, group), BF16),
            jax.ShapeDtypeStruct((width // 128, group, 128), BF16),
            jax.ShapeDtypeStruct((width // 128, group, 128), BF16),
            jax.ShapeDtypeStruct((group, 128), BF16),
            jax.ShapeDtypeStruct((rows, width), F32),
            jax.ShapeDtypeStruct((width, rows), BF16),
            jax.ShapeDtypeStruct((rows, 128), BF16),
            jax.ShapeDtypeStruct((rows, 128), BF16),
        ],
        compiler_params=params(),
        name="embed",
    )(own, notes, notes, mean_norm, table, entry, gain, shift, wq, wk, wv)


def pair_columns(target, pair, rows):
    target[0:HEAD_DIM, 0:rows] = pair[0:HEAD_DIM]
    target[0:HEAD_DIM, rows : 2 * rows] = jnp.zeros((HEAD_DIM, rows), BF16)
    target[HEAD_DIM : 2 * HEAD_DIM, 0:rows] = jnp.zeros((HEAD_DIM, rows), BF16)
    target[HEAD_DIM : 2 * HEAD_DIM, rows : 2 * rows] = pair[HEAD_DIM : 2 * HEAD_DIM]


def forward_kernel(query, keys, values, marks, slots, probs_out, mixed_out, inverse_out, right, scores):
    rows = query.shape[1]
    group = keys.shape[0]
    blocks = group // KEY_BLOCK
    pair_columns(right, query, rows)
    kinds = lax.broadcasted_iota(jnp.int32, (128, rows), 0)
    slot = jnp.concatenate([slots[line : line + 1, :] for line in range(rows // 128)], axis=1)
    away = jnp.where((kinds < DEAD) & (kinds != slot), MASKED, 0.0)
    away = jnp.where(kinds == DEAD, MASKED, away).astype(BF16)
    right[128:256, 0:rows] = away
    right[128:256, rows : 2 * rows] = away

    ones = jnp.ones((16, KEY_BLOCK), BF16)

    def left_of(part):
        return jnp.concatenate([keys[part, :], marks[part, :]], axis=1)

    def weigh(part, probs, total):
        probs_out[part, :] = probs
        return total + dot(jnp.concatenate([values[part, :].T, ones], axis=0), probs)

    def store(total):
        inverse = 1.0 / total[128:129]
        mixed_out[0:HEAD_DIM] = total[0:HEAD_DIM, 0:rows] * inverse[:, 0:rows]
        mixed_out[HEAD_DIM:128] = total[HEAD_DIM:128, rows : 2 * rows] * inverse[:, rows : 2 * rows]
        inverse_out[0, 0:1] = inverse[:, 0:rows]
        inverse_out[0, 1:2] = inverse[:, rows : 2 * rows]

    highest = jnp.max(jnp.abs(keys[...]).astype(F32), axis=0, keepdims=True)
    spans = jnp.abs(query[...].astype(F32)) * column_of(highest)
    first = jnp.max(jnp.sum(spans[0:HEAD_DIM], axis=0, keepdims=True))
    second = jnp.max(jnp.sum(spans[HEAD_DIM : 2 * HEAD_DIM], axis=0, keepdims=True))
    bounded = jnp.maximum(first, second) < SAFE

    @pl.when(bounded)
    def _():
        total = jnp.zeros((144, 2 * rows), F32)
        for index in range(blocks):
            part = slice(index * KEY_BLOCK, (index + 1) * KEY_BLOCK)
            probs = jnp.exp2(dot(left_of(part), right[...])).astype(BF16)
            total = weigh(part, probs, total)
        store(total)

    @pl.when(jnp.logical_not(bounded))
    def _():
        def part_of(index):
            return pl.ds(pl.multiple_of(index * KEY_BLOCK, KEY_BLOCK), KEY_BLOCK)

        def score(index, top):
            part = part_of(index)
            current = dot(left_of(part), right[...])
            scores[part, :] = current
            return jnp.maximum(top, jnp.max(current.reshape(KEY_BLOCK // 8, 8, 2 * rows), axis=0))

        top = lax.fori_loop(0, blocks, score, jnp.full((8, 2 * rows), MASKED, F32))
        top = jnp.max(top, axis=0, keepdims=True)

        def shifted(index, total):
            part = part_of(index)
            return weigh(part, jnp.exp2(scores[part, :] - top).astype(BF16), total)

        store(lax.fori_loop(0, blocks, shifted, jnp.zeros((144, 2 * rows), F32)))


def attend(query, keys, values, marks, slots):
    width, rows = query.shape
    group = keys.shape[1]
    pairs = width // 128
    column = pl.BlockSpec((None, group, 128), lambda pair: (pair, 0, 0))
    return pl.pallas_call(
        forward_kernel,
        grid=(pairs,),
        in_specs=[
            pl.BlockSpec((128, rows), lambda pair: (pair, 0)),
            column,
            column,
            whole((group, 128)),
            whole((rows // 128, 128)),
        ],
        out_specs=[
            pl.BlockSpec((None, group, 2 * rows), lambda pair: (pair, 0, 0)),
            pl.BlockSpec((128, rows), lambda pair: (pair, 0)),
            pl.BlockSpec((1, 2, rows), lambda pair: (pair, 0, 0)),
        ],
        out_shape=[
            jax.ShapeDtypeStruct((pairs, group, 2 * rows), BF16),
            jax.ShapeDtypeStruct((width, rows), F32),
            jax.ShapeDtypeStruct((pairs, 2, rows), F32),
        ],
        scratch_shapes=[pltpu.VMEM((256, 2 * rows), BF16), pltpu.VMEM((group, 2 * rows), F32)],
        compiler_params=params(),
        name="attend",
    )(query, keys, values, marks, slots)


def feed_kernel(
    mixed_wide,
    inverse,
    stream,
    upstream,
    gain,
    shift,
    output_hbm,
    up_hbm,
    down_hbm,
    activation_out,
    middle_grad_out,
    norm_out,
    mixed_grad_out,
    row_out,
    output_grad_hbm,
    up_grad_hbm,
    down_grad_hbm,
    output_weight,
    up_weight,
    down_weight,
    output_grad,
    up_grad,
    down_grad,
    activation_sum,
    normed_sum,
    loads,
    stores,
):
    rows, width = stream.shape
    hidden_width = up_weight.shape[1]
    chunk = width
    chunks = hidden_width // chunk
    load_output = pltpu.make_async_copy(output_hbm, output_weight, loads.at[0])
    load_output.start()

    def load_parts(index):
        part = pl.ds(pl.multiple_of(index * chunk, 128), chunk)
        return (
            pltpu.make_async_copy(up_hbm.at[:, part], up_weight.at[:, part], loads.at[1 + 2 * index]),
            pltpu.make_async_copy(down_hbm.at[part], down_weight.at[part], loads.at[2 + 2 * index]),
        )

    def store_parts(index):
        y, c = lax.rem(index, 2), lax.div(index, 2)
        return (
            pltpu.make_async_copy(
                down_grad.at[:, :, :, index], down_grad_hbm.at[:, :, :, index], stores.at[1 + 2 * index]
            ),
            pltpu.make_async_copy(up_grad.at[c, y], up_grad_hbm.at[c, y], stores.at[2 + 2 * index]),
        )

    for index in range(chunks):
        for copy in load_parts(index):
            copy.start()
    mixed = mixed_wide[...].astype(BF16)
    load_output.wait()
    middle = stream[...] + dot(mixed, output_weight[...], 0, 0)
    unit, scale = norm_parts(middle)
    wide_gain = gain[...].reshape(1, width)
    normed = (unit * wide_gain + shift[...].reshape(1, width)).astype(BF16)
    normed_t = normed.T
    incoming = upstream[...]
    activation_sum[...] = middle
    normed_sum[...] = jnp.zeros((rows, width), F32)

    def step(index, carry):
        part = pl.ds(pl.multiple_of(index * chunk, 128), chunk)
        for copy in load_parts(index):
            copy.wait()
        pre = dot(normed, up_weight[:, part])
        cdf = 0.5 * (1.0 + lax.erf(pre * math.sqrt(0.5)))
        slope = cdf + pre * jnp.exp(-0.5 * pre * pre) * (1.0 / math.sqrt(2.0 * math.pi))
        hidden = (pre * cdf).astype(BF16)
        back = dot(incoming, down_weight[part, :], 1, 1)
        pre_grad = (back * slope).astype(BF16)
        activation_sum[...] += dot(hidden, down_weight[part, :])
        down_part = dot(hidden, incoming, 0, 0).astype(BF16).reshape(8, PIECE, width)
        for piece in range(8):
            down_grad[piece // 4, piece // 2 % 2, piece % 2, index] = down_part[piece]
        up_part = dot(normed_t, pre_grad).astype(BF16).reshape(4, 2, PIECE, width)
        for half in range(2):
            up_grad[lax.div(index, 2), lax.rem(index, 2), half] = up_part[:, half]
        for copy in store_parts(index):
            copy.start()
        normed_sum[...] += dot(pre_grad, up_weight[:, part], 1, 1)
        return carry

    lax.fori_loop(0, chunks, step, 0)
    activation = activation_sum[...]
    normed_grad = normed_sum[...]
    activation_out[...] = activation.astype(BF16)
    norm_out[0:1] = jnp.sum(normed_grad * unit, axis=0, keepdims=True)
    norm_out[1:2] = jnp.sum(normed_grad, axis=0, keepdims=True)
    middle_grad = incoming.astype(F32) + norm_back(normed_grad, wide_gain, unit, scale)
    middle_grad_out[...] = middle_grad
    middle_low = middle_grad.astype(BF16)
    output_part = dot(mixed, middle_low).astype(BF16).reshape(4, 2, PIECE, width)
    for half in range(2):
        output_grad[half] = output_part[:, half]
    store_output = pltpu.make_async_copy(output_grad, output_grad_hbm, stores.at[0])
    store_output.start()
    mixed_grad = dot(output_weight[...], middle_low, 1, 1).astype(BF16).astype(F32)
    for head in range(HEADS):
        part = slice(head * HEAD_DIM, (head + 1) * HEAD_DIM)
        factor = inverse[head // 2, head % 2 : head % 2 + 1]
        mixed_grad_out[part, :] = (mixed_grad[part] * factor).astype(BF16)
        row_out[head // 2, head % 2 : head % 2 + 1] = factor * jnp.sum(
            mixed_grad[part] * mixed_wide[part, :], axis=0, keepdims=True
        )
    store_output.wait()
    for index in range(chunks):
        for copy in store_parts(index):
            copy.wait()


def feed(mixed, inverse, stream, upstream, gain, shift, output_weight, up_weight, down_weight):
    rows, width = stream.shape
    hidden_width = up_weight.shape[1]
    vmem = pl.BlockSpec(memory_space=pltpu.VMEM)
    hbm = pl.BlockSpec(memory_space=pltpu.HBM)
    return pl.pallas_call(
        feed_kernel,
        in_specs=[vmem] * 6 + [hbm] * 3,
        out_specs=[vmem] * 5 + [hbm] * 3,
        out_shape=[
            jax.ShapeDtypeStruct((rows, width), BF16),
            jax.ShapeDtypeStruct((rows, width), F32),
            jax.ShapeDtypeStruct((2, width), F32),
            jax.ShapeDtypeStruct((width, rows), BF16),
            jax.ShapeDtypeStruct((HEADS // 2, 2, rows), F32),
            jax.ShapeDtypeStruct((2, 4, PIECE, width), BF16),
            jax.ShapeDtypeStruct(UNIT, BF16),
            jax.ShapeDtypeStruct(UNIT, BF16),
        ],
        scratch_shapes=[
            pltpu.VMEM((width, width), BF16),
            pltpu.VMEM((width, hidden_width), BF16),
            pltpu.VMEM((hidden_width, width), BF16),
            pltpu.VMEM((2, 4, PIECE, width), BF16),
            pltpu.VMEM(UNIT, BF16),
            pltpu.VMEM(UNIT, BF16),
            pltpu.VMEM((rows, width), F32),
            pltpu.VMEM((rows, width), F32),
            pltpu.SemaphoreType.DMA((9,)),
            pltpu.SemaphoreType.DMA((9,)),
        ],
        compiler_params=params(),
        name="feed",
    )(mixed, inverse, stream, upstream, gain, shift, output_weight, up_weight, down_weight)


class Plane:
    def __init__(self, unit, local, scratch):
        self.unit, self.local = unit, local
        self.one, self.two_a, self.two_b, self.three, self.sems = *scratch[:4], scratch[4:6]
        self.z, self.x, self.y, self.c = place()
        (self.core, self.across, self.along), _ = neighbours()
        self.half = self.three.shape[-1] // 2

    def chunk(self, step):
        return lax.rem(self.z + step, 4)

    def copy(self, slot, step):
        x, y, z, half = self.x, self.y, self.chunk(step), self.half
        left, right = pl.ds(0, half), pl.ds(half, half)
        sem = slot * 4 + step
        if slot == 0:
            source, target = self.unit.at[1 - self.c, :, :, z], self.one.at[:, :, z]
            return send(source, target, self.sems, sem, self.core)
        if slot == 1:
            source, target = self.one.at[:, 1 - x, z, :, left], self.two_a.at[:, z]
            return send(source, target, self.sems, sem, self.across)
        if slot == 2:
            source, target = self.one.at[1 - y, :, z, :, right], self.two_b.at[:, z]
            return send(source, target, self.sems, sem, self.along)
        if slot == 3:
            source, target = self.two_a.at[1 - y, z], self.three.at[z, :, left]
            return send(source, target, self.sems, sem, self.along)
        source, target = self.two_b.at[1 - x, z], self.three.at[z, :, right]
        return send(source, target, self.sems, sem, self.across)

    def begin(self, step):
        self.copy(0, step).start()

    def add_one(self, step):
        z = self.chunk(step)
        self.copy(0, step).wait_recv()
        for y in range(2):
            for x in range(2):
                self.one[y, x, z] = self.one[y, x, z] + self.local(y, x, z)
        self.copy(1, step).start()
        self.copy(2, step).start()

    def add_two_a(self, step):
        z = self.chunk(step)
        self.copy(1, step).wait_recv()
        for y in range(2):
            self.two_a[y, z] = self.two_a[y, z] + self.one[y, self.x, z, :, 0 : self.half]
        self.copy(3, step).start()

    def add_two_b(self, step):
        z = self.chunk(step)
        self.copy(2, step).wait_recv()
        for x in range(2):
            self.two_b[x, z] = self.two_b[x, z] + self.one[self.y, x, z, :, self.half : 2 * self.half]
        self.copy(4, step).start()

    def add_three(self, step):
        z, half = self.chunk(step), self.half
        self.copy(3, step).wait_recv()
        self.copy(4, step).wait_recv()
        self.three[z, :, 0:half] = self.three[z, :, 0:half] + self.two_a[self.y, z]
        right = slice(half, 2 * half)
        self.three[z, :, right] = self.three[z, :, right] + self.two_b[self.x, z]

    def finish(self):
        for slot in range(5):
            for step in range(4):
                self.copy(slot, step).wait_send()

    def actions(self, first):
        kinds = (self.begin, self.add_one, self.add_two_a, self.add_two_b, self.add_three)
        return {
            first + 4 * index + step: functools.partial(kind, step)
            for index, kind in enumerate(kinds)
            for step in range(4)
        }


def plane_buffers():
    _, _, _, zs, piece, width = UNIT
    return [
        pltpu.VMEM((2, 2, zs, piece, width), BF16),
        pltpu.VMEM((2, zs, piece, width // 2), BF16),
        pltpu.VMEM((2, zs, piece, width // 2), BF16),
        pltpu.VMEM((zs, piece, width), BF16),
        pltpu.SemaphoreType.DMA((20,)),
        pltpu.SemaphoreType.DMA((20,)),
    ]


class Line:
    def __init__(self, three, scratch, out):
        self.three, self.four, self.sems, self.out = three, scratch[0], scratch[1:3], out
        self.z, self.x, self.y, self.c = place()
        (self.core, self.across, self.along), self.planes = neighbours()
        self.half = three.shape[-1] // 2

    def copy(self, slot):
        x, y, c = self.x, self.y, self.c
        left, right = pl.ds(0, self.half), pl.ds(self.half, self.half)
        if slot < 3:
            target = lax.rem(self.z + slot + 1, 4)
            return send(self.three.at[target], self.four.at[slot], self.sems, slot, self.planes[slot])
        mine = self.out.at[c, y, x]
        if slot == 3:
            return send(mine, mine, self.sems, 3, self.across)
        if slot == 4:
            return send(mine, mine, self.sems, 4, self.along)
        if slot == 5:
            other = self.out.at[c, y, 1 - x, :, left]
            return send(other, other, self.sems, 5, self.along)
        if slot == 6:
            other = self.out.at[c, 1 - y, x, :, right]
            return send(other, other, self.sems, 6, self.across)
        return send(self.out.at[c], self.out.at[c], self.sems, 7, self.core)

    def begin(self, step):
        if step:
            self.copy(step - 1).start()

    def add(self):
        total = self.three[self.z].astype(F32)
        for slot in range(3):
            self.copy(slot).wait_recv()
            total = total + self.four[slot].astype(F32)
        self.out[self.c, self.y, self.x] = total.astype(BF16)
        self.copy(3).start()
        self.copy(4).start()

    def forward(self, slot):
        self.copy(slot).wait_recv()
        self.copy(slot + 2).start()

    def share(self):
        self.copy(5).wait_recv()
        self.copy(6).wait_recv()
        self.copy(7).start()

    def end(self):
        self.copy(7).wait_recv()

    def finish(self):
        for slot in range(8):
            self.copy(slot).wait_send()

    def actions(self, first):
        steps = {first + step: functools.partial(self.begin, step) for step in range(4)}
        forward_x, forward_y = (functools.partial(self.forward, slot) for slot in (3, 4))
        rest = (self.add, forward_x, forward_y, self.share, self.end)
        steps.update({first + 4 + 4 * index: step for index, step in enumerate(rest)})
        return steps


def line_buffers():
    _, _, _, _, piece, width = UNIT
    return [
        pltpu.VMEM((3, piece, width), BF16),
        pltpu.SemaphoreType.DMA((8,)),
        pltpu.SemaphoreType.DMA((8,)),
    ]


def back_kernel(
    linked,
    query,
    keys,
    values,
    marks,
    probs,
    mixed_grad,
    row_sums,
    query_hbm,
    key_hbm,
    value_hbm,
    down_unit,
    up_unit,
    query_back_hbm,
    key_back_hbm,
    value_back_hbm,
    normed_unit,
    down_out,
    up_out,
    left,
    right,
    query_back,
    key_back,
    value_back,
    query_weight,
    key_weight,
    value_weight,
    staged,
    loads,
    stores,
    pair_sems,
    *scratch,
):
    pair = pl.program_id(0)
    pairs = pl.num_programs(0) - 1
    width, rows = query_back.shape
    group = keys.shape[0]
    blocks = group // KEY_BLOCK
    owners = group // rows
    copies = [
        pltpu.make_async_copy(source, target, loads.at[index])
        for index, (source, target) in enumerate(
            ((query_hbm, query_weight), (key_hbm, key_weight), (value_hbm, value_weight))
        )
    ]
    steps = {}
    if linked:
        down_local, up_local = scratch[0:2]
        down = Plane(down_unit, lambda y, x, z: down_local[y, x, z], scratch[2:8])
        up = Plane(up_unit, lambda y, x, z: up_local[y, x, z], scratch[8:14])
        line = Line(down.three, scratch[14:17], scratch[17])
        seat = lax.rem(lax.axis_index("seq"), 2)
        locals_ = [
            pltpu.make_async_copy(down_unit.at[seat], down_local, loads.at[3]),
            pltpu.make_async_copy(up_unit.at[seat], up_local, loads.at[4]),
        ]
        down_store = pltpu.make_async_copy(scratch[17], down_out, stores.at[5])
        up_store = pltpu.make_async_copy(up.three, up_out, stores.at[6])

        steps = {
            GREET: lambda: greet(neighbours()[0] + neighbours()[1]),
            D_LOCAL: locals_[0].wait,
            U_LOCAL: locals_[1].wait,
        }
        steps.update(down.actions(D_CORE))
        steps.update(up.actions(U_CORE))
        steps.update(line.actions(D_SEND))

    def pair_stores(pair):
        column = pl.ds(pl.multiple_of(pair * 128, 128), 128)
        return [
            pltpu.make_async_copy(source.at[:, column], target.at[:, column], pair_sems.at[index, pair])
            for index, (source, target) in enumerate(
                ((key_back, key_back_hbm), (value_back, value_back_hbm))
            )
        ]

    def run(spot):
        if linked:
            for key in BACK_ORDER[spot]:
                steps[key]()

    @pl.when(pair == 0)
    def _():
        if linked:
            locals_[0].start()
        run(0)

    @pl.when(pair == 1)
    def _():
        if linked:
            locals_[1].start()

    @pl.when(pair == 3)
    def _():
        for copy in copies:
            copy.start()

    @pl.when(pair < pairs)
    def _():
        pair_columns(left, query, rows)
        pair_columns(right, mixed_grad, rows)
        kinds = lax.broadcasted_iota(jnp.int32, (128, rows), 0)
        shape = (128, rows)
        for half in range(2):
            total = -row_sums[0, half : half + 1]
            high = total.astype(BF16).astype(F32)
            fill = jnp.where(kinds == ONES, jnp.broadcast_to(high, shape), 0.0)
            fill = jnp.where(kinds == ONES + 1, jnp.broadcast_to(total - high, shape), fill)
            right[128:256, half * rows : (half + 1) * rows] = fill.astype(BF16)

        column = pl.ds(pl.multiple_of(pair * 128, 128), 128)

        def block(index, total):
            part = pl.ds(pl.multiple_of(index * KEY_BLOCK, KEY_BLOCK), KEY_BLOCK)
            weights = probs[part, :]
            inner = dot(jnp.concatenate([values[part, :], marks[part, :]], axis=1), right[...])
            score_grad = (weights.astype(F32) * inner).astype(BF16)
            key_back[part, column] = (dot(score_grad, left[...], 1, 1) * LN2).astype(BF16)
            value_back[part, column] = dot(weights, right[0:128, :], 1, 1).astype(BF16)
            return total + dot(keys[part, :].T, score_grad)

        total = lax.fori_loop(0, blocks, block, jnp.zeros((128, 2 * rows), F32), unroll=3)
        scale = HEAD_DIM**-0.5
        base = pl.multiple_of(pair * 128, 128)
        query_back[pl.ds(base, HEAD_DIM), :] = (total[0:HEAD_DIM, 0:rows] * scale).astype(BF16)
        base = pl.multiple_of(pair * 128 + HEAD_DIM, HEAD_DIM)
        query_back[pl.ds(base, HEAD_DIM), :] = (total[HEAD_DIM:128, rows : 2 * rows] * scale).astype(BF16)

        for copy in pair_stores(pair):
            copy.start()
        for spot in range(1, 7):
            if linked and BACK_ORDER[spot]:
                pl.when(pair == spot - 1)(functools.partial(run, spot))

    @pl.when(pair == pairs)
    def _():
        query_store = pltpu.make_async_copy(query_back, query_back_hbm, stores.at[2])
        query_store.start()
        for copy in copies:
            copy.wait()
        own = lax.axis_index("head") * lax.axis_size("seq") + lax.axis_index("seq")

        def owner_store(owner):
            x, y, c = lax.div(owner, 4), lax.rem(lax.div(owner, 2), 2), lax.rem(owner, 2)
            slot = lax.rem(owner, 2)
            return pltpu.make_async_copy(staged.at[slot], normed_unit.at[c, y, x], stores.at[slot])

        def owner_step(owner, carry):
            part = pl.ds(pl.multiple_of(owner * rows, 128), rows)
            slot = lax.rem(owner, 2)
            total = dot(key_back[part, :], key_weight[...], 1, 1)
            total = total + dot(value_back[part, :], value_weight[...], 1, 1)

            @pl.when(owner >= 2)
            def _():
                owner_store(owner).wait()

            staged[slot] = total.astype(BF16).reshape(4, PIECE, width)

            @pl.when(own == owner)
            def _():
                extra = dot(query_back[...], query_weight[...], 0, 1)
                staged[slot] = (total + extra).astype(BF16).reshape(4, PIECE, width)

            owner_store(owner).start()
            return carry

        lax.fori_loop(0, owners // 2, owner_step, 0)
        run(7)
        lax.fori_loop(owners // 2, owners, owner_step, 0)
        run(8)
        for slot in range(2):
            owner_store(slot).wait()
        if linked:
            up_store.start()
            up_store.wait()
            down_store.start()
            down_store.wait()
            down.finish()
            up.finish()
            line.finish()
        query_store.wait()
        for done in range(6):
            for copy in pair_stores(done):
                copy.wait()


def attend_back(linked, query, keys, values, marks, probs, mixed_grad, row_sums, wq, wk, wv, down_unit, up_unit):
    width, rows = query.shape
    group = keys.shape[1]
    pairs = width // 128
    held = lambda pair: jnp.minimum(pair, pairs - 1)
    column = pl.BlockSpec((None, group, 128), lambda pair: (held(pair), 0, 0))
    row = pl.BlockSpec((128, rows), lambda pair: (held(pair), 0))
    hbm = pl.BlockSpec(memory_space=pltpu.HBM)
    third = jax.ShapeDtypeStruct(UNIT[3:], BF16)
    more = dict(collective_id=1, has_side_effects=True) if linked else {}
    scratch = []
    if linked:
        scratch = [pltpu.VMEM(UNIT[1:], BF16)] * 2 + plane_buffers() * 2 + line_buffers()
        scratch += [pltpu.VMEM(UNIT[:3] + UNIT[4:], BF16)]
    return pl.pallas_call(
        functools.partial(back_kernel, linked),
        grid=(pairs + 1,),
        in_specs=[
            row,
            column,
            column,
            pl.BlockSpec((group, 128), lambda pair: (0, 0), pipeline_mode=pl.Buffered(1)),
            pl.BlockSpec((None, group, 2 * rows), lambda pair: (held(pair), 0, 0)),
            row,
            pl.BlockSpec((1, 2, rows), lambda pair: (held(pair), 0, 0)),
        ]
        + [hbm] * 5,
        out_specs=[hbm] * 6,
        out_shape=[
            jax.ShapeDtypeStruct((width, rows), BF16),
            jax.ShapeDtypeStruct((group, width), BF16),
            jax.ShapeDtypeStruct((group, width), BF16),
            jax.ShapeDtypeStruct(UNIT, BF16),
            jax.ShapeDtypeStruct(UNIT[:3] + UNIT[4:], BF16),
            third,
        ],
        scratch_shapes=[
            pltpu.VMEM((128, 2 * rows), BF16),
            pltpu.VMEM((256, 2 * rows), BF16),
            pltpu.VMEM((width, rows), BF16),
            pltpu.VMEM((group, width), BF16),
            pltpu.VMEM((group, width), BF16),
            pltpu.VMEM((width, width), BF16),
            pltpu.VMEM((width, width), BF16),
            pltpu.VMEM((width, width), BF16),
            pltpu.VMEM((2, 4, PIECE, width), BF16),
            pltpu.SemaphoreType.DMA((5,)),
            pltpu.SemaphoreType.DMA((7,)),
            pltpu.SemaphoreType.DMA((2, 6)),
        ]
        + scratch,
        compiler_params=params(**more),
        name="attend_back",
    )(query, keys, values, marks, probs, mixed_grad, row_sums, wq, wk, wv, down_unit, up_unit)


class Rows:
    def __init__(self, given, part, landed, out, sems):
        self.given, self.part, self.landed, self.out, self.sems = given, part, landed, out, sems
        self.z, self.x, self.y, self.c = place()
        (self.core, self.across, self.along), self.planes = neighbours()

    def index(self, x, y, c):
        return x * 4 + y * 2 + c

    def copy(self, slot):
        x, y, c = self.x, self.y, self.c
        size = self.given.shape[1] // 2
        mine = self.given.at[self.index(x, y, c)]
        if slot < 3:
            return send(mine, mine, self.sems, slot, (self.core, self.across, self.along)[slot])
        if slot == 3:
            other = self.given.at[self.index(1 - x, y, c), pl.ds(0, size)]
            return send(other, other, self.sems, 3, self.along)
        if slot == 4:
            other = self.given.at[self.index(x, 1 - y, c), pl.ds(size, size)]
            return send(other, other, self.sems, 4, self.across)
        if slot < 8:
            flip_x, flip_y = ((1, 0), (0, 1), (1, 1))[slot - 5]
            other = self.given.at[
                self.index(x + flip_x - 2 * flip_x * x, y + flip_y - 2 * flip_y * y, c)
            ]
            return send(other, other, self.sems, slot, self.core)
        if slot < 11:
            step = slot - 8
            return send(
                self.part.at[step + 1], self.landed.at[step], self.sems, slot, self.planes[step]
            )
        if slot < 14:
            mine = self.out.at[x, self.z]
            return send(mine, mine, self.sems, slot, self.planes[slot - 11])
        other = self.out.at[x, lax.rem(self.z + 18 - slot, 4)]
        return send(other, other, self.sems, slot, self.across)

    def start(self, *slots):
        for slot in slots:
            self.copy(slot).start()

    def landed_all(self, *slots):
        for slot in slots:
            self.copy(slot).wait_recv()

    def finish(self):
        for slot in range(18):
            self.copy(slot).wait_send()


class Small:
    def __init__(self, rows, entry, half_rows, half_entry, landings, out, entry_out, sems):
        self.rows, self.entry, self.half_rows, self.half_entry = rows, entry, half_rows, half_entry
        self.landings, self.out, self.entry_out, self.sems = landings, out, entry_out, sems
        self.z, self.x, self.y, self.c = place()
        (self.core, self.across, self.along), self.planes = neighbours()
        half = rows.shape[-1] // 2
        self.mine = pl.ds(pl.multiple_of(self.c * half, 128), half)
        self.away = pl.ds(pl.multiple_of((1 - self.c) * half, 128), half)

    def copy(self, slot):
        rows_land, entry_land, last = self.landings
        stage, kind = slot // 2, slot % 2
        if stage == 0:
            source = (self.rows.at[:, self.away], self.entry.at[:, :, self.away])[kind]
        else:
            source = (self.half_rows, self.half_entry)[kind]
        if stage < 3:
            target = (rows_land, entry_land)[kind].at[stage]
            return send(source, target, self.sems, slot, (self.core, self.across, self.along)[stage])
        if stage < 6:
            step = stage - 3
            if kind == 0:
                target = self.out.at[self.z, :, self.mine]
            else:
                source = self.half_entry.at[lax.rem(self.z + step + 1, 4)]
                target = last.at[step]
            return send(source, target, self.sems, slot, self.planes[step])
        part = (self.out.at[:, :, self.mine], self.entry_out.at[:, self.mine])[kind]
        return send(part, part, self.sems, slot, self.core)

    def start(self, stage):
        self.copy(2 * stage).start()
        self.copy(2 * stage + 1).start()

    def landed(self, stage):
        self.copy(2 * stage).wait_recv()
        self.copy(2 * stage + 1).wait_recv()

    def add(self, stage):
        rows_land, entry_land, _ = self.landings
        self.landed(stage)
        if stage == 0:
            self.half_rows[...] = self.rows[:, self.mine] + rows_land[0]
            self.half_entry[...] = self.entry[:, :, self.mine] + entry_land[0]
        else:
            self.sent(stage)
            self.half_rows[...] = self.half_rows[...] + rows_land[stage]
            self.half_entry[...] = self.half_entry[...] + entry_land[stage]
        if stage < 2:
            self.start(stage + 1)
        else:
            for step in (3, 4, 5):
                self.start(step)

    def sent(self, stage):
        self.copy(2 * stage).wait_send()
        self.copy(2 * stage + 1).wait_send()

    def collect(self):
        last = self.landings[2]
        self.out[self.z, :, self.mine] = self.half_rows[...]
        total = self.half_entry[self.z].astype(F32)
        for step in range(3):
            self.landed(3 + step)
            total = total + last[step].astype(F32)
        self.entry_out[:, self.mine] = total.astype(BF16)
        self.start(6)


def late_kernel(
    slots,
    tokens,
    stream,
    middle_grad,
    gain,
    embed_low,
    found,
    input_weight,
    second_norm,
    query_back,
    up_three,
    normed_hbm,
    key_back_hbm,
    value_back_hbm,
    output_hbm,
    normed_unit,
    embed_grad_out,
    table_out,
    small_out,
    entry_out,
    up_out,
    heads_out,
    normed,
    key_back,
    value_back,
    heads_unit,
    normed_local,
    given,
    part,
    part_landed,
    rows_own,
    entry_own,
    half_rows,
    half_entry,
    rows_land,
    entry_land,
    entry_last,
    loads,
    *scratch,
):
    z, x, y, c = place()
    own = x * 4 + y * 2 + c
    width = stream.shape[1]
    rows = stream.shape[0]
    near, planes = neighbours()
    normed_plane = Plane(normed_unit, lambda yy, xx, zz: normed_local[yy, xx, zz], scratch[0:6])
    heads_plane = Plane(heads_unit, lambda yy, xx, zz: heads_unit[c, yy, xx, zz], scratch[6:12])
    up = Line(up_three, scratch[12:15], up_out)
    heads = Line(heads_plane.three, scratch[15:18], heads_out)
    table = Rows(given, part, part_landed, table_out, scratch[18:20])
    small = Small(
        rows_own,
        entry_own,
        half_rows,
        half_entry,
        (rows_land, entry_land, entry_last),
        small_out,
        entry_out,
        scratch[20:22],
    )
    local = pltpu.make_async_copy(normed_unit.at[c], normed_local, loads.at[0])
    copies = [
        pltpu.make_async_copy(source, target, loads.at[1 + index])
        for index, (source, target) in enumerate(
            (
                (normed_hbm, normed),
                (key_back_hbm, key_back),
                (value_back_hbm, value_back),
                (output_hbm, heads_unit.at[0, 0]),
            )
        )
    ]
    kept = {}

    def load():
        for copy in copies:
            copy.start()

    def loaded():
        for index in (0, 1, 3):
            copies[index].wait()

    def keep(kind):
        if kind == 1:
            mine = pl.ds(pl.multiple_of(own * rows, 128), rows)
            value = dot(normed[:, mine], query_back[...], 1, 1)
        else:
            if kind == 3:
                copies[2].wait()
            value = dot(normed[...], (key_back, value_back)[kind - 2][...])
        value = value.astype(BF16).reshape(4, 2, PIECE, width)
        for half in range(2):
            heads_unit[kind // 2, kind % 2, half] = value[:, half]

    def norm():
        unit, scale = norm_parts(stream[...])
        incoming = normed_plane.three[...].reshape(rows, width).astype(F32)
        stream_grad = middle_grad[...] + norm_back(incoming, gain[...].reshape(1, width), unit, scale)
        embed_grad = dot(stream_grad.astype(BF16), input_weight[...], 1, 1)
        given[own] = embed_grad.astype(BF16)
        embed_grad_out[...] = embed_grad
        kept["unit"], kept["incoming"], kept["stream_grad"] = unit, incoming, stream_grad
        kept["embed_grad"] = embed_grad

    def norm_rest():
        unit, incoming, stream_grad = kept["unit"], kept["incoming"], kept["stream_grad"]
        stream_low = stream_grad.astype(BF16)
        entry_own[...] = dot(embed_low[...], stream_low, 0, 0).astype(BF16).reshape(4, 32, width)
        kinds = lax.broadcasted_iota(jnp.int32, (SLOTS, rows), 0)
        slot = jnp.concatenate([slots[line : line + 1, :] for line in range(rows // 128)], axis=1)
        picker = jnp.where(kinds == slot, 1.0, 0.0).astype(BF16)
        rest = (stream_grad - stream_low.astype(F32)).astype(BF16)
        rows_own[...] = dot(picker, stream_low) + dot(picker, rest)
        rows_own[DEAD : DEAD + 1] = jnp.sum(incoming * unit, axis=0, keepdims=True)
        rows_own[DEAD + 1 : DEAD + 2] = jnp.sum(incoming, axis=0, keepdims=True)
        rows_own[DEAD + 2 : DEAD + 4] = second_norm[...]
        inner = jnp.sum(kept["embed_grad"] * found[...].astype(F32), axis=0, keepdims=True)
        inner = jnp.sum(inner, axis=1, keepdims=True)
        rows_own[DEAD + 4 : DEAD + 5] = jnp.broadcast_to(inner, (1, width))

    def hot(step):
        size = part.shape[1]
        seq = y * 2 + c
        base = seq * (8 * size) + x * (4 * size) + lax.rem(z + step, 4) * size
        ids = lax.broadcasted_iota(jnp.int32, (size, 128), 0) + base
        hits = [
            jnp.where(ids == tokens[owner, line : line + 1, :], 1.0, 0.0).astype(BF16)
            for owner in range(8)
            for line in range(rows // 128)
        ]
        hits = jnp.concatenate(hits, axis=1)
        part[step] = dot(hits, given[...].reshape(8 * rows, 128)).astype(BF16)
        if step:
            table.start(7 + step)

    def table_add():
        total = part[0].astype(F32)
        for slot in (8, 9, 10):
            table.landed_all(slot)
            total = total + part_landed[slot - 8].astype(F32)
        table_out[x, z] = total.astype(BF16)
        table.start(11, 12, 13, 14)

    def table_forward(*slots):
        for slot in slots:
            table.landed_all(slot)
            table.start(slot + 4)

    def after(wait, *starts):
        table.landed_all(*wait)
        table.start(*starts)

    def hot_first():
        table.landed_all(0, 5, 6, 7)
        hot(1)

    steps = {
        GREET: lambda: greet(near + planes),
        X_LOCAL: local.wait,
        LOAD: load,
        LOADED: loaded,
        GRAD_Q: lambda: keep(1),
        GRAD_K: lambda: keep(2),
        GRAD_V: lambda: keep(3),
        NORM: norm,
        NORM_REST: norm_rest,
        T_FIRST: lambda: table.start(0, 1, 2),
        T_PASS_X: lambda: after((1,), 3),
        T_PASS_Y: lambda: after((2,), 4),
        T_CORE: lambda: after((3, 4), 5, 6, 7),
        T_ROWS: hot_first,
        T_ROWS + 1: lambda: hot(2),
        T_ROWS + 2: lambda: hot(3),
        T_ROWS + 3: lambda: hot(0),
        T_SUM: table_add,
        T_PASS: lambda: table_forward(11, 12, 13),
        T_END: lambda: table.landed_all(14, 15, 16, 17),
        S_FIRST: lambda: small.start(0),
        S_CORE: lambda: small.add(0),
        S_X: lambda: small.add(1),
        S_Y: lambda: small.add(2),
        S_COLLECT: small.collect,
        S_END: lambda: small.landed(6),
    }
    steps.update(normed_plane.actions(X_CORE))
    steps.update(heads_plane.actions(H_CORE))
    steps.update(up.actions(U_SEND))
    steps.update(heads.actions(H_SEND))
    local.start()
    for key in LATE_ORDER:
        steps[key]()
    small.sent(0)
    for stage in (3, 4, 5, 6):
        small.sent(stage)
    table.finish()
    normed_plane.finish()
    heads_plane.finish()
    up.finish()
    heads.finish()


def late(
    slots,
    tokens,
    stream,
    middle_grad,
    gain,
    embed_low,
    found,
    input_weight,
    second_norm,
    query_back,
    up_three,
    normed,
    key_back,
    value_back,
    output_part,
    normed_unit,
):
    rows, width = stream.shape
    group = key_back.shape[0]
    quarter = VOCAB // 4 // 8
    vmem = pl.BlockSpec(memory_space=pltpu.VMEM)
    hbm = pl.BlockSpec(memory_space=pltpu.HBM)
    done = jax.ShapeDtypeStruct((2, 2, 2, PIECE, width), BF16)
    pair = lambda count: [pltpu.SemaphoreType.DMA((count,)), pltpu.SemaphoreType.DMA((count,))]
    return pl.pallas_call(
        late_kernel,
        in_specs=[vmem] * 11 + [hbm] * 5,
        out_specs=[vmem] * 6,
        out_shape=[
            jax.ShapeDtypeStruct((rows, 128), F32),
            jax.ShapeDtypeStruct((2, 4, quarter, 128), BF16),
            jax.ShapeDtypeStruct((4, 32, width), F32),
            jax.ShapeDtypeStruct((32, width), BF16),
            done,
            done,
        ],
        scratch_shapes=[
            pltpu.VMEM((width, group), BF16),
            pltpu.VMEM((group, width), BF16),
            pltpu.VMEM((group, width), BF16),
            pltpu.VMEM(UNIT, BF16),
            pltpu.VMEM(UNIT[1:], BF16),
            pltpu.VMEM((8, rows, 128), BF16),
            pltpu.VMEM((4, quarter, 128), BF16),
            pltpu.VMEM((3, quarter, 128), BF16),
            pltpu.VMEM((32, width), F32),
            pltpu.VMEM((4, 32, width), BF16),
            pltpu.VMEM((32, width // 2), F32),
            pltpu.VMEM((4, 32, width // 2), BF16),
            pltpu.VMEM((3, 32, width // 2), F32),
            pltpu.VMEM((3, 4, 32, width // 2), BF16),
            pltpu.VMEM((3, 32, width // 2), BF16),
            pltpu.SemaphoreType.DMA((5,)),
        ]
        + plane_buffers() * 2
        + line_buffers() * 2
        + pair(18)
        + pair(14),
        compiler_params=params(collective_id=2, has_side_effects=True),
        name="late",
    )(
        slots,
        tokens,
        stream,
        middle_grad,
        gain,
        embed_low,
        found,
        input_weight,
        second_norm,
        query_back,
        up_three,
        normed,
        key_back,
        value_back,
        output_part,
        normed_unit,
    )


def finish_kernel(
    embed_grad,
    table_sum,
    small,
    entry,
    down,
    up,
    heads,
    table,
    mean_norm,
    hidden,
    acts,
    features,
    second_weight,
    embed_out,
    table_out,
    entry_out,
    first_out,
    second_out,
    gain_one,
    shift_one,
    query_out,
    key_out,
    value_out,
    output_out,
    gain_two,
    shift_two,
    up_out,
    down_out,
):
    width = second_weight.shape[0]
    embed_out[...] = embed_grad[...]
    entry_out[...] = entry[...].astype(F32)
    for piece in range(8):
        c, y, x = piece // 4, (piece // 2) % 2, piece % 2
        down_out[piece * PIECE : (piece + 1) * PIECE, :] = down[c, y, x].astype(F32)
        quarter = piece // 2
        up_out[x * PIECE : (x + 1) * PIECE, quarter * width : (quarter + 1) * width] = up[c, y, x].astype(F32)
        target = (output_out, query_out, key_out, value_out)[quarter]
        target[x * PIECE : (x + 1) * PIECE, :] = heads[c, y, x].astype(F32)
    totals = small[0, DEAD : DEAD + 5]
    for plane in range(1, small.shape[0]):
        totals = totals + small[plane, DEAD : DEAD + 5]
    gain_one[...] = totals[0:1].reshape(width)
    shift_one[...] = totals[1:2].reshape(width)
    gain_two[...] = totals[2:3].reshape(width)
    shift_two[...] = totals[3:4].reshape(width)
    mean = mean_norm[0:1]
    inverse = 1.0 / mean
    mean_grad = -totals[4:5, 0:128] * inverse * inverse * (1.0 / VOCAB)
    wide = table[...].astype(F32)
    norms = jnp.sqrt(jnp.sum(wide * wide, axis=1, keepdims=True))
    sums = table_sum[...].reshape(table.shape).astype(F32)
    table_out[...] = sums * inverse + mean_grad * (wide / norms)
    tog = jnp.concatenate([small[plane, 0:SLOTS] for plane in range(small.shape[0])], axis=0)
    plane = lax.axis_index("dp")

    def rows_of(array, count):
        return array[pl.ds(pl.multiple_of(plane * count, 8), count), :]

    second_out[...] = lax.dot_general(
        rows_of(acts, second_out.shape[0]),
        tog,
        (((1,), (0,)), ((), ())),
        precision=lax.Precision.HIGHEST,
        preferred_element_type=F32,
    )
    high = tog.astype(BF16)
    rest = (tog - high.astype(F32)).astype(BF16)
    act_grad = dot(high, second_weight[...], 1, 1) + dot(rest, second_weight[...], 1, 1)
    value = hidden[...]
    gate = 1.0 / (1.0 + jnp.exp(-value))
    hidden_grad = act_grad * (gate * (1.0 + value * (1.0 - gate)))
    first_out[...] = lax.dot_general(
        rows_of(features, first_out.shape[0]),
        hidden_grad,
        (((1,), (0,)), ((), ())),
        precision=lax.Precision.HIGHEST,
        preferred_element_type=F32,
    )


def finish(embed_grad, table_sum, small, entry, down, up, heads, table, mean_norm, hidden, acts, features, second_weight):
    rows = embed_grad.shape[0]
    width = second_weight.shape[0]
    wide = lambda *shape: jax.ShapeDtypeStruct(shape, F32)
    shard = width // 4
    return pl.pallas_call(
        finish_kernel,
        out_shape=[
            wide(rows, 128),
            wide(*table.shape),
            wide(32, width),
            wide(features.shape[0] // 4, width),
            wide(acts.shape[0] // 4, width),
            wide(width),
            wide(width),
            wide(shard, width),
            wide(shard, width),
            wide(shard, width),
            wide(shard, width),
            wide(width),
            wide(width),
            wide(shard, 4 * width),
            wide(width, width),
        ],
        compiler_params=params(),
        name="finish",
    )(embed_grad, table_sum, small, entry, down, up, heads, table, mean_norm, hidden, acts, features, second_weight)


def body(
    tokens,
    segments,
    live_lengths,
    timesteps,
    table,
    input_weight,
    time_first,
    time_second,
    first_gain,
    first_shift,
    query_weight,
    key_weight,
    value_weight,
    output_weight,
    second_gain,
    second_shift,
    up_weight,
    down_weight,
    upstream,
):
    blocks = lax.axis_size("head") * lax.axis_size("seq")
    planes = lax.axis_size("dp")
    rows = tokens.shape[0]
    width = query_weight.shape[0]
    shard_rows = table.shape[0]
    slot_count = live_lengths.shape[1]
    highest = lax.Precision.HIGHEST
    plane = lax.axis_index("dp")
    seq_index = lax.axis_index("seq")
    own = lax.axis_index("head") * lax.axis_size("seq") + seq_index
    linked = planes == 4

    slot_rows = segments.reshape(rows // 128, 128)
    full_table, notes_all, mean_norm, entry, time_hidden, acts, features = gather(
        table,
        tokens.reshape(rows // 128, 128),
        slot_rows,
        timesteps,
        live_lengths,
        input_weight,
        time_first,
        time_second,
    )
    normed, keys, values, marks, stream, query, embed_low, found = embed(
        own[None],
        notes_all,
        mean_norm,
        full_table,
        entry,
        first_gain,
        first_shift,
        query_weight,
        key_weight,
        value_weight,
        rows,
        blocks,
    )
    probs, mixed, inverse = attend(query, keys, values, marks, slot_rows)
    activation, middle_grad, second_norm, mixed_grad, row_sums, output_part, up_unit, down_unit = feed(
        mixed,
        inverse,
        stream,
        upstream,
        second_gain,
        second_shift,
        output_weight,
        up_weight,
        down_weight,
    )
    query_back, key_back, value_back, normed_unit, down_sum, up_three = attend_back(
        linked,
        query,
        keys,
        values,
        marks,
        probs,
        mixed_grad,
        row_sums,
        query_weight,
        key_weight,
        value_weight,
        down_unit,
        up_unit,
    )
    if linked:
        embed_grad, table_sum, small, entry_sum, up_sum, heads_sum = late(
            slot_rows,
            notes_all,
            stream,
            middle_grad,
            first_gain,
            embed_low,
            found,
            input_weight,
            second_norm,
            query_back,
            up_three,
            normed,
            key_back,
            value_back,
            output_part,
            normed_unit,
        )
        outs = finish(
            embed_grad,
            table_sum,
            small,
            entry_sum,
            down_sum,
            up_sum,
            heads_sum,
            table,
            mean_norm,
            time_hidden,
            acts,
            features,
            time_second,
        )
        return (activation, *outs)

    output_grad = output_part.transpose(1, 0, 2, 3).reshape(width, width)
    query_grad = dot(lax.dynamic_slice_in_dim(normed, own * rows, rows, axis=1), query_back, 1, 1)
    key_grad = dot(normed, key_back)
    value_grad = dot(normed, value_back)
    down_grad = down_unit.transpose(3, 0, 1, 2, 4, 5).reshape(-1, width)
    up_grad = up_unit.transpose(3, 2, 4, 0, 1, 5).reshape(width, -1)
    normed_grad = lax.psum_scatter(
        normed_unit.transpose(2, 1, 0, 3, 4, 5).reshape(-1, width),
        ("head", "seq"),
        scatter_dimension=0,
        tiled=True,
    ).astype(F32)
    mean_norm = mean_norm[0, 0]
    features = lax.dynamic_slice_in_dim(features.T, plane * SLOTS, slot_count)
    time_hidden = lax.dynamic_slice_in_dim(time_hidden, plane * SLOTS, slot_count)
    time_act = lax.dynamic_slice_in_dim(acts.T, plane * SLOTS, slot_count)
    second_wide = time_second.astype(F32)

    def one_norm(values, gain, shift):
        unit, _ = norm_parts(values)
        return unit * gain + shift

    _, first_back = jax.vjp(one_norm, stream, first_gain, first_shift)
    stream_part, first_gain_grad, first_shift_grad = first_back(normed_grad)
    stream_grad = middle_grad + stream_part
    stream_low = stream_grad.astype(BF16)
    input_grad = dot(embed_low, stream_low, 0, 0)
    embed_grad = dot(stream_low, input_weight, 1, 1)
    picker = (segments[:, None] == jnp.arange(slot_count, dtype=jnp.int32)[None, :]).astype(F32)
    time_out_grad = contract_exact(picker, stream_grad)
    time_second_grad = contract_exact(time_act, time_out_grad)
    act_grad = lax.dot_general(
        time_out_grad, second_wide, (((1,), (1,)), ((), ())), precision=highest
    )
    _, silu_back = jax.vjp(jax.nn.silu, time_hidden)
    time_hidden_grad = silu_back(act_grad)[0]
    time_first_grad = contract_exact(features, time_hidden_grad)

    def reduce(value):
        part = lax.psum_scatter(value.astype(BF16), "dp", scatter_dimension=0, tiled=True)
        return lax.psum(part, ("head", "seq")).astype(F32)

    shards = [
        reduce(value)
        for value in (
            input_grad,
            time_first_grad,
            time_second_grad,
            query_grad,
            key_grad,
            value_grad,
            output_grad,
            up_grad,
            down_grad,
        )
    ]
    mean_part = -jnp.sum(embed_grad * found.astype(F32)) / (mean_norm * mean_norm)
    scaled_grad = embed_grad / mean_norm
    table_sum = jax.ops.segment_sum(scaled_grad, tokens, num_segments=VOCAB)
    small = lax.psum(
        (first_gain_grad, first_shift_grad, second_norm[0], second_norm[1], mean_part, table_sum),
        ("dp", "head", "seq"),
    )
    table_rows = lax.dynamic_slice_in_dim(small[5], seq_index * shard_rows, shard_rows)
    table_wide = table.astype(F32)
    row_norms = jnp.sqrt(jnp.sum(table_wide * table_wide, axis=1))
    table_grad = table_rows + small[4] / VOCAB * table_wide / row_norms[:, None]
    return (
        activation,
        embed_grad,
        table_grad,
        shards[0],
        shards[1],
        shards[2],
        small[0],
        small[1],
        shards[3],
        shards[4],
        shards[5],
        shards[6],
        small[2],
        small[3],
        shards[7],
        shards[8],
    )


def solution(mesh):
    tokens = P(("dp", "head", "seq"))
    wide = P(("dp", "head", "seq"), None)
    group = P("dp", None)
    return jax.shard_map(
        body,
        mesh=mesh,
        in_specs=(tokens, tokens, group, group, P("seq", None)) + (P(),) * 13 + (wide,),
        out_specs=(wide, wide, P("seq", None), group, group, group, P(), P())
        + (group,) * 4
        + (P(), P(), group, group),
        check_vma=False,
    )
```

time: 315 us -> 240 us (0.76)
  Pallas kernels: 294 us -> 237 us
  local copies, waits for them, and re-layouts: 10 us -> 0 us
    pallas_call x2, Pallas kernels: 127 us -> 94.4 us  [the longest x1 70.7 us: late(): pl.pallas_call(late_kernel, in_specs=[vmem] * 11 + [hbm] * 5, out_specs=[...]
    pallas_call x1, Pallas kernels: 34.2 us -> 23.6 us  [attend(): pl.pallas_call(forward_kernel, grid=(pairs,), in_specs=[pl.BlockSpec((128...]
    pallas_call x1, Pallas kernels: 71 us -> 65.2 us  [attend_back(): pl.pallas_call(functools.partial(back_kernel, linked), grid=(pairs + 1,),...]
    pallas_call x1, Pallas kernels: 29.7 us -> 24 us  [embed(): pl.pallas_call(embed_kernel, grid_spec=pltpu.PrefetchScalarGridSpec(num_s...]
    reshape x3 -> x0, local copies, waits for them, and re-layouts: 3.33 us -> none  [the longest x1 1.36 us: body(): row_sums.reshape(HEADS // 2, 2, rows)]
where the time goes in v3:
time: 240 us; the launch traced here: 238 us
  Pallas kernels  237 us (99%)
    pallas_call x1, Pallas kernels, late(): pl.pallas_call(late_kernel, in_specs=[vmem] * 11 + [hbm] * 5, out_specs=[...  70.7 us
    pallas_call x1, Pallas kernels, attend_back(): pl.pallas_call(functools.partial(back_kernel, linked), grid=(pairs + 1,),...  65.2 us
    pallas_call x1, Pallas kernels, embed(): pl.pallas_call(embed_kernel, grid_spec=pltpu.PrefetchScalarGridSpec(num_s...  24 us
    pallas_call x1, Pallas kernels, gather(): pl.pallas_call(gather_kernel, in_specs=[vmem] * 8, out_specs=[hbm] + [vme...  23.6 us
    pallas_call x1, Pallas kernels, attend(): pl.pallas_call(forward_kernel, grid=(pairs,), in_specs=[pl.BlockSpec((128...  23.6 us
    pallas_call x1, Pallas kernels, feed(): pl.pallas_call(feed_kernel, in_specs=[vmem] * 6 + [hbm] * 3, out_specs=[v...  21.5 us
    pallas_call x1, Pallas kernels, finish(): pl.pallas_call(finish_kernel, out_shape=[wide(rows, 128), wide(*table.sha...  8.41 us

profile of v3, /device:TPU:0, one launch (start us, length us, event | category | flops | bytes accessed | tf_op | source)
XLA Modules:
  0.0 237.7 jit_solution(17593197563268084983)
XLA Ops:
  0.7 23.6 %gather.1 = (bf16[4,2048,128]{2,1,0:T(8,128)(2,1)}, s32[8,8,128]{2,1,0:T(8,128)}, f32[8,128]{1,0:T(8,128)}, bf16[256,768]{1,0:T(8,128)(2,1)}, f32[128,768]{1,0:T...) custom-call(bf16[2048,128]{1,0:T(8,128)(2,1)} %table.3, s32[3,128]{1,0:T(4,128)} %bitcast.6, s32[3,128]{1,0:T(4,128)} %bitcast.3, ...), custom_call_target="tpu_custom_call" | custom-call | tf_op jit(solution)/shard_map/gather/pallas_call | solution.py:332
  24.3 24.0 %embed.1 = (bf16[768,3072]{1,0:T(8,128)(2,1)}, bf16[6,3072,128]{2,1,0:T(8,128)(2,1)}, bf16[6,3072,128]{2,1,0:T(8,128)(2,1)}, bf16[3072,128]{1,0:T(8,128)(2,1)}, ...) custom-call(s32[1]{0:T(128)} %bitcast.own, ...), custom_call_target="tpu_custom_call" | custom-call | tf_op jit(solution)/shard_map/embed/pallas_call | solution.py:457
  48.3 23.6 %attend.1 = (bf16[6,3072,768]{2,1,0:T(8,128)(2,1)}, f32[768,384]{1,0:T(8,128)}, f32[6,2,384]{2,1,0:T(2,128)}) custom-call(bf16[768,384]{1,0:T(8,128)(2,1)} %get-tuple-element.73.query, bf16[6,3072,128]{2,1,0:T(8,128)(2,1)} %get-tuple-element.74.keys, bf16[6,3072,128]{2,1,0:T(8,128)(2,1)} %get-tuple-element.75.values, ...), custom_call_target="tpu_custom_call" | custom-call | tf_op jit(solution)/shard_map/attend/pallas_call | solution.py:581
  71.9 21.5 %feed.1 = (bf16[384,768]{1,0:T(8,128)(2,1)}, f32[384,768]{1,0:T(8,128)}, f32[2,768]{1,0:T(2,128)}, bf16[768,384]{1,0:T(8,128)(2,1)}, f32[6,2,384]{2,1,0:T(2,128)...) custom-call(f32[768,384]{1,0:T(8,128)} %get-tuple-element.77.mixed_w, ...), custom_call_target="tpu_custom_call" | custom-call | tf_op jit(solution)/shard_map/feed/pallas_call | solution.py:728
  93.4 65.2 %attend_back.1 = (bf16[768,384]{1,0:T(8,128)(2,1)}, bf16[3072,768]{1,0:T(8,128)(2,1)}, bf16[3072,768]{1,0:T(8,128)(2,1)}, bf16[2,2,2,4,96,768]{5,4,3,2,1,0:T(8,1...) custom-call(bf16[768,384]{1,0:T(8,128)(2,1)} %get-tuple-element.73.query, ...), custom_call_target="tpu_custom_call" | custom-call | tf_op jit(solution)/shard_map/attend_back/pallas_call | solution.py:1124
  158.6 70.7 %late.1 = (f32[384,128]{1,0:T(8,128)}, bf16[2,4,256,128]{3,2,1,0:T(8,128)(2,1)}, f32[4,32,768]{2,1,0:T(8,128)}, bf16[32,768]{1,0:T(8,128)(2,1)}, bf16[2,2,2,96,7...) custom-call(s32[3,128]{1,0:T(4,128)} %bitcast.5, s32[8,8,128]{2,1,0:T(8,128)} %get-tuple-element.69.tokens.notes, ...), custom_call_target="tpu_custom_call" | custom-call | tf_op jit(solution)/shard_map/late/pallas_call | solution.py:1514
  229.3 8.4 %finish.1 = (f32[384,128]{1,0:T(8,128)}, f32[2048,128]{1,0:T(8,128)}, f32[32,768]{1,0:T(8,128)}, f32[32,768]{1,0:T(8,128)}, f32[192,768]{1,0:T(8,128)}, /*index=...) custom-call(f32[384,128]{1,0:T(8,128)} %get-tuple-element.97.embed_g, ...), custom_call_target="tpu_custom_call" | custom-call | tf_op jit(solution)/shard_map/finish/pallas_call | solution.py:1657
